TPU v7x, 32 devices: a whole 2x2x4 slice. The times are simulated.
32 devices in a mesh: section: 8 (over y, x, core), expert: 4 (over z).
Axes of the slice: x: 2, y: 2, z: 4, core: 2. Of those that a mesh axis runs over, the one named last changes fastest.
Arguments:
- grad_out: bfloat16 [8, 512, 1024], P('section', 'expert'), may hold values from -6 to 6
- saved_inputs: bfloat16 [8, 2, 512, 1024], P('section', None, 'expert'), may hold values from -6 to 6
- routes: int32 [8, 2, 512, 8], P('section', None, 'expert'), may hold values from 0 to 31, all different within a row; in each aligned block of 128 rows (0 to 127, 128 to 255, ..., all dimensions but the last counted through in order) at most 40 rows name the same one
- gate_weights: float32 [8, 2, 512, 8], P('section', None, 'expert'), may hold values from 0.05 to 0.3
- w_gate: bfloat16 [8, 32, 1024, 512], P('section', 'expert'), may hold values from -0.1875 to 0.1875
- w_up: bfloat16 [8, 32, 1024, 512], P('section', 'expert'), may hold values from -0.1875 to 0.1875
- w_down: bfloat16 [8, 32, 512, 1024], P('section', 'expert'), may hold values from -0.25 to 0.25
Outputs:
- input_grad: bfloat16 [8, 512, 1024], P('section', 'expert')
Inputs may be any that keep to these rules, and one draw needn't show every extreme that they name: `routes`: each row names 8 different experts. In the rows of one device at one step (aligned blocks of 128 rows) no expert is named by more than 40 rows; in some blocks one expert is named by exactly 40.
All inputs are finite; a program needn't handle non-finite values.
Results may differ from a plain program's by a relative error of at most 0.007.
Values may be sent and summed in bfloat16 or wider, within the bound.
No kernel may reach another device: no remote copies, remote signals or barrier semaphores. Data moves between devices by JAX's collectives and lax.ppermute only.
A program may use at most 128 MiB of HBM per device.

v0:
```python
import jax
import jax.numpy as jnp
from jax import lax
from jax.sharding import PartitionSpec as P

MOST = 40


def passed_along(value, axis, by):
    devices = lax.axis_size(axis)
    return lax.ppermute(value, axis, [(i, (i + by) % devices) for i in range(devices)])


def shards(grad_out, saved_inputs, routes, gate_weights, w_gate, w_up, w_down):
    owners = lax.axis_size("expert")
    gate_local = w_gate[0]
    up_local = w_up[0]
    down_local = w_down[0]
    local_count = gate_local.shape[0]
    expert_total = owners * local_count
    token_count = grad_out.shape[1]
    width = grad_out.shape[2]
    step_count = routes.shape[1]
    top_count = routes.shape[3]
    row_total = token_count * top_count

    def layout(step_index):
        flat_routes = routes[0, step_index].reshape(-1)
        one_hot = (
            flat_routes[:, None] == jnp.arange(expert_total, dtype=jnp.int32)[None, :]
        ).astype(jnp.int32)
        earlier = jnp.cumsum(one_hot, axis=0) - one_hot
        position = jnp.sum(earlier * one_hot, axis=1)
        slot_index = flat_routes * MOST + position
        token_index = jnp.arange(row_total, dtype=jnp.int32) // top_count
        slot_token = jnp.zeros((expert_total * MOST,), jnp.int32).at[slot_index].set(token_index)
        slot_live = jnp.zeros((expert_total * MOST,), jnp.int32).at[slot_index].set(1)
        return (slot_index, slot_token, slot_live)

    def pack(source, slot_token, slot_live):
        picked = jnp.where(slot_live[:, None] == 1, source[slot_token], jnp.zeros((), source.dtype))
        return picked.reshape(owners, local_count, MOST, width)

    plans = [layout(step_index) for step_index in range(step_count)]
    grad = grad_out[0]
    total = grad
    for step_index in range(step_count):
        slot_index, slot_token, slot_live = plans[step_index]
        grad_rows = pack(grad, slot_token, slot_live)
        input_rows = pack(saved_inputs[0, step_index], slot_token, slot_live)
        expert_input_rows = lax.all_to_all(
            input_rows, "expert", split_axis=0, concat_axis=0, tiled=True
        )
        expert_grad_rows = lax.all_to_all(
            grad_rows, "expert", split_axis=0, concat_axis=0, tiled=True
        )
        gate_pre = jnp.einsum(
            "sjmd,jdh->sjmh", expert_input_rows, gate_local, preferred_element_type=jnp.float32
        )
        up_pre = jnp.einsum(
            "sjmd,jdh->sjmh", expert_input_rows, up_local, preferred_element_type=jnp.float32
        )
        hidden_grad = jnp.einsum(
            "sjmd,jhd->sjmh", expert_grad_rows, down_local, preferred_element_type=jnp.float32
        )
        sigmoid_gate = jax.nn.sigmoid(gate_pre)
        gate_grad = (
            hidden_grad * up_pre * sigmoid_gate * (1.0 + gate_pre * (1.0 - sigmoid_gate))
        ).astype(jnp.bfloat16)
        up_grad = (hidden_grad * gate_pre * sigmoid_gate).astype(jnp.bfloat16)
        row_grad = jnp.einsum(
            "sjmh,jdh->sjmd", gate_grad, gate_local, preferred_element_type=jnp.float32
        )
        row_grad = row_grad + jnp.einsum(
            "sjmh,jdh->sjmd", up_grad, up_local, preferred_element_type=jnp.float32
        )
        row_grad = row_grad.astype(jnp.bfloat16)
        back_rows = lax.all_to_all(row_grad, "expert", split_axis=0, concat_axis=0, tiled=True)
        gathered = back_rows.reshape(expert_total * MOST, width)[slot_index].reshape(
            token_count, top_count, width
        )
        weights = gate_weights[0, step_index]
        summed = grad.astype(jnp.float32) + jnp.sum(
            weights[:, :, None] * gathered.astype(jnp.float32), axis=1
        )
        total = summed.astype(jnp.bfloat16)
        if step_index + 1 < step_count:
            grad = passed_along(total, "section", -1)
    return total[None]


def solution(mesh):
    placed = (
        P("section", "expert", None),
        P("section", None, "expert", None),
        P("section", None, "expert", None),
        P("section", None, "expert", None),
        P("section", "expert", None, None),
        P("section", "expert", None, None),
        P("section", "expert", None, None),
    )
    return jax.shard_map(
        shards, mesh=mesh, in_specs=placed, out_specs=P("section", "expert", None), check_vma=False
    )
```

profile of v0, /device:TPU:0, one launch (start us, length us, event | category | flops | bytes accessed | tf_op | source)
XLA Modules:
  0.0 510.2 jit_solution(7759710680432306046)
XLA Ops:
  0.0 0.7 fusion.100
  0.7 0.1 copy.32
  1.0 9.0 %reduce-window.14 = s32[32,8,128]{2,1,0:T(8,128)S(1)} reduce-window(s32[32,8,128]{2,1,0:T(8,128)S(1)} %fusion.83, s32[]{:T(128)} %constant.32.clone.1), window={size=1x1x128 pad=0_0x0_0x127_0}, to_apply=%region_0.0 | reduce-window | flops 4161536 | bytes 262148 | tf_op jit(solution)/shard_map/reduce-window
  10.1 0.1 copy.34
  10.4 0.1 broadcast_add_fusion.1
  10.5 0.1 copy.31
  10.8 4.3 scatter_custom_fusion.1
  15.1 1.1 slice_bitcast_fusion.1
  16.2 4.3 gather_fusion.1
  20.5 5.1 %gather_fusion = bf16[1280,1024]{1,0:T(8,128)(2,1)} fusion(bf16[128,1024]{1,0:T(8,128)(2,1)S(1)} %bitcast.200, s32[2048]{0:T(1024)S(1)} %pad_clamp_fusion.1), kind=kCustom, calls=%fused_computation | custom fusion | bytes 5248000 | tf_op jit(solution)/shard_map/gather | solution.py:41
  25.6 4.3 scatter_custom_fusion
  30.1 3.1 broadcast_select_fusion.3
  33.2 65.6 %all_to_all.30 = bf16[4,8,40,1024]{3,2,1,0:T(8,128)(2,1)} all-to-all(bf16[4,8,40,1024]{3,2,1,0:T(8,128)(2,1)S(1)} %get-tuple-element.16), channel_id=1, replica_groups=mesh['section'=8,'expert'=4] {'expert'}, dimensions={0} | all-to-all | bytes 5242880 | tf_op jit(solution)/shard_map/all_to_all | solution.py:51
  98.8 3.8 all-to-all-start
  102.6 7.3 %fusion.6 = f32[8,4,40,512]{3,2,1,0:T(8,128)} fusion(bf16[1,8,1024,512]{3,2,1,0:T(8,128)(2,1)} %param.11, bf16[4,8,40,1024]{3,2,1,0:T(8,128)(2,1)} %all_to_all.30), kind=kOutput, calls=%fused_computation.16 | convolution fusion | flops 1342177280 | bytes 13631488 | tf_op jit(solution)/shard_map/sjmd,jdh->sjmh/dot_general | solution.py:57
  110.0 51.0 %all-to-all-done = bf16[4,8,40,1024]{3,2,1,0:T(8,128)(2,1)S(1)} async-done(((bf16[4,8,40,1024]{3,2,1,0:T(8,128)(2,1)}), bf16[4,8,40,1024]{3,2,1,0:T(8,128)(2,1)S(1)}, u32[]{:S(2)}, u32[]{:S(2)}) %all-to-all-start) | async-done | bytes 2621472 | tf_op jit(solution)/shard_map/all_to_all | solution.py:54
  161.0 7.8 %fusion.10 = f32[8,4,40,512]{3,2,1,0:T(8,128)} fusion(bf16[1,8,512,1024]{3,2,1,0:T(8,128)(2,1)} %param.13, bf16[4,8,40,1024]{3,2,1,0:T(8,128)(2,1)S(1)} %all-to-all-done), kind=kOutput, calls=%fused_computation.20 | convolution fusion | flops 1342177280 | bytes 13631488 | tf_op jit(solution)/shard_map/sjmd,jhd->sjmh/dot_general | solution.py:63
  168.8 15.3 %fusion.4 = f32[8,4,40,1024]{3,2,1,0:T(8,128)} fusion(bf16[1,8,1024,512]{3,2,1,0:T(8,128)(2,1)} %param.11, f32[8,4,40,512]{3,2,1,0:T(8,128)} %fusion.6, f32[8,4,40,512]{3,2,1,0:T(8,128)} %fusion.10, bf16[1,8,1024,512]{3,2,1,0:T(8,128)(2,1)} %param.12, bf16[4,8,40,1024]{3,2,1,0:T(8,128)(2,1)} %all_to_all.30), kind=kOutput, calls=%fused_computation.14 | convolution fusion | flops 2690908160 | bytes 29884416 | tf_op jit(solution)/shard_map/sjmh,jdh->sjmd/dot_general | solution.py:71
  184.1 8.5 %fusion.22 = bf16[4,8,40,1024]{3,2,0,1:T(8,128)(2,1)S(1)} fusion(f32[8,4,40,1024]{3,2,1,0:T(8,128)} %fusion.4, bf16[1,8,1024,512]{3,2,1,0:T(8,128)(2,1)} %param.12, f32[8,4,40,512]{3,2,1,0:T(8,128)} %fusion.6, f32[8,4,40,512]{3,2,1,0:T(8,128)S(1)} %copy-done.1), kind=kOutput, calls=%fused_computation.36 | convolution fusion | flops 1348730880 | bytes 21495808 | tf_op jit(solution)/shard_map/sjmh,jdh->sjmd/dot_general | solution.py:74
  192.6 1.7 copy.39
  194.3 3.8 all-to-all-start.2
  198.1 0.1 copy.42
  198.4 9.0 %reduce-window.16 = s32[32,8,128]{2,1,0:T(8,128)S(1)} reduce-window(s32[32,8,128]{2,1,0:T(8,128)S(1)} %fusion.84, s32[]{:T(128)} %constant.32.clone.1), window={size=1x1x128 pad=0_0x0_0x127_0}, to_apply=%region_6.7 | reduce-window | flops 4161536 | bytes 262148 | tf_op jit(solution)/shard_map/reduce-window.2
  207.5 0.1 copy.44
  207.9 0.1 mul.103
  208.2 4.3 scatter_custom_fusion.3
  212.5 4.5 scatter_custom_fusion.2
  217.0 0.1 copy.30
  217.3 39.7 %all-to-all-done.2 = bf16[4,8,40,1024]{3,2,1,0:T(8,128)(2,1)S(1)} async-done(((bf16[4,8,40,1024]{3,2,1,0:T(8,128)(2,1)}), bf16[4,8,40,1024]{3,2,1,0:T(8,128)(2,1)S(1)}, u32[]{:S(2)}, u32[]{:S(2)}) %all-to-all-start.2) | async-done | bytes 2621472 | tf_op jit(solution)/shard_map/all_to_all | solution.py:78
  257.0 5.4 %gather_fusion.2 = bf16[1024,1024]{1,0:T(8,128)(2,1)} fusion(bf16[1280,1024]{1,0:T(8,128)(2,1)S(1)} %bitcast.201, s32[1024]{0:T(1024)S(1)} %broadcast_clamp_fusion.1), kind=kCustom, calls=%fused_computation.2 | custom fusion | bytes 4198400 | tf_op jit(solution)/shard_map/gather | solution.py:79
  262.4 2.9 fusion.21
  265.4 1.1 collective-permute-start
  266.5 4.3 gather_fusion.4
  270.9 5.1 %gather_fusion.3 = bf16[1280,1024]{1,0:T(8,128)(2,1)} fusion(bf16[128,1024]{1,0:T(8,128)(2,1)S(1)} %collective-permute-done, s32[2048]{0:T(1024)S(1)} %pad_clamp_fusion), kind=kCustom, calls=%fused_computation.3 | custom fusion | bytes 5248000 | tf_op jit(solution)/shard_map/gather | solution.py:41
  276.0 3.1 broadcast_select_fusion.1
  279.0 63.4 %all_to_all.31 = bf16[4,8,40,1024]{3,2,1,0:T(8,128)(2,1)} all-to-all(bf16[4,8,40,1024]{3,2,1,0:T(8,128)(2,1)S(1)} %get-tuple-element.14), channel_id=1, replica_groups=mesh['section'=8,'expert'=4] {'expert'}, dimensions={0} | all-to-all | bytes 5242880 | tf_op jit(solution)/shard_map/all_to_all | solution.py:51
  342.4 3.7 all-to-all-start.3
  346.1 7.3 %fusion.2 = f32[8,4,40,512]{3,2,1,0:T(8,128)} fusion(bf16[1,8,1024,512]{3,2,1,0:T(8,128)(2,1)} %param.11, bf16[4,8,40,1024]{3,2,1,0:T(8,128)(2,1)} %all_to_all.31), kind=kOutput, calls=%fused_computation.12 | convolution fusion | flops 1342177280 | bytes 13631488 | tf_op jit(solution)/shard_map/sjmd,jdh->sjmh/dot_general | solution.py:57
  353.4 51.9 %all-to-all-done.3 = bf16[4,8,40,1024]{3,2,1,0:T(8,128)(2,1)S(1)} async-done(((bf16[4,8,40,1024]{3,2,1,0:T(8,128)(2,1)}), bf16[4,8,40,1024]{3,2,1,0:T(8,128)(2,1)S(1)}, u32[]{:S(2)}, u32[]{:S(2)}) %all-to-all-start.3) | async-done | bytes 2621472 | tf_op jit(solution)/shard_map/all_to_all | solution.py:54
  405.3 7.8 %fusion.8 = f32[8,4,40,512]{3,2,1,0:T(8,128)} fusion(bf16[1,8,512,1024]{3,2,1,0:T(8,128)(2,1)} %param.13, bf16[4,8,40,1024]{3,2,1,0:T(8,128)(2,1)S(1)} %all-to-all-done.3), kind=kOutput, calls=%fused_computation.18 | convolution fusion | flops 1342177280 | bytes 13631488 | tf_op jit(solution)/shard_map/sjmd,jhd->sjmh/dot_general | solution.py:63
  413.1 15.3 %fusion = f32[8,4,40,1024]{3,2,1,0:T(8,128)} fusion(bf16[1,8,1024,512]{3,2,1,0:T(8,128)(2,1)} %param.11, f32[8,4,40,512]{3,2,1,0:T(8,128)} %fusion.2, f32[8,4,40,512]{3,2,1,0:T(8,128)} %fusion.8, bf16[1,8,1024,512]{3,2,1,0:T(8,128)(2,1)} %param.12, bf16[4,8,40,1024]{3,2,1,0:T(8,128)(2,1)} %all_to_all.31), kind=kOutput, calls=%fused_computation.10 | convolution fusion | flops 2690908160 | bytes 29884416 | tf_op jit(solution)/shard_map/sjmh,jdh->sjmd/dot_general | solution.py:71
  428.4 8.5 %fusion.23 = bf16[4,8,40,1024]{3,2,0,1:T(8,128)(2,1)S(1)} fusion(f32[8,4,40,1024]{3,2,1,0:T(8,128)} %fusion, bf16[1,8,1024,512]{3,2,1,0:T(8,128)(2,1)} %param.12, f32[8,4,40,512]{3,2,1,0:T(8,128)} %fusion.2, f32[8,4,40,512]{3,2,1,0:T(8,128)S(1)} %copy-done.2), kind=kOutput, calls=%fused_computation.37 | convolution fusion | flops 1348730880 | bytes 21495808 | tf_op jit(solution)/shard_map/sjmh,jdh->sjmd/dot_general | solution.py:74
  436.9 1.7 copy.49
  438.6 3.7 all-to-all-start.5
  442.4 58.8 %all-to-all-done.5 = bf16[4,8,40,1024]{3,2,1,0:T(8,128)(2,1)S(1)} async-done(((bf16[4,8,40,1024]{3,2,1,0:T(8,128)(2,1)}), bf16[4,8,40,1024]{3,2,1,0:T(8,128)(2,1)S(1)}, u32[]{:S(2)}, u32[]{:S(2)}) %all-to-all-start.5) | async-done | bytes 2621472 | tf_op jit(solution)/shard_map/all_to_all | solution.py:78
  501.2 5.4 %gather_fusion.5 = bf16[1024,1024]{1,0:T(8,128)(2,1)} fusion(bf16[1280,1024]{1,0:T(8,128)(2,1)S(1)} %bitcast.202, s32[1024]{0:T(1024)S(1)} %broadcast_clamp_fusion), kind=kCustom, calls=%fused_computation.5 | custom fusion | bytes 4198400 | tf_op jit(solution)/shard_map/gather | solution.py:79
  506.6 2.9 fusion.20
  509.5 0.8 fusion.60
  (45 shorter events, 1.6 us)
Async XLA Ops:
  16.2 4.3 copy-start
  98.8 62.2 %all-to-all-start = ((bf16[4,8,40,1024]{3,2,1,0:T(8,128)(2,1)}), bf16[4,8,40,1024]{3,2,1,0:T(8,128)(2,1)S(1)}, u32[]{:S(2)}, u32[]{:S(2)}) async-start(bf16[4,8,40,1024]{3,2,1,0:T(8,128)(2,1)} %get-tuple-element.15), calls=%async_computation | async-start | bytes 5242880 | tf_op jit(solution)/shard_map/all_to_all | solution.py:54
  168.8 15.3 %copy-start.1 = (f32[8,4,40,512]{3,2,1,0:T(8,128)S(1)}, f32[8,4,40,512]{3,2,1,0:T(8,128)}, u32[]{:S(2)}) copy-start(f32[8,4,40,512]{3,2,1,0:T(8,128)} %fusion.10) | copy-start | bytes 7864324
  194.3 22.7 %copy-start.3 = (f32[1,2,128,8]{2,3,1,0:T(8,128)S(1)}, f32[1,2,128,8]{2,3,1,0:T(8,128)}, u32[]{:S(2)}) copy-start(f32[1,2,128,8]{2,3,1,0:T(8,128)} %param.10) | copy-start | bytes 24580
  194.3 62.7 %all-to-all-start.2 = ((bf16[4,8,40,1024]{3,2,1,0:T(8,128)(2,1)}), bf16[4,8,40,1024]{3,2,1,0:T(8,128)(2,1)S(1)}, u32[]{:S(2)}, u32[]{:S(2)}) async-start(bf16[4,8,40,1024]{3,2,1,0:T(8,128)(2,1)} %copy.39), calls=%async_computation.2 | async-start | bytes 5242880 | tf_op jit(solution)/shard_map/all_to_all | solution.py:78
  265.4 5.5 %collective-permute-start = (bf16[128,1024]{1,0:T(8,128)(2,1)S(1)}, bf16[128,1024]{1,0:T(8,128)(2,1)S(1)}, u32[]{:S(2)}, u32[]{:S(2)}) collective-permute-start(bf16[128,1024]{1,0:T(8,128)(2,1)S(1)} %add_convert_fusion.3), channel_id=1, source_target_pairs={{0,28},{4,0},{8,4},{12,8},{16,12},{20,16},{24,20},{28,24},{1,29},{... | collective-permute-start | bytes 786440 | tf_op jit(solution)/shard_map/ppermute | solution.py:11
  342.4 62.9 %all-to-all-start.3 = ((bf16[4,8,40,1024]{3,2,1,0:T(8,128)(2,1)}), bf16[4,8,40,1024]{3,2,1,0:T(8,128)(2,1)S(1)}, u32[]{:S(2)}, u32[]{:S(2)}) async-start(bf16[4,8,40,1024]{3,2,1,0:T(8,128)(2,1)} %get-tuple-element.13), calls=%async_computation.3 | async-start | bytes 5242880 | tf_op jit(solution)/shard_map/all_to_all | solution.py:54
  413.1 15.3 %copy-start.2 = (f32[8,4,40,512]{3,2,1,0:T(8,128)S(1)}, f32[8,4,40,512]{3,2,1,0:T(8,128)}, u32[]{:S(2)}) copy-start(f32[8,4,40,512]{3,2,1,0:T(8,128)} %fusion.8) | copy-start | bytes 7864324
  438.6 62.5 %all-to-all-start.5 = ((bf16[4,8,40,1024]{3,2,1,0:T(8,128)(2,1)}), bf16[4,8,40,1024]{3,2,1,0:T(8,128)(2,1)S(1)}, u32[]{:S(2)}, u32[]{:S(2)}) async-start(bf16[4,8,40,1024]{3,2,1,0:T(8,128)(2,1)} %copy.49), calls=%async_computation.5 | async-start | bytes 5242880 | tf_op jit(solution)/shard_map/all_to_all | solution.py:78
where the time goes:
time: 511 us; the launch traced here: 510 us
  waiting for transfers between devices  201 us (39%)
  blocking collectives  129 us (25%)
  matrix products  77.8 us (15%)
  local copies, waits for them, and re-layouts  53.6 us (10%)
  other arithmetic  32 us (6%)
  starting transfers between devices  16.1 us (3%)
    all_to_all x2, blocking collectives, shards(): lax.all_to_all(input_rows, 'expert', split_axis=0, concat_axis=0, tiled=T...  129 us
    all_to_all x2, waiting for transfers between devices, shards(): lax.all_to_all(grad_rows, 'expert', split_axis=0, concat_axis=0, tiled=True)  103 us
    all_to_all x2, waiting for transfers between devices, shards(): lax.all_to_all(row_grad, 'expert', split_axis=0, concat_axis=0, tiled=True)  98.5 us
    dot_general x2, matrix products, shards(): jnp.einsum('sjmh,jdh->sjmd', gate_grad, gate_local, preferred_element_typ...  30.7 us
    gather x4, local copies, waits for them, and re-layouts, pack(): source[slot_token]  18.9 us
    another operation x6, other arithmetic  18.3 us
    dot_general x2, matrix products, shards(): jnp.einsum('sjmh,jdh->sjmd', up_grad, up_local, preferred_element_type=jn...  16.9 us
    dot_general x2, matrix products, shards(): jnp.einsum('sjmd,jhd->sjmh', expert_grad_rows, down_local, preferred_elem...  15.5 us
  transfers between devices with their start and end apart: 5, of which 4 were waited for; matrix products, arithmetic and copies ran while one was open for 7% of the time, Pallas kernels for 0%

commit v1 on v0

v1 whole, which is shorter than its diff:
```python
import functools

import jax
import jax.numpy as jnp
from jax import lax
from jax.experimental import pallas as pl
from jax.experimental.pallas import tpu as pltpu
from jax.sharding import PartitionSpec as P

MOST = 40
PAIR = 2 * MOST
F32 = jnp.float32
BF16 = jnp.bfloat16


def dot(a, b, dims):
    return lax.dot_general(a, b, (dims, ((), ())), preferred_element_type=F32)


def expanded(local):
    slot = lax.broadcasted_iota(jnp.int32, (local, local * PAIR), 1)
    first = lax.broadcasted_iota(jnp.int32, (local, local * PAIR), 0) * PAIR
    return jnp.where((slot >= first) & (slot < first + PAIR), 1.0, 0.0).astype(BF16)


def forward_kernel(sources, local, step, base_ref, *refs):
    x_refs, refs = refs[:sources], refs[sources:]
    meta_refs, refs = refs[:sources], refs[sources:]
    gate_ref, up_ref, a_ref, b_ref, pick_ref, place_ref, rows_ref, weight_ref = refs
    tokens = x_refs[0].shape[0]
    width = x_refs[0].shape[1]
    top = meta_refs[0].shape[1] // 2

    @pl.when(pl.program_id(0) == 0)
    def _():
        mine = lax.broadcasted_iota(jnp.int32, (local, tokens), 0).astype(F32) + base_ref[0].astype(F32)
        before = (
            lax.broadcasted_iota(jnp.int32, (tokens, tokens), 0)
            < lax.broadcasted_iota(jnp.int32, (tokens, tokens), 1)
        )
        before = jnp.where(before, 1.0, 0.0).astype(BF16)
        table = expanded(local)
        for pair in range(sources // 2):
            targets, weights = [], []
            for half in range(2):
                meta = meta_refs[2 * pair + half][step]
                named = jnp.zeros((local, tokens), F32)
                weight = jnp.zeros((local, tokens), F32)
                for k in range(top):
                    same = meta[k : k + 1] == mine
                    named = jnp.where(same, 1.0, named)
                    weight = jnp.where(same, meta[top + k : top + k + 1], weight)
                position = dot(named.astype(BF16), before, ((1,), (0,)))
                targets.append(jnp.where(named > 0.5, position + half * MOST, -1.0))
                weights.append(weight)
            target = jnp.concatenate(targets, axis=1).astype(BF16)
            weight = jnp.concatenate(weights, axis=1)
            spread = dot(table, target, ((0,), (0,)))
            slot = lax.broadcasted_iota(jnp.int32, spread.shape, 0) % PAIR
            picked = spread == slot.astype(F32)
            pick = jnp.where(picked, 1.0, 0.0)
            pick_ref[pair] = pick.astype(BF16)
            spread_t = dot(target, table, ((0,), (0,)))
            slot_t = lax.broadcasted_iota(jnp.int32, spread_t.shape, 1) % PAIR
            place_ref[pair] = jnp.where(spread_t == slot_t.astype(F32), 1.0, 0.0).astype(BF16)
            for e in range(local):
                block = jnp.where(picked[e * PAIR : (e + 1) * PAIR], weight[e : e + 1], 0.0)
                weight_ref[e, pair * PAIR : (pair + 1) * PAIR, :] = jnp.sum(block, axis=1, keepdims=True)
            source = jnp.concatenate([x_refs[2 * pair][...], x_refs[2 * pair + 1][...]], axis=0)
            for n in range(0, width, 256):
                rows = dot(pick_ref[pair], source[:, n : n + 256], ((1,), (0,))).astype(BF16)
                rows_ref[:, pair * PAIR : (pair + 1) * PAIR, n : n + 256] = rows.reshape(local, PAIR, 256)

    e = pl.program_id(0)
    rows = rows_ref[e]
    gate = dot(rows, gate_ref[0], ((1,), (0,)))
    up = dot(rows, up_ref[0], ((1,), (0,)))
    sig = 1.0 / (1.0 + jnp.exp(-gate))
    scaled = sig * weight_ref[e]
    a_ref[0] = up * scaled * (1.0 + gate * (1.0 - sig))
    b_ref[0] = gate * scaled


def backward_kernel(sources, local, *refs):
    g_refs, refs = refs[:sources], refs[sources:]
    a_ref, b_ref, pick_ref, place_ref, gate_ref, up_ref, down_ref = refs[:7]
    out_refs, refs = refs[7 : 7 + sources], refs[7 + sources :]
    rows_ref, back_ref = refs
    tokens, width = g_refs[0].shape
    e = pl.program_id(0)

    @pl.when(e == 0)
    def _():
        for pair in range(sources // 2):
            source = jnp.concatenate([g_refs[2 * pair][...], g_refs[2 * pair + 1][...]], axis=0)
            for n in range(0, width, 256):
                rows = dot(pick_ref[pair], source[:, n : n + 256], ((1,), (0,))).astype(BF16)
                rows_ref[:, pair * PAIR : (pair + 1) * PAIR, n : n + 256] = rows.reshape(local, PAIR, 256)

    hidden = dot(rows_ref[e], down_ref[0], ((1,), (1,)))
    gate_grad = (hidden * a_ref[0]).astype(BF16)
    up_grad = (hidden * b_ref[0]).astype(BF16)
    row = dot(gate_grad, gate_ref[0], ((1,), (1,))) + dot(up_grad, up_ref[0], ((1,), (1,)))
    row = row.astype(BF16)
    for pair in range(sources // 2):
        back_ref[pair, e] = row[pair * PAIR : (pair + 1) * PAIR]

    @pl.when(e == local - 1)
    def _():
        for pair in range(sources // 2):
            for n in range(0, width, 256):
                rows = back_ref[pair, :, :, n : n + 256].reshape(local * PAIR, 256)
                total = dot(place_ref[pair], rows, ((1,), (0,)))
                for half in range(2):
                    out = out_refs[2 * pair + half]
                    out[:, n : n + 256] = total[half * tokens : (half + 1) * tokens].astype(out.dtype)


def whole(shape):
    return pl.BlockSpec(shape, lambda e: (0,) * len(shape))


def one(shape):
    return pl.BlockSpec((1,) + shape[1:], lambda e: (e,) + (0,) * (len(shape) - 1))


def forward(step, base, xs, metas, gate, up):
    sources, local = len(xs), gate.shape[0]
    tokens, width = xs[0].shape
    hidden = gate.shape[2]
    rows = sources * MOST
    factor = jax.ShapeDtypeStruct((local, rows, hidden), F32)
    pick = jax.ShapeDtypeStruct((sources // 2, local * PAIR, 2 * tokens), BF16)
    place = jax.ShapeDtypeStruct((sources // 2, 2 * tokens, local * PAIR), BF16)
    outs = (factor, factor, pick, place)
    return pl.pallas_call(
        functools.partial(forward_kernel, sources, local, step),
        grid=(local,),
        in_specs=[pl.BlockSpec(memory_space=pltpu.SMEM)]
        + [whole(x.shape) for x in xs]
        + [whole(m.shape) for m in metas]
        + [one(gate.shape), one(up.shape)],
        out_specs=(one(factor.shape), one(factor.shape), whole(pick.shape), whole(place.shape)),
        out_shape=outs,
        scratch_shapes=[
            pltpu.VMEM((local, rows, width), BF16),
            pltpu.VMEM((local, rows, 1), F32),
        ],
        compiler_params=pltpu.CompilerParams(vmem_limit_bytes=32 * 1024 * 1024),
        cost_estimate=pl.CostEstimate(
            flops=4 * local * rows * width * hidden,
            bytes_accessed=4 * local * width * hidden,
            transcendentals=local * rows * hidden,
        ),
        name="forward",
    )(base, *xs, *metas, gate, up)


def backward(gs, a, b, pick, place, gate, up, down):
    sources, local = len(gs), gate.shape[0]
    tokens, width = gs[0].shape
    hidden = gate.shape[2]
    rows = sources * MOST
    outs = tuple(
        jax.ShapeDtypeStruct((tokens, width), F32 if k == 0 else BF16) for k in range(sources)
    )
    return pl.pallas_call(
        functools.partial(backward_kernel, sources, local),
        grid=(local,),
        in_specs=[whole(g.shape) for g in gs]
        + [one(a.shape), one(b.shape), whole(pick.shape), whole(place.shape)]
        + [one(gate.shape), one(up.shape), one(down.shape)],
        out_specs=tuple(whole(o.shape) for o in outs),
        out_shape=outs,
        scratch_shapes=[
            pltpu.VMEM((local, rows, width), BF16),
            pltpu.VMEM((sources // 2, local, PAIR, width), BF16),
        ],
        compiler_params=pltpu.CompilerParams(vmem_limit_bytes=40 * 1024 * 1024),
        cost_estimate=pl.CostEstimate(
            flops=6 * local * rows * width * hidden,
            bytes_accessed=6 * local * width * hidden,
            transcendentals=0,
        ),
        name="backward",
    )(*gs, a, b, pick, place, gate, up, down)


def moved(value, by):
    count = lax.axis_size("expert")
    return lax.ppermute(value, "expert", [(i, (i + by) % count) for i in range(count)])


def swapped(value):
    return lax.ppermute(value, "expert", [(i, i ^ 1) for i in range(lax.axis_size("expert"))])


def moved_back(value, by):
    sections, count = lax.axis_size("section"), lax.axis_size("expert")
    pairs = [
        (s * count + i, ((s - 1) % sections) * count + (i + by) % count)
        for s in range(sections)
        for i in range(count)
    ]
    return lax.ppermute(value, ("section", "expert"), pairs)


def gathered(value):
    count = lax.axis_size("expert")
    if count != 4:
        return [value] + [moved(value, k) for k in range(1, count)]
    left, right = moved(value, 1), moved(value, -1)
    odd = lax.axis_index("expert") % 2 == 1
    far = swapped(jnp.where(odd, right, left))
    return [value, left, far, right]


def scattered(parts, kept, move):
    count = lax.axis_size("expert")
    if count != 4:
        sent = [(parts[k], -k) for k in range(1, count)]
    else:
        _, left, far, right = parts
        far = swapped(far).astype(F32)
        odd = lax.axis_index("expert") % 2 == 1
        added_left = (left.astype(F32) + far).astype(BF16)
        added_right = (right.astype(F32) + far).astype(BF16)
        sent = [(jnp.where(odd, left, added_left), -1), (jnp.where(odd, added_right, right), 1)]
    total = kept + parts[0]
    if move is moved_back:
        total = moved_back(total.astype(BF16), 0).astype(F32)
    for part, by in sent:
        total = total + move(part, by).astype(F32)
    return total.astype(BF16)


def shards(grad_out, saved_inputs, routes, gate_weights, w_gate, w_up, w_down):
    gate, up, down = w_gate[0], w_up[0], w_down[0]
    local = gate.shape[0]
    steps = routes.shape[1]
    base = (lax.axis_index("expert") * local).astype(jnp.int32).reshape(1)
    meta = jnp.concatenate(
        [routes[0].astype(F32).transpose(0, 2, 1), gate_weights[0].transpose(0, 2, 1)], axis=1
    )
    metas = gathered(meta)
    grad = grad_out[0]
    for step in range(steps):
        xs = gathered(saved_inputs[0, step])
        a, b, pick, place = forward(step, base, xs, metas, gate, up)
        gs = gathered(grad)
        parts = backward(gs, a, b, pick, place, gate, up, down)
        last = step + 1 == steps
        grad = scattered(parts, grad.astype(F32), moved if last else moved_back)
    return grad[None]


def solution(mesh):
    placed = (
        P("section", "expert", None),
        P("section", None, "expert", None),
        P("section", None, "expert", None),
        P("section", None, "expert", None),
        P("section", "expert", None, None),
        P("section", "expert", None, None),
        P("section", "expert", None, None),
    )
    return jax.shard_map(
        shards, mesh=mesh, in_specs=placed, out_specs=P("section", "expert", None), check_vma=False
    )
```

time: 511 us -> 164 us (0.32)
  waiting for transfers between devices: 201 us -> 65.7 us
  blocking collectives: 129 us -> 0 us
  matrix products: 77.8 us -> 0 us
  Pallas kernels: 0 us -> 50.7 us
  local copies, waits for them, and re-layouts: 53.6 us -> 4.46 us
  other arithmetic: 32 us -> 2.87 us
  starting transfers between devices: 16.1 us -> 39.7 us
    all_to_all x4 -> x0, waiting for transfers between devices: 201 us -> none  [the longest x2 103 us: shards(): lax.all_to_all(grad_rows, 'expert', split_axis=0, concat_axis=0, tiled=True)]
    all_to_all x2 -> x0, blocking collectives: 129 us -> none  [shards(): lax.all_to_all(input_rows, 'expert', split_axis=0, concat_axis=0, tiled=T...]
    dot_general x8 -> x0, matrix products: 77.8 us -> none  [the longest x2 30.7 us: shards(): jnp.einsum('sjmh,jdh->sjmd', gate_grad, gate_local, preferred_element_typ...]
    ppermute x1 -> x22, waiting for transfers between devices: 0.01 us -> 65.7 us  [the longest x12 33.3 us: moved(): lax.ppermute(value, 'expert', [(i, (i + by) % count) for i in range(count)])]
    pallas_call x0 -> x4, Pallas kernels: none -> 50.7 us  [the longest x2 32 us: backward(): pl.pallas_call(functools.partial(backward_kernel, sources, local), grid=(...]
    ppermute x1 -> x22, starting transfers between devices: 1.15 us -> 39.7 us  [the longest x12 26.8 us: moved(): lax.ppermute(value, 'expert', [(i, (i + by) % count) for i in range(count)])]
    gather x6 -> x0, local copies, waits for them, and re-layouts: 29.6 us -> none  [the longest x4 18.9 us: pack(): source[slot_token]]
    another operation x6 -> x0, other arithmetic: 18.3 us -> none
  transfers between devices with their start and end apart: 5 -> 22, of which waited for: 4 -> 14; matrix products, arithmetic and copies ran while one was open for 7% -> 1% of each run, Pallas kernels for 0% -> 11%
where the time goes in v1:
time: 164 us
  waiting for transfers between devices  65.7 us (40%)
  Pallas kernels  50.7 us (31%)
  starting transfers between devices  39.7 us (24%)
  local copies, waits for them, and re-layouts  4.46 us (3%)
  other arithmetic  2.87 us (2%)
    ppermute x12, waiting for transfers between devices, moved(): lax.ppermute(value, 'expert', [(i, (i + by) % count) for i in range(count)])  33.3 us
    pallas_call x2, Pallas kernels, backward(): pl.pallas_call(functools.partial(backward_kernel, sources, local), grid=(...  32 us
    ppermute x12, starting transfers between devices, moved(): lax.ppermute(value, 'expert', [(i, (i + by) % count) for i in range(count)])  26.8 us
    ppermute x7, waiting for transfers between devices, swapped(): lax.ppermute(value, 'expert', [(i, i ^ 1) for i in range(lax.axis_size('e...  25.4 us
    pallas_call x2, Pallas kernels, forward(): pl.pallas_call(functools.partial(forward_kernel, sources, local, step), g...  18.7 us
    ppermute x7, starting transfers between devices, swapped(): lax.ppermute(value, 'expert', [(i, i ^ 1) for i in range(lax.axis_size('e...  9.23 us
    ppermute x3, waiting for transfers between devices, moved_back(): return lax.ppermute(value, ('section', 'expert'), pairs)  6.94 us
    ppermute x3, starting transfers between devices, moved_back(): return lax.ppermute(value, ('section', 'expert'), pairs)  3.74 us
  transfers between devices with their start and end apart: 22, of which 14 were waited for; matrix products, arithmetic and copies ran while one was open for 1% of the time, Pallas kernels for 11%

profile of v1, /device:TPU:0, one launch (start us, length us, event | category | flops | bytes accessed | tf_op | source)
XLA Modules:
  0.0 163.7 jit_solution(13496359354731256532)
XLA Ops:
  0.0 1.1 slice_bitcast_fusion
  1.1 3.1 %collective-permute-start.3 = (bf16[128,1024]{1,0:T(8,128)(2,1)S(1)}, bf16[128,1024]{1,0:T(8,128)(2,1)S(1)}, u32[]{:S(2)}, u32[]{:S(2)}) collective-permute-start(bf16[128,1024]{1,0:T(8,128)(2,1)S(1)} %get-tuple-element.38.refs_0_), channel_id=1, source_target_pairs={{0,1},{1,2},{2,3},{3,0},{4,5},{5,6},{6,7},{7,4},{8,9},{9,10},{10,1... | collective-permute-start | bytes 786440 | tf_op jit(solution)/shard_map/ppermute | solution.py:191
  4.1 2.1 %collective-permute-start.4 = (bf16[128,1024]{1,0:T(8,128)(2,1)S(1)}, bf16[128,1024]{1,0:T(8,128)(2,1)S(1)}, u32[]{:S(2)}, u32[]{:S(2)}) collective-permute-start(bf16[128,1024]{1,0:T(8,128)(2,1)S(1)} %get-tuple-element.38.refs_0_), channel_id=1, source_target_pairs={{0,3},{1,0},{2,1},{3,2},{4,7},{5,4},{6,5},{7,6},{8,11},{9,8},{10,9... | collective-permute-start | bytes 786440 | tf_op jit(solution)/shard_map/ppermute | solution.py:191
  6.2 0.7 convert_bitcast_fusion
  6.9 0.7 pad_maximum_fusion.refs_4_
  7.6 0.0 collective-permute-start.6
  7.6 3.8 %collective-permute-start.7 = (f32[2,16,128]{2,1,0:T(8,128)S(1)}, f32[2,16,128]{2,1,0:T(8,128)S(1)}, u32[]{:S(2)}, u32[]{:S(2)}) collective-permute-start(f32[2,16,128]{2,1,0:T(8,128)S(1)} %pad_maximum_fusion.refs_4_), channel_id=1, source_target_pairs={{0,3},{1,0},{2,1},{3,2},{4,7},{5,4},{6,5},{7,6},{8,11},{9,8},{10,9... | collective-permute-start | bytes 49160 | tf_op jit(solution)/shard_map/ppermute | solution.py:191
  11.5 1.9 %collective-permute-done.3.refs_1_ = bf16[128,1024]{1,0:T(8,128)(2,1)S(1)} collective-permute-done((bf16[128,1024]{1,0:T(8,128)(2,1)S(1)}, bf16[128,1024]{1,0:T(8,128)(2,1)S(1)}, u32[]{:S(2)}, u32[]{:S(2)}) %collective-permute-start.3) | collective-permute-done | bytes 262176 | tf_op jit(solution)/shard_map/ppermute | solution.py:191
  13.3 7.8 %collective-permute-start.1 = (bf16[128,1024]{1,0:T(8,128)(2,1)}, bf16[128,1024]{1,0:T(8,128)(2,1)S(1)}, u32[]{:S(2)}, u32[]{:S(2)}) collective-permute-start(bf16[128,1024]{1,0:T(8,128)(2,1)} %bitcast.26), channel_id=1, source_target_pairs={{0,3},{1,0},{2,1},{3,2},{4,7},{5,4},{6,5},{7,6},{8,11},{9,8},{10,9... | collective-permute-start | bytes 786440 | tf_op jit(solution)/shard_map/ppermute | solution.py:191
  21.2 0.1 collective-permute-start.5
  21.3 2.4 %collective-permute-done.7.refs_7_ = f32[2,16,128]{2,1,0:T(8,128)S(1)} collective-permute-done((f32[2,16,128]{2,1,0:T(8,128)S(1)}, f32[2,16,128]{2,1,0:T(8,128)S(1)}, u32[]{:S(2)}, u32[]{:S(2)}) %collective-permute-start.7) | collective-permute-done | bytes 16416 | tf_op jit(solution)/shard_map/ppermute | solution.py:191
  23.7 1.6 collective-permute-done.refs_1_
  25.3 4.9 %collective-permute-done.1.refs_3_ = bf16[128,1024]{1,0:T(8,128)(2,1)S(1)} collective-permute-done((bf16[128,1024]{1,0:T(8,128)(2,1)}, bf16[128,1024]{1,0:T(8,128)(2,1)S(1)}, u32[]{:S(2)}, u32[]{:S(2)}) %collective-permute-start.1) | collective-permute-done | bytes 262176 | tf_op jit(solution)/shard_map/ppermute | solution.py:191
  30.2 0.5 collective-permute-start.2
  30.7 5.5 %collective-permute-done.8.refs_6_ = f32[2,16,128]{2,1,0:T(8,128)S(1)} collective-permute-done((f32[2,16,128]{2,1,0:T(8,128)S(1)}, f32[2,16,128]{2,1,0:T(8,128)S(1)}, u32[]{:S(2)}, u32[]{:S(2)}) %collective-permute-start.8) | collective-permute-done | bytes 16416 | tf_op jit(solution)/shard_map/ppermute | solution.py:195
  36.2 3.4 %copy-done = bf16[1,8,1024,512]{3,2,1,0:T(8,128)(2,1)S(1)} copy-done((bf16[1,8,1024,512]{3,2,1,0:T(8,128)(2,1)S(1)}, bf16[1,8,1024,512]{3,2,1,0:T(8,128)(2,1)}, u32[]{:S(2)}) %copy-start) | copy-done | bytes 8388632
  39.5 9.4 %forward.2 = (f32[8,160,512]{2,1,0:T(8,128)S(1)}, f32[8,160,512]{2,1,0:T(8,128)S(1)}, bf16[2,640,256]{2,1,0:T(8,128)(2,1)S(1)}, bf16[2,256,640]{2,1,0:T(8,128)(2,1)S(1)}) custom-call(s32[1]{0:T(128)} %bitcast.1.base_ref, bf16[128,1024]{1,0:T(8,128)(2,1)S(1)} %get-tuple-element.38.refs_0_, bf16[128,1024]{1,0:T(8,128)(2,1)S(1)} %collective-permute-done.3.refs_1_, ...), custom_call_target="tpu_custom_call" | custom-call | flops 2684354560 | bytes 16777216 | tf_op jit(solution)/shard_map/forward/pallas_call | solution.py:136
  48.9 0.0 slice-start
  49.0 16.1 %backward.2 = (f32[128,1024]{1,0:T(8,128)S(1)}, bf16[128,1024]{1,0:T(8,128)(2,1)S(1)}, bf16[128,1024]{1,0:T(8,128)(2,1)S(1)}, bf16[128,1024]{1,0:T(8,128)(2,1)S(1)}) custom-call(bf16[128,1024]{1,0:T(8,128)(2,1)S(1)} %bitcast.27, bf16[128,1024]{1,0:T(8,128)(2,1)S(1)} %collective-permute-done.refs_1_, bf16[128,1024]{1,0:T(8,128)(2,1)S(1)} %collective-permute-done.2.refs_2_, ...), custom_call_target="tpu_custom_call" | custom-call | flops 4026531840 | bytes 25165824 | tf_op jit(solution)/shard_map/backward/pallas_call | solution.py:167
  65.1 0.9 collective-permute-start.10
  65.9 0.1 add_convert_fusion.2
  66.0 0.1 collective-permute-start.9
  66.1 6.0 %collective-permute-done.10 = bf16[128,1024]{1,0:T(8,128)(2,1)S(1)} collective-permute-done((bf16[128,1024]{1,0:T(8,128)(2,1)S(1)}, bf16[128,1024]{1,0:T(8,128)(2,1)S(1)}, u32[]{:S(2)}, u32[]{:S(2)}) %collective-permute-start.10) | collective-permute-done | bytes 262176 | tf_op jit(solution)/shard_map/ppermute | solution.py:195
  72.1 0.2 fusion.7
  72.2 0.4 collective-permute-start.11
  72.6 3.3 %collective-permute-start.12 = (bf16[128,1024]{1,0:T(8,128)(2,1)S(1)}, bf16[128,1024]{1,0:T(8,128)(2,1)S(1)}, u32[]{:S(2)}, u32[]{:S(2)}) collective-permute-start(bf16[128,1024]{1,0:T(8,128)(2,1)S(1)} %get-tuple-element.42), channel_id=1, source_target_pairs={{0,29},{1,30},{2,31},{3,28},{4,1},{5,2},{6,3},{7,0},{8,5},{9,6},{1... | collective-permute-start | bytes 786440 | tf_op jit(solution)/shard_map/ppermute | solution.py:205
  75.9 0.3 collective-permute-start.16
  76.2 3.7 %collective-permute-start.17 = (bf16[128,1024]{1,0:T(8,128)(2,1)S(1)}, bf16[128,1024]{1,0:T(8,128)(2,1)S(1)}, u32[]{:S(2)}, u32[]{:S(2)}) collective-permute-start(bf16[128,1024]{1,0:T(8,128)(2,1)S(1)} %get-tuple-element.37.refs_0_), channel_id=1, source_target_pairs={{0,3},{1,0},{2,1},{3,2},{4,7},{5,4},{6,5},{7,6},{8,11},{9,8},{10,9... | collective-permute-start | bytes 786440 | tf_op jit(solution)/shard_map/ppermute | solution.py:191
  79.9 1.0 collective-permute-done.11
  80.9 6.0 %collective-permute-done.12 = bf16[128,1024]{1,0:T(8,128)(2,1)S(1)} collective-permute-done((bf16[128,1024]{1,0:T(8,128)(2,1)S(1)}, bf16[128,1024]{1,0:T(8,128)(2,1)S(1)}, u32[]{:S(2)}, u32[]{:S(2)}) %collective-permute-start.12) | collective-permute-done | bytes 262176 | tf_op jit(solution)/shard_map/ppermute | solution.py:205
  86.8 0.1 add_convert_fusion.1.refs_0_
  87.0 1.9 %collective-permute-start.13 = (bf16[128,1024]{1,0:T(8,128)(2,1)S(1)}, bf16[128,1024]{1,0:T(8,128)(2,1)S(1)}, u32[]{:S(2)}, u32[]{:S(2)}) collective-permute-start(bf16[128,1024]{1,0:T(8,128)(2,1)S(1)} %add_convert_fusion.1.refs_0_), channel_id=1, source_target_pairs={{0,1},{1,2},{2,3},{3,0},{4,5},{5,6},{6,7},{7,4},{8,9},{9,10},{10,1... | collective-permute-start | bytes 786440 | tf_op jit(solution)/shard_map/ppermute | solution.py:191
  88.9 1.9 %collective-permute-start.14 = (bf16[128,1024]{1,0:T(8,128)(2,1)S(1)}, bf16[128,1024]{1,0:T(8,128)(2,1)S(1)}, u32[]{:S(2)}, u32[]{:S(2)}) collective-permute-start(bf16[128,1024]{1,0:T(8,128)(2,1)S(1)} %add_convert_fusion.1.refs_0_), channel_id=1, source_target_pairs={{0,3},{1,0},{2,1},{3,2},{4,7},{5,4},{6,5},{7,6},{8,11},{9,8},{10,9... | collective-permute-start | bytes 786440 | tf_op jit(solution)/shard_map/ppermute | solution.py:191
  90.9 2.1 %collective-permute-done.16.refs_1_ = bf16[128,1024]{1,0:T(8,128)(2,1)S(1)} collective-permute-done((bf16[128,1024]{1,0:T(8,128)(2,1)S(1)}, bf16[128,1024]{1,0:T(8,128)(2,1)S(1)}, u32[]{:S(2)}, u32[]{:S(2)}) %collective-permute-start.16) | collective-permute-done | bytes 262176 | tf_op jit(solution)/shard_map/ppermute | solution.py:191
  92.9 4.4 %collective-permute-done.17.refs_3_ = bf16[128,1024]{1,0:T(8,128)(2,1)S(1)} collective-permute-done((bf16[128,1024]{1,0:T(8,128)(2,1)S(1)}, bf16[128,1024]{1,0:T(8,128)(2,1)S(1)}, u32[]{:S(2)}, u32[]{:S(2)}) %collective-permute-start.17) | collective-permute-done | bytes 262176 | tf_op jit(solution)/shard_map/ppermute | solution.py:191
  97.4 7.1 %collective-permute-start.18 = (bf16[128,1024]{1,0:T(8,128)(2,1)S(1)}, bf16[128,1024]{1,0:T(8,128)(2,1)S(1)}, u32[]{:S(2)}, u32[]{:S(2)}) collective-permute-start(bf16[128,1024]{1,0:T(8,128)(2,1)S(1)} %broadcast_select_fusion), channel_id=1, source_target_pairs={{0,1},{1,0},{2,3},{3,2},{4,5},{5,4},{6,7},{7,6},{8,9},{9,8},{10,11... | collective-permute-start | bytes 786440 | tf_op jit(solution)/shard_map/ppermute | solution.py:195
  104.4 4.1 %collective-permute-done.14.refs_3_ = bf16[128,1024]{1,0:T(8,128)(2,1)S(1)} collective-permute-done((bf16[128,1024]{1,0:T(8,128)(2,1)S(1)}, bf16[128,1024]{1,0:T(8,128)(2,1)S(1)}, u32[]{:S(2)}, u32[]{:S(2)}) %collective-permute-start.14) | collective-permute-done | bytes 262176 | tf_op jit(solution)/shard_map/ppermute | solution.py:191
  108.6 0.6 collective-permute-start.15
  109.2 5.0 %collective-permute-done.18.refs_2_ = bf16[128,1024]{1,0:T(8,128)(2,1)S(1)} collective-permute-done((bf16[128,1024]{1,0:T(8,128)(2,1)S(1)}, bf16[128,1024]{1,0:T(8,128)(2,1)S(1)}, u32[]{:S(2)}, u32[]{:S(2)}) %collective-permute-start.18) | collective-permute-done | bytes 262176 | tf_op jit(solution)/shard_map/ppermute | solution.py:195
  114.2 9.3 %forward.3 = (f32[8,160,512]{2,1,0:T(8,128)S(1)}, f32[8,160,512]{2,1,0:T(8,128)S(1)}, bf16[2,640,256]{2,1,0:T(8,128)(2,1)S(1)}, bf16[2,256,640]{2,1,0:T(8,128)(2,1)S(1)}) custom-call(s32[1]{0:T(128)} %bitcast.1.base_ref, bf16[128,1024]{1,0:T(8,128)(2,1)S(1)} %get-tuple-element.37.refs_0_, bf16[128,1024]{1,0:T(8,128)(2,1)S(1)} %collective-permute-done.16.refs_1_, ...), custom_call_target="tpu_custom_call" | custom-call | flops 2684354560 | bytes 16777216 | tf_op jit(solution)/shard_map/forward/pallas_call | solution.py:136
  123.6 15.9 %backward.3 = (f32[128,1024]{1,0:T(8,128)S(1)}, bf16[128,1024]{1,0:T(8,128)(2,1)S(1)}, bf16[128,1024]{1,0:T(8,128)(2,1)S(1)}, bf16[128,1024]{1,0:T(8,128)(2,1)S(1)}) custom-call(bf16[128,1024]{1,0:T(8,128)(2,1)S(1)} %add_convert_fusion.1.refs_0_, bf16[128,1024]{1,0:T(8,128)(2,1)S(1)} %collective-permute-done.13.refs_1_, ...), custom_call_target="tpu_custom_call" | custom-call | flops 4026531840 | bytes 25165824 | tf_op jit(solution)/shard_map/backward/pallas_call | solution.py:167
  139.5 0.2 collective-permute-start.19
  139.6 9.0 %collective-permute-done.19 = bf16[128,1024]{1,0:T(8,128)(2,1)S(1)} collective-permute-done((bf16[128,1024]{1,0:T(8,128)(2,1)S(1)}, bf16[128,1024]{1,0:T(8,128)(2,1)S(1)}, u32[]{:S(2)}, u32[]{:S(2)}) %collective-permute-start.19) | collective-permute-done | bytes 262176 | tf_op jit(solution)/shard_map/ppermute | solution.py:195
  148.7 0.2 fusion.5
  148.8 1.3 collective-permute-start.20
  150.1 0.8 collective-permute-start.21
  150.9 11.9 %collective-permute-done.20 = bf16[128,1024]{1,0:T(8,128)(2,1)S(1)} collective-permute-done((bf16[128,1024]{1,0:T(8,128)(2,1)S(1)}, bf16[128,1024]{1,0:T(8,128)(2,1)S(1)}, u32[]{:S(2)}, u32[]{:S(2)}) %collective-permute-start.20) | collective-permute-done | bytes 262176 | tf_op jit(solution)/shard_map/ppermute | solution.py:191
  162.8 0.9 fusion.8
  (22 shorter events, 0.2 us)
Async XLA Ops:
  1.1 12.3 %collective-permute-start.3 = (bf16[128,1024]{1,0:T(8,128)(2,1)S(1)}, bf16[128,1024]{1,0:T(8,128)(2,1)S(1)}, u32[]{:S(2)}, u32[]{:S(2)}) collective-permute-start(bf16[128,1024]{1,0:T(8,128)(2,1)S(1)} %get-tuple-element.38.refs_0_), channel_id=1, source_target_pairs={{0,1},{1,2},{2,3},{3,0},{4,5},{5,6},{6,7},{7,4},{8,9},{9,10},{10,1... | collective-permute-start | bytes 786440 | tf_op jit(solution)/shard_map/ppermute | solution.py:191
  4.1 17.0 %collective-permute-start.4 = (bf16[128,1024]{1,0:T(8,128)(2,1)S(1)}, bf16[128,1024]{1,0:T(8,128)(2,1)S(1)}, u32[]{:S(2)}, u32[]{:S(2)}) collective-permute-start(bf16[128,1024]{1,0:T(8,128)(2,1)S(1)} %get-tuple-element.38.refs_0_), channel_id=1, source_target_pairs={{0,3},{1,0},{2,1},{3,2},{4,7},{5,4},{6,5},{7,6},{8,11},{9,8},{10,9... | collective-permute-start | bytes 786440 | tf_op jit(solution)/shard_map/ppermute | solution.py:191
  7.6 13.6 %collective-permute-start.6 = (f32[2,16,128]{2,1,0:T(8,128)S(1)}, f32[2,16,128]{2,1,0:T(8,128)S(1)}, u32[]{:S(2)}, u32[]{:S(2)}) collective-permute-start(f32[2,16,128]{2,1,0:T(8,128)S(1)} %pad_maximum_fusion.refs_4_), channel_id=1, source_target_pairs={{0,1},{1,2},{2,3},{3,0},{4,5},{5,6},{6,7},{7,4},{8,9},{9,10},{10,1... | collective-permute-start | bytes 49160 | tf_op jit(solution)/shard_map/ppermute | solution.py:191
  7.6 16.1 %collective-permute-start.7 = (f32[2,16,128]{2,1,0:T(8,128)S(1)}, f32[2,16,128]{2,1,0:T(8,128)S(1)}, u32[]{:S(2)}, u32[]{:S(2)}) collective-permute-start(f32[2,16,128]{2,1,0:T(8,128)S(1)} %pad_maximum_fusion.refs_4_), channel_id=1, source_target_pairs={{0,3},{1,0},{2,1},{3,2},{4,7},{5,4},{6,5},{7,6},{8,11},{9,8},{10,9... | collective-permute-start | bytes 49160 | tf_op jit(solution)/shard_map/ppermute | solution.py:191
  11.5 13.8 %collective-permute-start = (bf16[128,1024]{1,0:T(8,128)(2,1)}, bf16[128,1024]{1,0:T(8,128)(2,1)S(1)}, u32[]{:S(2)}, u32[]{:S(2)}) collective-permute-start(bf16[128,1024]{1,0:T(8,128)(2,1)} %bitcast.25), channel_id=1, source_target_pairs={{0,1},{1,2},{2,3},{3,0},{4,5},{5,6},{6,7},{7,4},{8,9},{9,10},{10,1... | collective-permute-start | bytes 786440 | tf_op jit(solution)/shard_map/ppermute | solution.py:191
  13.3 16.8 %collective-permute-start.1 = (bf16[128,1024]{1,0:T(8,128)(2,1)}, bf16[128,1024]{1,0:T(8,128)(2,1)S(1)}, u32[]{:S(2)}, u32[]{:S(2)}) collective-permute-start(bf16[128,1024]{1,0:T(8,128)(2,1)} %bitcast.26), channel_id=1, source_target_pairs={{0,3},{1,0},{2,1},{3,2},{4,7},{5,4},{6,5},{7,6},{8,11},{9,8},{10,9... | collective-permute-start | bytes 786440 | tf_op jit(solution)/shard_map/ppermute | solution.py:191
  21.2 15.0 %collective-permute-start.5 = (bf16[128,1024]{1,0:T(8,128)(2,1)S(1)}, bf16[128,1024]{1,0:T(8,128)(2,1)S(1)}, u32[]{:S(2)}, u32[]{:S(2)}) collective-permute-start(bf16[128,1024]{1,0:T(8,128)(2,1)S(1)} %broadcast_select_fusion.2), channel_id=1, source_target_pairs={{0,1},{1,0},{2,3},{3,2},{4,5},{5,4},{6,7},{7,6},{8,9},{9,8},{10,11... | collective-permute-start | bytes 786440 | tf_op jit(solution)/shard_map/ppermute | solution.py:195
  23.7 12.4 %collective-permute-start.8 = (f32[2,16,128]{2,1,0:T(8,128)S(1)}, f32[2,16,128]{2,1,0:T(8,128)S(1)}, u32[]{:S(2)}, u32[]{:S(2)}) collective-permute-start(f32[2,16,128]{2,1,0:T(8,128)S(1)} %broadcast_select_fusion.4), channel_id=1, source_target_pairs={{0,1},{1,0},{2,3},{3,2},{4,5},{5,4},{6,7},{7,6},{8,9},{9,8},{10,11... | collective-permute-start | bytes 49160 | tf_op jit(solution)/shard_map/ppermute | solution.py:195
  30.2 18.7 %collective-permute-start.2 = (bf16[128,1024]{1,0:T(8,128)(2,1)S(1)}, bf16[128,1024]{1,0:T(8,128)(2,1)S(1)}, u32[]{:S(2)}, u32[]{:S(2)}) collective-permute-start(bf16[128,1024]{1,0:T(8,128)(2,1)S(1)} %broadcast_select_fusion.3), channel_id=1, source_target_pairs={{0,1},{1,0},{2,3},{3,2},{4,5},{5,4},{6,7},{7,6},{8,9},{9,8},{10,11... | collective-permute-start | bytes 786440 | tf_op jit(solution)/shard_map/ppermute | solution.py:195
  36.2 3.4 %copy-start = (bf16[1,8,1024,512]{3,2,1,0:T(8,128)(2,1)S(1)}, bf16[1,8,1024,512]{3,2,1,0:T(8,128)(2,1)}, u32[]{:S(2)}) copy-start(bf16[1,8,1024,512]{3,2,1,0:T(8,128)(2,1)} %param.11) | copy-start | bytes 25165828
  39.5 9.4 %copy-start.1 = (bf16[1,128,1024]{2,1,0:T(8,128)(2,1)S(1)}, bf16[1,128,1024]{2,1,0:T(8,128)(2,1)}, u32[]{:S(2)}) copy-start(bf16[1,128,1024]{2,1,0:T(8,128)(2,1)} %param.7) | copy-start | bytes 786436
  48.9 65.3 %slice-start = ((s8[8388608]{0:T(1024)(128)(4,1)}), s8[4194304]{0:T(1024)(128)(4,1)S(1)}, s32[]{:S(2)}) async-start(s8[8388608]{0:T(1024)(128)(4,1)} %bitcast.22), calls=%async_computation | async-start | bytes 8388608
  49.0 65.3 %slice-start.1 = ((s8[8388608]{0:T(1024)(128)(4,1)}), s8[4194304]{0:T(1024)(128)(4,1)S(1)}, s32[]{:S(2)}) async-start(s8[8388608]{0:T(1024)(128)(4,1)} %bitcast.22), calls=%async_computation.1 | async-start | bytes 8388608
  65.1 7.0 %collective-permute-start.10 = (bf16[128,1024]{1,0:T(8,128)(2,1)S(1)}, bf16[128,1024]{1,0:T(8,128)(2,1)S(1)}, u32[]{:S(2)}, u32[]{:S(2)}) collective-permute-start(bf16[128,1024]{1,0:T(8,128)(2,1)S(1)} %get-tuple-element.27), channel_id=1, source_target_pairs={{0,1},{1,0},{2,3},{3,2},{4,5},{5,4},{6,7},{7,6},{8,9},{9,8},{10,11... | collective-permute-start | bytes 786440 | tf_op jit(solution)/shard_map/ppermute | solution.py:195
  66.0 13.9 %collective-permute-start.9 = (bf16[128,1024]{1,0:T(8,128)(2,1)S(1)}, bf16[128,1024]{1,0:T(8,128)(2,1)S(1)}, u32[]{:S(2)}, u32[]{:S(2)}) collective-permute-start(bf16[128,1024]{1,0:T(8,128)(2,1)S(1)} %add_convert_fusion.2), channel_id=1, source_target_pairs={{0,28},{1,29},{2,30},{3,31},{4,0},{5,1},{6,2},{7,3},{8,4},{9,5},{1... | collective-permute-start | bytes 786440 | tf_op jit(solution)/shard_map/ppermute | solution.py:205
  72.2 8.7 %collective-permute-start.11 = (bf16[128,1024]{1,0:T(8,128)(2,1)S(1)}, bf16[128,1024]{1,0:T(8,128)(2,1)S(1)}, u32[]{:S(2)}, u32[]{:S(2)}) collective-permute-start(bf16[128,1024]{1,0:T(8,128)(2,1)S(1)} %get-tuple-element.41), channel_id=1, source_target_pairs={{0,31},{1,28},{2,29},{3,30},{4,3},{5,0},{6,1},{7,2},{8,7},{9,4},{1... | collective-permute-start | bytes 786440 | tf_op jit(solution)/shard_map/ppermute | solution.py:205
  72.6 14.2 %collective-permute-start.12 = (bf16[128,1024]{1,0:T(8,128)(2,1)S(1)}, bf16[128,1024]{1,0:T(8,128)(2,1)S(1)}, u32[]{:S(2)}, u32[]{:S(2)}) collective-permute-start(bf16[128,1024]{1,0:T(8,128)(2,1)S(1)} %get-tuple-element.42), channel_id=1, source_target_pairs={{0,29},{1,30},{2,31},{3,28},{4,1},{5,2},{6,3},{7,0},{8,5},{9,6},{1... | collective-permute-start | bytes 786440 | tf_op jit(solution)/shard_map/ppermute | solution.py:205
  75.9 17.0 %collective-permute-start.16 = (bf16[128,1024]{1,0:T(8,128)(2,1)S(1)}, bf16[128,1024]{1,0:T(8,128)(2,1)S(1)}, u32[]{:S(2)}, u32[]{:S(2)}) collective-permute-start(bf16[128,1024]{1,0:T(8,128)(2,1)S(1)} %get-tuple-element.37.refs_0_), channel_id=1, source_target_pairs={{0,1},{1,2},{2,3},{3,0},{4,5},{5,6},{6,7},{7,4},{8,9},{9,10},{10,1... | collective-permute-start | bytes 786440 | tf_op jit(solution)/shard_map/ppermute | solution.py:191
  76.2 21.2 %collective-permute-start.17 = (bf16[128,1024]{1,0:T(8,128)(2,1)S(1)}, bf16[128,1024]{1,0:T(8,128)(2,1)S(1)}, u32[]{:S(2)}, u32[]{:S(2)}) collective-permute-start(bf16[128,1024]{1,0:T(8,128)(2,1)S(1)} %get-tuple-element.37.refs_0_), channel_id=1, source_target_pairs={{0,3},{1,0},{2,1},{3,2},{4,7},{5,4},{6,5},{7,6},{8,11},{9,8},{10,9... | collective-permute-start | bytes 786440 | tf_op jit(solution)/shard_map/ppermute | solution.py:191
  87.0 17.5 %collective-permute-start.13 = (bf16[128,1024]{1,0:T(8,128)(2,1)S(1)}, bf16[128,1024]{1,0:T(8,128)(2,1)S(1)}, u32[]{:S(2)}, u32[]{:S(2)}) collective-permute-start(bf16[128,1024]{1,0:T(8,128)(2,1)S(1)} %add_convert_fusion.1.refs_0_), channel_id=1, source_target_pairs={{0,1},{1,2},{2,3},{3,0},{4,5},{5,6},{6,7},{7,4},{8,9},{9,10},{10,1... | collective-permute-start | bytes 786440 | tf_op jit(solution)/shard_map/ppermute | solution.py:191
  88.9 19.7 %collective-permute-start.14 = (bf16[128,1024]{1,0:T(8,128)(2,1)S(1)}, bf16[128,1024]{1,0:T(8,128)(2,1)S(1)}, u32[]{:S(2)}, u32[]{:S(2)}) collective-permute-start(bf16[128,1024]{1,0:T(8,128)(2,1)S(1)} %add_convert_fusion.1.refs_0_), channel_id=1, source_target_pairs={{0,3},{1,0},{2,1},{3,2},{4,7},{5,4},{6,5},{7,6},{8,11},{9,8},{10,9... | collective-permute-start | bytes 786440 | tf_op jit(solution)/shard_map/ppermute | solution.py:191
  97.4 16.8 %collective-permute-start.18 = (bf16[128,1024]{1,0:T(8,128)(2,1)S(1)}, bf16[128,1024]{1,0:T(8,128)(2,1)S(1)}, u32[]{:S(2)}, u32[]{:S(2)}) collective-permute-start(bf16[128,1024]{1,0:T(8,128)(2,1)S(1)} %broadcast_select_fusion), channel_id=1, source_target_pairs={{0,1},{1,0},{2,3},{3,2},{4,5},{5,4},{6,7},{7,6},{8,9},{9,8},{10,11... | collective-permute-start | bytes 786440 | tf_op jit(solution)/shard_map/ppermute | solution.py:195
  108.6 14.9 %collective-permute-start.15 = (bf16[128,1024]{1,0:T(8,128)(2,1)S(1)}, bf16[128,1024]{1,0:T(8,128)(2,1)S(1)}, u32[]{:S(2)}, u32[]{:S(2)}) collective-permute-start(bf16[128,1024]{1,0:T(8,128)(2,1)S(1)} %broadcast_select_fusion.1), channel_id=1, source_target_pairs={{0,1},{1,0},{2,3},{3,2},{4,5},{5,4},{6,7},{7,6},{8,9},{9,8},{10,11... | collective-permute-start | bytes 786440 | tf_op jit(solution)/shard_map/ppermute | solution.py:195
  139.5 9.2 %collective-permute-start.19 = (bf16[128,1024]{1,0:T(8,128)(2,1)S(1)}, bf16[128,1024]{1,0:T(8,128)(2,1)S(1)}, u32[]{:S(2)}, u32[]{:S(2)}) collective-permute-start(bf16[128,1024]{1,0:T(8,128)(2,1)S(1)} %get-tuple-element.35), channel_id=1, source_target_pairs={{0,1},{1,0},{2,3},{3,2},{4,5},{5,4},{6,7},{7,6},{8,9},{9,8},{10,11... | collective-permute-start | bytes 786440 | tf_op jit(solution)/shard_map/ppermute | solution.py:195
  148.8 14.0 %collective-permute-start.20 = (bf16[128,1024]{1,0:T(8,128)(2,1)S(1)}, bf16[128,1024]{1,0:T(8,128)(2,1)S(1)}, u32[]{:S(2)}, u32[]{:S(2)}) collective-permute-start(bf16[128,1024]{1,0:T(8,128)(2,1)S(1)} %get-tuple-element.39), channel_id=1, source_target_pairs={{0,3},{1,0},{2,1},{3,2},{4,7},{5,4},{6,5},{7,6},{8,11},{9,8},{10,9... | collective-permute-start | bytes 786440 | tf_op jit(solution)/shard_map/ppermute | solution.py:191
  150.1 12.7 %collective-permute-start.21 = (bf16[128,1024]{1,0:T(8,128)(2,1)S(1)}, bf16[128,1024]{1,0:T(8,128)(2,1)S(1)}, u32[]{:S(2)}, u32[]{:S(2)}) collective-permute-start(bf16[128,1024]{1,0:T(8,128)(2,1)S(1)} %get-tuple-element.40), channel_id=1, source_target_pairs={{0,1},{1,2},{2,3},{3,0},{4,5},{5,6},{6,7},{7,4},{8,9},{9,10},{10,1... | collective-permute-start | bytes 786440 | tf_op jit(solution)/shard_map/ppermute | solution.py:191

commit v2 on v1

v2 whole, which is shorter than its diff:
```python
import functools

import jax
import jax.numpy as jnp
from jax import lax
from jax.experimental import pallas as pl
from jax.experimental.pallas import tpu as pltpu
from jax.sharding import PartitionSpec as P

MOST = 40
PAIR = 2 * MOST
F32 = jnp.float32
BF16 = jnp.bfloat16


def dot(a, b, dims):
    return lax.dot_general(a, b, (dims, ((), ())), preferred_element_type=F32)


def expanded(local):
    slot = lax.broadcasted_iota(jnp.int32, (local, local * PAIR), 1)
    first = lax.broadcasted_iota(jnp.int32, (local, local * PAIR), 0) * PAIR
    return jnp.where((slot >= first) & (slot < first + PAIR), 1.0, 0.0).astype(BF16)


def forward_kernel(sources, local, tokens, step, base_ref, *refs):
    x_refs, refs = refs[:sources], refs[sources:]
    if step:
        meta_refs, refs = refs[:sources], refs[sources:]
    else:
        meta_refs = x_refs
    gate_ref, up_ref, a_ref, b_ref, pick_ref, place_ref, done_ref, rows_ref, weight_ref = refs
    top = x_refs[0].shape[1] // tokens

    mine = lax.broadcasted_iota(jnp.int32, (local, tokens), 0).astype(F32) + base_ref[0].astype(F32)
    before = (
        lax.broadcasted_iota(jnp.int32, (tokens, tokens), 0)
        < lax.broadcasted_iota(jnp.int32, (tokens, tokens), 1)
    )
    before = jnp.where(before, 1.0, 0.0).astype(BF16)
    table = expanded(local)
    for pair in range(sources // 2):
        targets, weights = [], []
        for half in range(2):
            meta = meta_refs[2 * pair + half][tokens:, :].astype(F32)[4 * step : 4 * step + 4]
            weights_of = meta[1:2] + meta[2:3] + meta[3:4]
            named = jnp.zeros((local, tokens), F32)
            weight = jnp.zeros((local, tokens), F32)
            for k in range(top):
                lanes = slice(k * tokens, (k + 1) * tokens)
                same = meta[0:1, lanes] == mine
                named = jnp.where(same, 1.0, named)
                weight = jnp.where(same, weights_of[:, lanes], weight)
            position = dot(named.astype(BF16), before, ((1,), (0,)))
            targets.append(jnp.where(named > 0.5, position + half * MOST, -1.0))
            weights.append(weight)
        target = jnp.concatenate(targets, axis=1).astype(BF16)
        weight = jnp.concatenate(weights, axis=1)
        spread = dot(table, target, ((0,), (0,)))
        slot = lax.broadcasted_iota(jnp.int32, spread.shape, 0) % PAIR
        picked = spread == slot.astype(F32)
        pick_ref[pair] = jnp.where(picked, 1.0, 0.0).astype(BF16)
        spread_t = dot(target, table, ((0,), (0,)))
        slot_t = lax.broadcasted_iota(jnp.int32, spread_t.shape, 1) % PAIR
        place_ref[pair] = jnp.where(spread_t == slot_t.astype(F32), 1.0, 0.0).astype(BF16)
        for e in range(local):
            block = jnp.where(picked[e * PAIR : (e + 1) * PAIR], weight[e : e + 1], 0.0)
            weight_ref[e, pair * PAIR : (pair + 1) * PAIR, :] = jnp.sum(block, axis=1, keepdims=True)
    pick_rows(x_refs, tokens, pick_ref, rows_ref)
    for e in range(local):
        rows = rows_ref[e]
        gate = dot(rows, gate_ref[e], ((1,), (1,)))
        up = dot(rows, up_ref[e], ((1,), (1,)))
        sig = 1.0 / (1.0 + jnp.exp(-gate))
        scaled = sig * weight_ref[e]
        a_ref[e] = up * scaled * (1.0 + gate * (1.0 - sig))
        b_ref[e] = gate * scaled
    done_ref[...] = jnp.zeros_like(done_ref)


def pick_rows(source_refs, tokens, pick_ref, rows_ref):
    local, width = rows_ref.shape[0], rows_ref.shape[2]
    for pair in range(len(source_refs) // 2):
        source = jnp.concatenate([ref[:tokens] for ref in source_refs[2 * pair : 2 * pair + 2]], axis=0)
        for n in range(0, width, 256):
            rows = dot(pick_ref[pair], source[:, n : n + 256], ((1,), (0,))).astype(BF16)
            rows_ref[:, pair * PAIR : (pair + 1) * PAIR, n : n + 256] = rows.reshape(local, PAIR, 256)


def backward_kernel(sources, local, *refs):
    g_refs, refs = refs[:sources], refs[sources:]
    a_ref, b_ref, pick_ref, place_ref, gate_ref, up_ref, down_ref = refs[:7]
    out_refs, refs = refs[7 : 7 + sources], refs[7 + sources :]
    rows_ref, back_ref = refs
    tokens, width = g_refs[0].shape

    pick_rows(g_refs, tokens, pick_ref, rows_ref)
    for e in range(local):
        hidden = dot(rows_ref[e], down_ref[e], ((1,), (0,)))
        gate_grad = (hidden * a_ref[e]).astype(BF16)
        up_grad = (hidden * b_ref[e]).astype(BF16)
        row = dot(gate_grad, gate_ref[e], ((1,), (0,))) + dot(up_grad, up_ref[e], ((1,), (0,)))
        row = row.astype(BF16)
        for pair in range(sources // 2):
            back_ref[pair, e] = row[pair * PAIR : (pair + 1) * PAIR]
    for pair in range(sources // 2):
        for n in range(0, width, 256):
            rows = back_ref[pair, :, :, n : n + 256].reshape(local * PAIR, 256)
            total = dot(place_ref[pair], rows, ((1,), (0,)))
            for half in range(2):
                out = out_refs[2 * pair + half]
                out[:, n : n + 256] = total[half * tokens : (half + 1) * tokens].astype(out.dtype)


def turn_kernel(*refs):
    e = pl.program_id(0)
    refs = refs[2:]
    count = len(refs) // 2
    for from_ref, to_ref in zip(refs[:count], refs[count:-1]):
        to_ref[e] = from_ref[0].T
    refs[-1][...] = jnp.zeros_like(refs[-1])


def first_kernel(saved_ref, grad_ref, routes_from, weights_from, out_ref, grad_out_ref, routes_ref, weights_ref, sems):
    tokens = saved_ref.shape[1]
    copies = [
        pltpu.make_async_copy(routes_from, routes_ref, sems.at[0]),
        pltpu.make_async_copy(weights_from, weights_ref, sems.at[1]),
        pltpu.make_async_copy(saved_ref.at[0], out_ref.at[:tokens], sems.at[2]),
        pltpu.make_async_copy(grad_ref, grad_out_ref, sems.at[3]),
    ]
    for copy in copies:
        copy.start()
    copies[0].wait()
    copies[1].wait()
    rows = []
    for step in range(routes_ref.shape[0]):
        weight = weights_ref[step]
        high = weight.astype(BF16).astype(F32)
        middle = (weight - high).astype(BF16).astype(F32)
        for part in (routes_ref[step].astype(F32), high, middle, weight - high - middle):
            rows.append(jnp.concatenate([part[k : k + 1] for k in range(part.shape[0])], axis=1))
    out_ref[tokens:] = jnp.concatenate(rows, axis=0).astype(BF16)
    copies[2].wait()
    copies[3].wait()


VMEM = pl.BlockSpec(memory_space=pltpu.VMEM)
MIB = 1024 * 1024
SMALL = pl.CostEstimate(flops=0, bytes_accessed=1024, transcendentals=0)
DONE = pltpu.VMEM((8, 128), F32)


def near(*values):
    return [pltpu.with_memory_space_constraint(v, pltpu.VMEM) for v in values]


def one(shape):
    return pl.BlockSpec((1,) + shape[1:], lambda e: (e,) + (0,) * (len(shape) - 1))


def turned(who, *weights):
    local = weights[0].shape[0]
    shapes = [(local, w.shape[2], w.shape[1]) for w in weights]
    return pl.pallas_call(
        turn_kernel,
        grid=(local,),
        in_specs=[pl.BlockSpec(memory_space=pltpu.SMEM)] * 2 + [one(w.shape) for w in weights],
        out_specs=(VMEM,) * (len(weights) + 1),
        out_shape=(*[pltpu.VMEM(shape, BF16) for shape in shapes], DONE),
        compiler_params=pltpu.CompilerParams(vmem_limit_bytes=10 * MIB),
        cost_estimate=SMALL,
        name="turn",
    )(*who, *[pltpu.with_memory_space_constraint(w, pltpu.HBM) for w in weights])


def first_blocks(saved, grad, routes, weights):
    steps, tokens, width = saved.shape
    return pl.pallas_call(
        first_kernel,
        in_specs=[pl.BlockSpec(memory_space=pl.ANY)] * 4,
        out_specs=(VMEM,) * 2,
        out_shape=(pltpu.VMEM((tokens + 4 * steps, width), BF16), pltpu.VMEM(grad.shape, BF16)),
        scratch_shapes=[
            pltpu.VMEM(routes.shape, routes.dtype),
            pltpu.VMEM(weights.shape, weights.dtype),
            pltpu.SemaphoreType.DMA((4,)),
        ],
        compiler_params=pltpu.CompilerParams(vmem_limit_bytes=4 * MIB),
        cost_estimate=SMALL,
        name="first",
    )(*[pltpu.with_memory_space_constraint(v, pltpu.HBM) for v in (saved, grad, routes, weights)])


def choose_kernel(odd_ref, done_ref, left_ref, right_ref, out_ref):
    @pl.when(odd_ref[0] == 1)
    def _():
        out_ref[...] = right_ref[...]

    @pl.when(odd_ref[0] == 0)
    def _():
        out_ref[...] = left_ref[...]


def chosen(who, done, left, right):
    done = left if done is who[1] else done
    return pl.pallas_call(
        choose_kernel,
        in_specs=[pl.BlockSpec(memory_space=pltpu.SMEM)] + [VMEM] * 3,
        out_specs=VMEM,
        out_shape=pltpu.VMEM(left.shape, left.dtype),
        compiler_params=pltpu.CompilerParams(vmem_limit_bytes=4 * MIB),
        cost_estimate=SMALL,
        name="choose",
    )(who[1], *near(done, left, right))


def join_kernel(odd_ref, far_ref, left_ref, right_ref, *refs):
    to_left_ref, to_right_ref = refs[-2:]
    far = far_ref[...].astype(F32)

    @pl.when(odd_ref[0] == 1)
    def _():
        to_left_ref[...] = left_ref[...]
        to_right_ref[...] = (right_ref[...].astype(F32) + far).astype(BF16)

    @pl.when(odd_ref[0] == 0)
    def _():
        to_left_ref[...] = (left_ref[...].astype(F32) + far).astype(BF16)
        to_right_ref[...] = right_ref[...]


def joined(who, far, left, right, beside):
    return pl.pallas_call(
        join_kernel,
        in_specs=[pl.BlockSpec(memory_space=pltpu.SMEM)] + [VMEM] * (3 + len(beside)),
        out_specs=(VMEM,) * 2,
        out_shape=(pltpu.VMEM(left.shape, left.dtype),) * 2,
        compiler_params=pltpu.CompilerParams(vmem_limit_bytes=4 * MIB),
        cost_estimate=SMALL,
        name="join",
    )(who[1], *near(far, left, right, *beside))


def later_kernel(index, saved_ref, done_ref, out_ref, sem):
    copy = pltpu.make_async_copy(saved_ref.at[index], out_ref, sem)
    copy.start()
    copy.wait()


def later_block(saved, index, done):
    return pl.pallas_call(
        functools.partial(later_kernel, index),
        in_specs=[pl.BlockSpec(memory_space=pl.ANY), VMEM],
        out_specs=VMEM,
        out_shape=pltpu.VMEM(saved.shape[1:], saved.dtype),
        scratch_shapes=[pltpu.SemaphoreType.DMA],
        compiler_params=pltpu.CompilerParams(vmem_limit_bytes=4 * MIB),
        cost_estimate=SMALL,
        name="later",
    )(pltpu.with_memory_space_constraint(saved, pltpu.HBM), *near(done))


def forward(step, who, tokens, xs, metas, gate, up):
    sources, local = len(xs), gate.shape[0]
    width = xs[0].shape[1]
    hidden = gate.shape[1]
    rows = sources * MOST
    arrays = (*xs, *metas, gate, up) if step else (*xs, gate, up)
    return pl.pallas_call(
        functools.partial(forward_kernel, sources, local, tokens, step),
        in_specs=[pl.BlockSpec(memory_space=pltpu.SMEM)] + [VMEM] * len(arrays),
        out_specs=(VMEM,) * 5,
        out_shape=(
            pltpu.VMEM((local, rows, hidden), F32),
            pltpu.VMEM((local, rows, hidden), F32),
            pltpu.VMEM((sources // 2, local * PAIR, 2 * tokens), BF16),
            pltpu.VMEM((sources // 2, 2 * tokens, local * PAIR), BF16),
            DONE,
        ),
        scratch_shapes=[
            pltpu.VMEM((local, rows, width), BF16),
            pltpu.VMEM((local, rows, 1), F32),
        ],
        compiler_params=pltpu.CompilerParams(vmem_limit_bytes=11 * MIB),
        cost_estimate=SMALL,
        name="forward",
    )(who[0], *near(*arrays))


def backward(gs, a, b, pick, place, gate, up, down):
    sources, local = len(gs), gate.shape[0]
    tokens, width = gs[0].shape
    hidden = gate.shape[1]
    rows = sources * MOST
    outs = tuple(pltpu.VMEM((tokens, width), F32 if k == 0 else BF16) for k in range(sources))
    return pl.pallas_call(
        functools.partial(backward_kernel, sources, local),
        in_specs=[VMEM] * (sources + 7),
        out_specs=(VMEM,) * sources,
        out_shape=outs,
        scratch_shapes=[
            pltpu.VMEM((local, rows, width), BF16),
            pltpu.VMEM((sources // 2, local, PAIR, width), BF16),
        ],
        compiler_params=pltpu.CompilerParams(vmem_limit_bytes=13 * MIB),
        cost_estimate=SMALL,
        name="backward",
    )(*near(*gs, a, b, pick, place, gate, up, down))


def moved(value, by):
    count = lax.axis_size("expert")
    return lax.ppermute(value, "expert", [(i, (i + by) % count) for i in range(count)])


def swapped(value):
    return lax.ppermute(value, "expert", [(i, i ^ 1) for i in range(lax.axis_size("expert"))])


def moved_back(value, by):
    sections, count = lax.axis_size("section"), lax.axis_size("expert")
    pairs = [
        (s * count + i, ((s - 1) % sections) * count + (i + by) % count)
        for s in range(sections)
        for i in range(count)
    ]
    return lax.ppermute(value, ("section", "expert"), pairs)


def gathered_near(value):
    count = lax.axis_size("expert")
    if count != 4:
        return [value] + [moved(value, k) for k in range(1, count)]
    return [value, moved(value, 1), None, moved(value, -1)]


def gathered_far(who, blocks, done):
    if blocks[2] is not None:
        return blocks
    value, left, _, right = blocks
    return [value, left, swapped(chosen(who, done, left, right)), right]


def scattered(who, parts, kept, move, beside, done):
    count = lax.axis_size("expert")
    if count != 4:
        sent = [(parts[k], -k) for k in range(1, count)]
    else:
        own, left, far, right = parts
        far = swapped(far)
        to_left, to_right = joined(who, far, left, right, beside[1::2] if beside else ())
        if beside is not None:
            beside = gathered_far(who, beside, done)
        sent = [(to_left, -1), (to_right, 1)]
    total = kept + parts[0]
    if move is moved_back:
        total = moved_back(total.astype(BF16), 0).astype(F32)
    for part, by in sent:
        total = total + move(part, by).astype(F32)
    return total.astype(BF16), beside


def shards(grad_out, saved_inputs, routes, gate_weights, w_gate, w_up, w_down):
    gate, up, down = w_gate[0], w_up[0], w_down[0]
    local = gate.shape[0]
    tokens = grad_out.shape[1]
    steps = routes.shape[1]
    place = lax.axis_index("expert").astype(jnp.int32)
    who = ((place * local).reshape(1), (place % 2).reshape(1))
    first, grad = first_blocks(
        saved_inputs[0], grad_out[0], routes[0].transpose(0, 2, 1), gate_weights[0].transpose(0, 2, 1)
    )
    xs = gathered_near(first)
    gs = gathered_near(grad)
    *back, done = turned(who, gate, up, down)
    xs = gathered_far(who, xs, who[1])
    metas = xs
    for step in range(steps):
        last = step + 1 == steps
        if step == 0:
            gs = gathered_far(who, gs, done)
        *factors, done = forward(step, who, tokens, xs, metas, back[0], back[1])
        if step:
            gs = gathered_far(who, gs, done)
        beside = None
        if not last:
            beside = gathered_near(later_block(saved_inputs[0], step + 1, done))
        parts = backward(gs, *factors, *back)
        grad, xs = scattered(
            who, parts, grad.astype(F32), moved if last else moved_back, beside, done
        )
        if not last:
            gs = gathered_near(grad)
    return grad[None]


def solution(mesh):
    placed = (
        P("section", "expert", None),
        P("section", None, "expert", None),
        P("section", None, "expert", None),
        P("section", None, "expert", None),
        P("section", "expert", None, None),
        P("section", "expert", None, None),
        P("section", "expert", None, None),
    )
    return jax.shard_map(
        shards, mesh=mesh, in_specs=placed, out_specs=P("section", "expert", None), check_vma=False
    )
```

time: 164 us -> 131 us (0.80)
  Pallas kernels: 50.7 us -> 40.9 us
  starting transfers between devices: 39.7 us -> 29.9 us
  waiting for transfers between devices: 65.7 us -> 58.4 us
  local copies, waits for them, and re-layouts: 4.46 us -> 0 us
  other arithmetic: 2.87 us -> 1.02 us
    ppermute x12 -> x10, starting transfers between devices: 26.8 us -> 16.3 us  [moved(): lax.ppermute(value, 'expert', [(i, (i + by) % count) for i in range(count)])]
    pallas_call x4 -> x13, Pallas kernels: 50.7 us -> 40.9 us  [the longest x2 13.4 us: backward(): pl.pallas_call(functools.partial(backward_kernel, sources, local), in_spe...]
    ppermute x12 -> x10, waiting for transfers between devices: 33.3 us -> 27.7 us  [moved(): lax.ppermute(value, 'expert', [(i, (i + by) % count) for i in range(count)])]
    ppermute x7 -> x6, waiting for transfers between devices: 25.4 us -> 21.4 us  [swapped(): lax.ppermute(value, 'expert', [(i, i ^ 1) for i in range(lax.axis_size('e...]
    unnamed x8 -> x0, local copies, waits for them, and re-layouts: 3.4 us -> none
    ppermute x3, waiting for transfers between devices: 6.94 us -> 9.27 us  [moved_back(): return lax.ppermute(value, ('section', 'expert'), pairs)]
    ppermute x7 -> x6, starting transfers between devices: 9.23 us -> 9.78 us  [swapped(): lax.ppermute(value, 'expert', [(i, i ^ 1) for i in range(lax.axis_size('e...]
  transfers between devices with their start and end apart: 22 -> 19, of which waited for: 14 -> 12; matrix products, arithmetic and copies ran while one was open for 1% -> 0% of each run, Pallas kernels for 11% -> 25%
where the time goes in v2:
time: 131 us; the launch traced here: 130 us
  waiting for transfers between devices  58.4 us (45%)
  Pallas kernels  40.9 us (31%)
  starting transfers between devices  29.9 us (23%)
    ppermute x10, waiting for transfers between devices, moved(): lax.ppermute(value, 'expert', [(i, (i + by) % count) for i in range(count)])  27.7 us
    ppermute x6, waiting for transfers between devices, swapped(): lax.ppermute(value, 'expert', [(i, i ^ 1) for i in range(lax.axis_size('e...  21.4 us
    ppermute x10, starting transfers between devices, moved(): lax.ppermute(value, 'expert', [(i, (i + by) % count) for i in range(count)])  16.3 us
    pallas_call x2, Pallas kernels, backward(): pl.pallas_call(functools.partial(backward_kernel, sources, local), in_spe...  13.4 us
    pallas_call x1, Pallas kernels, turned(): pl.pallas_call(turn_kernel, grid=(local,), in_specs=[pl.BlockSpec(memory_...  12.6 us
    pallas_call x2, Pallas kernels, forward(): pl.pallas_call(functools.partial(forward_kernel, sources, local, tokens,...  12.4 us
    ppermute x6, starting transfers between devices, swapped(): lax.ppermute(value, 'expert', [(i, i ^ 1) for i in range(lax.axis_size('e...  9.78 us
    ppermute x3, waiting for transfers between devices, moved_back(): return lax.ppermute(value, ('section', 'expert'), pairs)  9.27 us
  transfers between devices with their start and end apart: 19, of which 12 were waited for; matrix products, arithmetic and copies ran while one was open for 0% of the time, Pallas kernels for 25%

profile of v2, /device:TPU:0, one launch (start us, length us, event | category | flops | bytes accessed | tf_op | source)
XLA Modules:
  0.0 130.3 jit_solution(16729761921992923215)
XLA Ops:
  0.0 1.1 first.1
  1.1 5.1 %collective-permute-start.4 = (bf16[136,1024]{1,0:T(8,128)(2,1)S(1)}, bf16[136,1024]{1,0:T(8,128)(2,1)S(1)}, u32[]{:S(2)}, u32[]{:S(2)}) collective-permute-start(bf16[136,1024]{1,0:T(8,128)(2,1)S(1)} %get-tuple-element.35.refs_0_.refs_4_), channel_id=1, source_target_pairs={{0,3},{1,0},{2,1},{3,2},{4,7},{5,4},{6,5},{7,6},{8,11},{9,8},{10,9... | collective-permute-start | bytes 835592 | tf_op jit(solution)/shard_map/ppermute | solution.py:314
  6.2 3.8 %collective-permute-start.1 = (bf16[128,1024]{1,0:T(8,128)(2,1)S(1)}, bf16[128,1024]{1,0:T(8,128)(2,1)S(1)}, u32[]{:S(2)}, u32[]{:S(2)}) collective-permute-start(bf16[128,1024]{1,0:T(8,128)(2,1)S(1)} %get-tuple-element.33.refs_0_), channel_id=1, source_target_pairs={{0,3},{1,0},{2,1},{3,2},{4,7},{5,4},{6,5},{7,6},{8,11},{9,8},{10,9... | collective-permute-start | bytes 786440 | tf_op jit(solution)/shard_map/ppermute | solution.py:314
  10.0 0.0 collective-permute-start
  10.0 3.2 %collective-permute-done.4.right_ref.refs_3_.refs_7_ = bf16[136,1024]{1,0:T(8,128)(2,1)S(1)} collective-permute-done((bf16[136,1024]{1,0:T(8,128)(2,1)S(1)}, bf16[136,1024]{1,0:T(8,128)(2,1)S(1)}, u32[]{:S(2)}, u32[]{:S(2)}) %collective-permute-start.4) | collective-permute-done | bytes 278560 | tf_op jit(solution)/shard_map/ppermute | solution.py:314
  13.3 6.9 %collective-permute-done.3.done_ref.left_ref.refs_1_.refs_5_ = bf16[136,1024]{1,0:T(8,128)(2,1)S(1)} collective-permute-done((bf16[136,1024]{1,0:T(8,128)(2,1)S(1)}, bf16[136,1024]{1,0:T(8,128)(2,1)S(1)}, u32[]{:S(2)}, u32[]{:S(2)}) %collective-permute-start.3) | collective-permute-done | bytes 278560 | tf_op jit(solution)/shard_map/ppermute | solution.py:314
  20.2 1.6 %collective-permute-start.5 = (bf16[136,1024]{1,0:T(8,128)(2,1)S(1)}, bf16[136,1024]{1,0:T(8,128)(2,1)S(1)}, u32[]{:S(2)}, u32[]{:S(2)}) collective-permute-start(bf16[136,1024]{1,0:T(8,128)(2,1)S(1)} %choose.5), channel_id=1, source_target_pairs={{0,1},{1,0},{2,3},{3,2},{4,5},{5,4},{6,7},{7,6},{8,9},{9,8},{10,11... | collective-permute-start | bytes 835592 | tf_op jit(solution)/shard_map/ppermute | solution.py:318
  21.8 12.6 %turn.1 = (bf16[8,512,1024]{2,1,0:T(8,128)(2,1)S(1)}, bf16[8,512,1024]{2,1,0:T(8,128)(2,1)S(1)}, bf16[8,1024,512]{2,1,0:T(8,128)(2,1)S(1)}, f32[8,128]{1,0:T(8,128)S(1)}) custom-call(s32[1]{0:T(128)} %bitcast.7.refs_0_.base_ref, s32[1]{0:T(128)} %bitcast.6.refs_1_.odd_ref, bf16[8,1024,512]{2,1,0:T(8,128)(2,1)} %bitcast.15, bf16[8,1024,512]{2,1,0:T(8,128)(2,1)} %bitcast.16, ...), custom_call_target="tpu_custom_call" | custom-call | bytes 1024 | tf_op jit(solution)/shard_map/turn/pallas_call | solution.py:165
  34.4 0.0 collective-permute-done.1.right_ref.refs_3_
  34.5 0.6 collective-permute-start.2
  35.1 1.4 %collective-permute-done.5.refs_2_.refs_6_ = bf16[136,1024]{1,0:T(8,128)(2,1)S(1)} collective-permute-done((bf16[136,1024]{1,0:T(8,128)(2,1)S(1)}, bf16[136,1024]{1,0:T(8,128)(2,1)S(1)}, u32[]{:S(2)}, u32[]{:S(2)}) %collective-permute-start.5) | collective-permute-done | bytes 278560 | tf_op jit(solution)/shard_map/ppermute | solution.py:318
  36.5 6.2 %forward.2 = (f32[8,160,512]{2,1,0:T(8,128)S(1)}, f32[8,160,512]{2,1,0:T(8,128)S(1)}, bf16[2,640,256]{2,1,0:T(8,128)(2,1)S(1)}, bf16[2,256,640]{2,1,0:T(8,128)(2,1)S(1)}, f32[8,128]{1,0:T(8,128)S(1)}) custom-call(s32[1]{0:T(128)} %bitcast.7.refs_0_.base_ref, bf16[136,1024]{1,0:T(8,128)(2,1)S(1)} %get-tuple-element.35.refs_0_.refs_4_, ...), custom_call_target="tpu_custom_call" | custom-call | bytes 1024 | tf_op jit(solution)/shard_map/forward/pallas_call | solution.py:270
  42.7 1.0 later.1.refs_0_
  43.6 3.0 %collective-permute-start.9 = (bf16[128,1024]{1,0:T(8,128)(2,1)S(1)}, bf16[128,1024]{1,0:T(8,128)(2,1)S(1)}, u32[]{:S(2)}, u32[]{:S(2)}) collective-permute-start(bf16[128,1024]{1,0:T(8,128)(2,1)S(1)} %later.1.refs_0_), channel_id=1, source_target_pairs={{0,3},{1,0},{2,1},{3,2},{4,7},{5,4},{6,5},{7,6},{8,11},{9,8},{10,9... | collective-permute-start | bytes 786440 | tf_op jit(solution)/shard_map/ppermute | solution.py:314
  46.6 0.0 collective-permute-start.8
  46.6 0.0 collective-permute-done.2.refs_2_
  46.6 6.7 %backward.2 = (f32[128,1024]{1,0:T(8,128)S(1)}, bf16[128,1024]{1,0:T(8,128)(2,1)S(1)}, bf16[128,1024]{1,0:T(8,128)(2,1)S(1)}, bf16[128,1024]{1,0:T(8,128)(2,1)S(1)}) custom-call(bf16[128,1024]{1,0:T(8,128)(2,1)S(1)} %get-tuple-element.33.refs_0_, bf16[128,1024]{1,0:T(8,128)(2,1)S(1)} %collective-permute-done.left_ref.refs_1_, ...), custom_call_target="tpu_custom_call" | custom-call | bytes 1024 | tf_op jit(solution)/shard_map/backward/pallas_call | solution.py:297
  53.3 1.6 %collective-permute-start.7 = (bf16[128,1024]{1,0:T(8,128)(2,1)S(1)}, bf16[128,1024]{1,0:T(8,128)(2,1)S(1)}, u32[]{:S(2)}, u32[]{:S(2)}) collective-permute-start(bf16[128,1024]{1,0:T(8,128)(2,1)S(1)} %get-tuple-element.44), channel_id=1, source_target_pairs={{0,1},{1,0},{2,3},{3,2},{4,5},{5,4},{6,7},{7,6},{8,9},{9,8},{10,11... | collective-permute-start | bytes 786440 | tf_op jit(solution)/shard_map/ppermute | solution.py:318
  55.0 0.1 add_convert_fusion.2
  55.0 0.1 collective-permute-start.6
  55.1 0.0 collective-permute-done.9.refs_1_.right_ref.refs_3_
  55.1 2.8 %collective-permute-done.8.refs_0_.left_ref.refs_1_ = bf16[128,1024]{1,0:T(8,128)(2,1)S(1)} collective-permute-done((bf16[128,1024]{1,0:T(8,128)(2,1)S(1)}, bf16[128,1024]{1,0:T(8,128)(2,1)S(1)}, u32[]{:S(2)}, u32[]{:S(2)}) %collective-permute-start.8) | collective-permute-done | bytes 262176 | tf_op jit(solution)/shard_map/ppermute | solution.py:314
  57.9 3.9 %collective-permute-done.7.far_ref = bf16[128,1024]{1,0:T(8,128)(2,1)S(1)} collective-permute-done((bf16[128,1024]{1,0:T(8,128)(2,1)S(1)}, bf16[128,1024]{1,0:T(8,128)(2,1)S(1)}, u32[]{:S(2)}, u32[]{:S(2)}) %collective-permute-start.7) | collective-permute-done | bytes 262176 | tf_op jit(solution)/shard_map/ppermute | solution.py:318
  61.8 0.1 join.2
  61.9 2.2 %collective-permute-start.10 = (bf16[128,1024]{1,0:T(8,128)(2,1)S(1)}, bf16[128,1024]{1,0:T(8,128)(2,1)S(1)}, u32[]{:S(2)}, u32[]{:S(2)}) collective-permute-start(bf16[128,1024]{1,0:T(8,128)(2,1)S(1)} %get-tuple-element.48), channel_id=1, source_target_pairs={{0,31},{1,28},{2,29},{3,30},{4,3},{5,0},{6,1},{7,2},{8,7},{9,4},{1... | collective-permute-start | bytes 786440 | tf_op jit(solution)/shard_map/ppermute | solution.py:328
  64.1 1.5 %collective-permute-start.11 = (bf16[128,1024]{1,0:T(8,128)(2,1)S(1)}, bf16[128,1024]{1,0:T(8,128)(2,1)S(1)}, u32[]{:S(2)}, u32[]{:S(2)}) collective-permute-start(bf16[128,1024]{1,0:T(8,128)(2,1)S(1)} %get-tuple-element.49), channel_id=1, source_target_pairs={{0,29},{1,30},{2,31},{3,28},{4,1},{5,2},{6,3},{7,0},{8,5},{9,6},{1... | collective-permute-start | bytes 786440 | tf_op jit(solution)/shard_map/ppermute | solution.py:328
  65.6 1.6 %collective-permute-start.13 = (bf16[128,1024]{1,0:T(8,128)(2,1)S(1)}, bf16[128,1024]{1,0:T(8,128)(2,1)S(1)}, u32[]{:S(2)}, u32[]{:S(2)}) collective-permute-start(bf16[128,1024]{1,0:T(8,128)(2,1)S(1)} %choose.6), channel_id=1, source_target_pairs={{0,1},{1,0},{2,3},{3,2},{4,5},{5,4},{6,7},{7,6},{8,9},{9,8},{10,11... | collective-permute-start | bytes 786440 | tf_op jit(solution)/shard_map/ppermute | solution.py:318
  67.2 0.0 collective-permute-done.6
  67.2 3.7 %collective-permute-done.10 = bf16[128,1024]{1,0:T(8,128)(2,1)S(1)} collective-permute-done((bf16[128,1024]{1,0:T(8,128)(2,1)S(1)}, bf16[128,1024]{1,0:T(8,128)(2,1)S(1)}, u32[]{:S(2)}, u32[]{:S(2)}) %collective-permute-start.10) | collective-permute-done | bytes 262176 | tf_op jit(solution)/shard_map/ppermute | solution.py:328
  70.9 5.6 %collective-permute-done.11 = bf16[128,1024]{1,0:T(8,128)(2,1)S(1)} collective-permute-done((bf16[128,1024]{1,0:T(8,128)(2,1)S(1)}, bf16[128,1024]{1,0:T(8,128)(2,1)S(1)}, u32[]{:S(2)}, u32[]{:S(2)}) %collective-permute-start.11) | collective-permute-done | bytes 262176 | tf_op jit(solution)/shard_map/ppermute | solution.py:328
  76.5 0.1 add_convert_fusion.1.refs_0_
  76.6 0.7 collective-permute-start.14
  77.4 1.6 %collective-permute-start.12 = (bf16[128,1024]{1,0:T(8,128)(2,1)S(1)}, bf16[128,1024]{1,0:T(8,128)(2,1)S(1)}, u32[]{:S(2)}, u32[]{:S(2)}) collective-permute-start(bf16[128,1024]{1,0:T(8,128)(2,1)S(1)} %add_convert_fusion.1.refs_0_), channel_id=1, source_target_pairs={{0,1},{1,2},{2,3},{3,0},{4,5},{5,6},{6,7},{7,4},{8,9},{9,10},{10,1... | collective-permute-start | bytes 786440 | tf_op jit(solution)/shard_map/ppermute | solution.py:314
  79.0 3.7 %collective-permute-done.13.refs_2_ = bf16[128,1024]{1,0:T(8,128)(2,1)S(1)} collective-permute-done((bf16[128,1024]{1,0:T(8,128)(2,1)S(1)}, bf16[128,1024]{1,0:T(8,128)(2,1)S(1)}, u32[]{:S(2)}, u32[]{:S(2)}) %collective-permute-start.13) | collective-permute-done | bytes 262176 | tf_op jit(solution)/shard_map/ppermute | solution.py:318
  82.7 6.2 %forward.3 = (f32[8,160,512]{2,1,0:T(8,128)S(1)}, f32[8,160,512]{2,1,0:T(8,128)S(1)}, bf16[2,640,256]{2,1,0:T(8,128)(2,1)S(1)}, bf16[2,256,640]{2,1,0:T(8,128)(2,1)S(1)}, f32[8,128]{1,0:T(8,128)S(1)}) custom-call(s32[1]{0:T(128)} %bitcast.7.refs_0_.base_ref, bf16[128,1024]{1,0:T(8,128)(2,1)S(1)} %later.1.refs_0_, ...), custom_call_target="tpu_custom_call" | custom-call | bytes 1024 | tf_op jit(solution)/shard_map/forward/pallas_call | solution.py:270
  88.9 0.0 collective-permute-done.14.right_ref.refs_3_
  88.9 4.4 %collective-permute-done.12.left_ref.refs_1_ = bf16[128,1024]{1,0:T(8,128)(2,1)S(1)} collective-permute-done((bf16[128,1024]{1,0:T(8,128)(2,1)S(1)}, bf16[128,1024]{1,0:T(8,128)(2,1)S(1)}, u32[]{:S(2)}, u32[]{:S(2)}) %collective-permute-start.12) | collective-permute-done | bytes 262176 | tf_op jit(solution)/shard_map/ppermute | solution.py:314
  93.3 0.2 choose.7
  93.5 2.6 %collective-permute-start.15 = (bf16[128,1024]{1,0:T(8,128)(2,1)S(1)}, bf16[128,1024]{1,0:T(8,128)(2,1)S(1)}, u32[]{:S(2)}, u32[]{:S(2)}) collective-permute-start(bf16[128,1024]{1,0:T(8,128)(2,1)S(1)} %choose.7), channel_id=1, source_target_pairs={{0,1},{1,0},{2,3},{3,2},{4,5},{5,4},{6,7},{7,6},{8,9},{9,8},{10,11... | collective-permute-start | bytes 786440 | tf_op jit(solution)/shard_map/ppermute | solution.py:318
  96.1 6.5 %collective-permute-done.15.refs_2_ = bf16[128,1024]{1,0:T(8,128)(2,1)S(1)} collective-permute-done((bf16[128,1024]{1,0:T(8,128)(2,1)S(1)}, bf16[128,1024]{1,0:T(8,128)(2,1)S(1)}, u32[]{:S(2)}, u32[]{:S(2)}) %collective-permute-start.15) | collective-permute-done | bytes 262176 | tf_op jit(solution)/shard_map/ppermute | solution.py:318
  102.5 6.7 %backward.3 = (f32[128,1024]{1,0:T(8,128)S(1)}, bf16[128,1024]{1,0:T(8,128)(2,1)S(1)}, bf16[128,1024]{1,0:T(8,128)(2,1)S(1)}, bf16[128,1024]{1,0:T(8,128)(2,1)S(1)}) custom-call(bf16[128,1024]{1,0:T(8,128)(2,1)S(1)} %add_convert_fusion.1.refs_0_, bf16[128,1024]{1,0:T(8,128)(2,1)S(1)} %collective-permute-done.12.left_ref.refs_1_, ...), custom_call_target="tpu_custom_call" | custom-call | bytes 1024 | tf_op jit(solution)/shard_map/backward/pallas_call | solution.py:297
  109.2 1.8 %collective-permute-start.16 = (bf16[128,1024]{1,0:T(8,128)(2,1)S(1)}, bf16[128,1024]{1,0:T(8,128)(2,1)S(1)}, u32[]{:S(2)}, u32[]{:S(2)}) collective-permute-start(bf16[128,1024]{1,0:T(8,128)(2,1)S(1)} %get-tuple-element.56), channel_id=1, source_target_pairs={{0,1},{1,0},{2,3},{3,2},{4,5},{5,4},{6,7},{7,6},{8,9},{9,8},{10,11... | collective-permute-start | bytes 786440 | tf_op jit(solution)/shard_map/ppermute | solution.py:318
  111.1 5.9 %collective-permute-done.16.far_ref = bf16[128,1024]{1,0:T(8,128)(2,1)S(1)} collective-permute-done((bf16[128,1024]{1,0:T(8,128)(2,1)S(1)}, bf16[128,1024]{1,0:T(8,128)(2,1)S(1)}, u32[]{:S(2)}, u32[]{:S(2)}) %collective-permute-start.16) | collective-permute-done | bytes 262176 | tf_op jit(solution)/shard_map/ppermute | solution.py:318
  117.0 0.1 join.3
  117.1 0.1 collective-permute-start.17
  117.1 2.0 %collective-permute-start.18 = (bf16[128,1024]{1,0:T(8,128)(2,1)S(1)}, bf16[128,1024]{1,0:T(8,128)(2,1)S(1)}, u32[]{:S(2)}, u32[]{:S(2)}) collective-permute-start(bf16[128,1024]{1,0:T(8,128)(2,1)S(1)} %get-tuple-element.60), channel_id=1, source_target_pairs={{0,1},{1,2},{2,3},{3,0},{4,5},{5,6},{6,7},{7,4},{8,9},{9,10},{10,1... | collective-permute-start | bytes 786440 | tf_op jit(solution)/shard_map/ppermute | solution.py:314
  119.1 10.3 %collective-permute-done.17 = bf16[128,1024]{1,0:T(8,128)(2,1)S(1)} collective-permute-done((bf16[128,1024]{1,0:T(8,128)(2,1)S(1)}, bf16[128,1024]{1,0:T(8,128)(2,1)S(1)}, u32[]{:S(2)}, u32[]{:S(2)}) %collective-permute-start.17) | collective-permute-done | bytes 262176 | tf_op jit(solution)/shard_map/ppermute | solution.py:314
  129.5 0.8 fusion
  (6 shorter events, 0.1 us)
Async XLA Ops:
  1.1 12.2 %collective-permute-start.4 = (bf16[136,1024]{1,0:T(8,128)(2,1)S(1)}, bf16[136,1024]{1,0:T(8,128)(2,1)S(1)}, u32[]{:S(2)}, u32[]{:S(2)}) collective-permute-start(bf16[136,1024]{1,0:T(8,128)(2,1)S(1)} %get-tuple-element.35.refs_0_.refs_4_), channel_id=1, source_target_pairs={{0,3},{1,0},{2,1},{3,2},{4,7},{5,4},{6,5},{7,6},{8,11},{9,8},{10,9... | collective-permute-start | bytes 835592 | tf_op jit(solution)/shard_map/ppermute | solution.py:314
  6.2 14.0 %collective-permute-start.3 = (bf16[136,1024]{1,0:T(8,128)(2,1)S(1)}, bf16[136,1024]{1,0:T(8,128)(2,1)S(1)}, u32[]{:S(2)}, u32[]{:S(2)}) collective-permute-start(bf16[136,1024]{1,0:T(8,128)(2,1)S(1)} %get-tuple-element.35.refs_0_.refs_4_), channel_id=1, source_target_pairs={{0,1},{1,2},{2,3},{3,0},{4,5},{5,6},{6,7},{7,4},{8,9},{9,10},{10,1... | collective-permute-start | bytes 835592 | tf_op jit(solution)/shard_map/ppermute | solution.py:314
  6.2 28.2 %collective-permute-start.1 = (bf16[128,1024]{1,0:T(8,128)(2,1)S(1)}, bf16[128,1024]{1,0:T(8,128)(2,1)S(1)}, u32[]{:S(2)}, u32[]{:S(2)}) collective-permute-start(bf16[128,1024]{1,0:T(8,128)(2,1)S(1)} %get-tuple-element.33.refs_0_), channel_id=1, source_target_pairs={{0,3},{1,0},{2,1},{3,2},{4,7},{5,4},{6,5},{7,6},{8,11},{9,8},{10,9... | collective-permute-start | bytes 786440 | tf_op jit(solution)/shard_map/ppermute | solution.py:314
  10.0 24.4 %collective-permute-start = (bf16[128,1024]{1,0:T(8,128)(2,1)S(1)}, bf16[128,1024]{1,0:T(8,128)(2,1)S(1)}, u32[]{:S(2)}, u32[]{:S(2)}) collective-permute-start(bf16[128,1024]{1,0:T(8,128)(2,1)S(1)} %get-tuple-element.33.refs_0_), channel_id=1, source_target_pairs={{0,1},{1,2},{2,3},{3,0},{4,5},{5,6},{6,7},{7,4},{8,9},{9,10},{10,1... | collective-permute-start | bytes 786440 | tf_op jit(solution)/shard_map/ppermute | solution.py:314
  20.2 16.3 %collective-permute-start.5 = (bf16[136,1024]{1,0:T(8,128)(2,1)S(1)}, bf16[136,1024]{1,0:T(8,128)(2,1)S(1)}, u32[]{:S(2)}, u32[]{:S(2)}) collective-permute-start(bf16[136,1024]{1,0:T(8,128)(2,1)S(1)} %choose.5), channel_id=1, source_target_pairs={{0,1},{1,0},{2,3},{3,2},{4,5},{5,4},{6,7},{7,6},{8,9},{9,8},{10,11... | collective-permute-start | bytes 835592 | tf_op jit(solution)/shard_map/ppermute | solution.py:318
  34.5 12.1 %collective-permute-start.2 = (bf16[128,1024]{1,0:T(8,128)(2,1)S(1)}, bf16[128,1024]{1,0:T(8,128)(2,1)S(1)}, u32[]{:S(2)}, u32[]{:S(2)}) collective-permute-start(bf16[128,1024]{1,0:T(8,128)(2,1)S(1)} %choose.4), channel_id=1, source_target_pairs={{0,1},{1,0},{2,3},{3,2},{4,5},{5,4},{6,7},{7,6},{8,9},{9,8},{10,11... | collective-permute-start | bytes 786440 | tf_op jit(solution)/shard_map/ppermute | solution.py:318
  43.6 11.5 %collective-permute-start.9 = (bf16[128,1024]{1,0:T(8,128)(2,1)S(1)}, bf16[128,1024]{1,0:T(8,128)(2,1)S(1)}, u32[]{:S(2)}, u32[]{:S(2)}) collective-permute-start(bf16[128,1024]{1,0:T(8,128)(2,1)S(1)} %later.1.refs_0_), channel_id=1, source_target_pairs={{0,3},{1,0},{2,1},{3,2},{4,7},{5,4},{6,5},{7,6},{8,11},{9,8},{10,9... | collective-permute-start | bytes 786440 | tf_op jit(solution)/shard_map/ppermute | solution.py:314
  46.6 11.3 %collective-permute-start.8 = (bf16[128,1024]{1,0:T(8,128)(2,1)S(1)}, bf16[128,1024]{1,0:T(8,128)(2,1)S(1)}, u32[]{:S(2)}, u32[]{:S(2)}) collective-permute-start(bf16[128,1024]{1,0:T(8,128)(2,1)S(1)} %later.1.refs_0_), channel_id=1, source_target_pairs={{0,1},{1,2},{2,3},{3,0},{4,5},{5,6},{6,7},{7,4},{8,9},{9,10},{10,1... | collective-permute-start | bytes 786440 | tf_op jit(solution)/shard_map/ppermute | solution.py:314
  53.3 8.5 %collective-permute-start.7 = (bf16[128,1024]{1,0:T(8,128)(2,1)S(1)}, bf16[128,1024]{1,0:T(8,128)(2,1)S(1)}, u32[]{:S(2)}, u32[]{:S(2)}) collective-permute-start(bf16[128,1024]{1,0:T(8,128)(2,1)S(1)} %get-tuple-element.44), channel_id=1, source_target_pairs={{0,1},{1,0},{2,3},{3,2},{4,5},{5,4},{6,7},{7,6},{8,9},{9,8},{10,11... | collective-permute-start | bytes 786440 | tf_op jit(solution)/shard_map/ppermute | solution.py:318
  55.0 12.2 %collective-permute-start.6 = (bf16[128,1024]{1,0:T(8,128)(2,1)S(1)}, bf16[128,1024]{1,0:T(8,128)(2,1)S(1)}, u32[]{:S(2)}, u32[]{:S(2)}) collective-permute-start(bf16[128,1024]{1,0:T(8,128)(2,1)S(1)} %add_convert_fusion.2), channel_id=1, source_target_pairs={{0,28},{1,29},{2,30},{3,31},{4,0},{5,1},{6,2},{7,3},{8,4},{9,5},{1... | collective-permute-start | bytes 786440 | tf_op jit(solution)/shard_map/ppermute | solution.py:328
  61.9 9.0 %collective-permute-start.10 = (bf16[128,1024]{1,0:T(8,128)(2,1)S(1)}, bf16[128,1024]{1,0:T(8,128)(2,1)S(1)}, u32[]{:S(2)}, u32[]{:S(2)}) collective-permute-start(bf16[128,1024]{1,0:T(8,128)(2,1)S(1)} %get-tuple-element.48), channel_id=1, source_target_pairs={{0,31},{1,28},{2,29},{3,30},{4,3},{5,0},{6,1},{7,2},{8,7},{9,4},{1... | collective-permute-start | bytes 786440 | tf_op jit(solution)/shard_map/ppermute | solution.py:328
  64.1 12.4 %collective-permute-start.11 = (bf16[128,1024]{1,0:T(8,128)(2,1)S(1)}, bf16[128,1024]{1,0:T(8,128)(2,1)S(1)}, u32[]{:S(2)}, u32[]{:S(2)}) collective-permute-start(bf16[128,1024]{1,0:T(8,128)(2,1)S(1)} %get-tuple-element.49), channel_id=1, source_target_pairs={{0,29},{1,30},{2,31},{3,28},{4,1},{5,2},{6,3},{7,0},{8,5},{9,6},{1... | collective-permute-start | bytes 786440 | tf_op jit(solution)/shard_map/ppermute | solution.py:328
  65.6 17.1 %collective-permute-start.13 = (bf16[128,1024]{1,0:T(8,128)(2,1)S(1)}, bf16[128,1024]{1,0:T(8,128)(2,1)S(1)}, u32[]{:S(2)}, u32[]{:S(2)}) collective-permute-start(bf16[128,1024]{1,0:T(8,128)(2,1)S(1)} %choose.6), channel_id=1, source_target_pairs={{0,1},{1,0},{2,3},{3,2},{4,5},{5,4},{6,7},{7,6},{8,9},{9,8},{10,11... | collective-permute-start | bytes 786440 | tf_op jit(solution)/shard_map/ppermute | solution.py:318
  76.6 12.3 %collective-permute-start.14 = (bf16[128,1024]{1,0:T(8,128)(2,1)S(1)}, bf16[128,1024]{1,0:T(8,128)(2,1)S(1)}, u32[]{:S(2)}, u32[]{:S(2)}) collective-permute-start(bf16[128,1024]{1,0:T(8,128)(2,1)S(1)} %add_convert_fusion.1.refs_0_), channel_id=1, source_target_pairs={{0,3},{1,0},{2,1},{3,2},{4,7},{5,4},{6,5},{7,6},{8,11},{9,8},{10,9... | collective-permute-start | bytes 786440 | tf_op jit(solution)/shard_map/ppermute | solution.py:314
  77.4 15.9 %collective-permute-start.12 = (bf16[128,1024]{1,0:T(8,128)(2,1)S(1)}, bf16[128,1024]{1,0:T(8,128)(2,1)S(1)}, u32[]{:S(2)}, u32[]{:S(2)}) collective-permute-start(bf16[128,1024]{1,0:T(8,128)(2,1)S(1)} %add_convert_fusion.1.refs_0_), channel_id=1, source_target_pairs={{0,1},{1,2},{2,3},{3,0},{4,5},{5,6},{6,7},{7,4},{8,9},{9,10},{10,1... | collective-permute-start | bytes 786440 | tf_op jit(solution)/shard_map/ppermute | solution.py:314
  93.5 9.0 %collective-permute-start.15 = (bf16[128,1024]{1,0:T(8,128)(2,1)S(1)}, bf16[128,1024]{1,0:T(8,128)(2,1)S(1)}, u32[]{:S(2)}, u32[]{:S(2)}) collective-permute-start(bf16[128,1024]{1,0:T(8,128)(2,1)S(1)} %choose.7), channel_id=1, source_target_pairs={{0,1},{1,0},{2,3},{3,2},{4,5},{5,4},{6,7},{7,6},{8,9},{9,8},{10,11... | collective-permute-start | bytes 786440 | tf_op jit(solution)/shard_map/ppermute | solution.py:318
  109.2 7.7 %collective-permute-start.16 = (bf16[128,1024]{1,0:T(8,128)(2,1)S(1)}, bf16[128,1024]{1,0:T(8,128)(2,1)S(1)}, u32[]{:S(2)}, u32[]{:S(2)}) collective-permute-start(bf16[128,1024]{1,0:T(8,128)(2,1)S(1)} %get-tuple-element.56), channel_id=1, source_target_pairs={{0,1},{1,0},{2,3},{3,2},{4,5},{5,4},{6,7},{7,6},{8,9},{9,8},{10,11... | collective-permute-start | bytes 786440 | tf_op jit(solution)/shard_map/ppermute | solution.py:318
  117.1 12.4 %collective-permute-start.17 = (bf16[128,1024]{1,0:T(8,128)(2,1)S(1)}, bf16[128,1024]{1,0:T(8,128)(2,1)S(1)}, u32[]{:S(2)}, u32[]{:S(2)}) collective-permute-start(bf16[128,1024]{1,0:T(8,128)(2,1)S(1)} %get-tuple-element.59), channel_id=1, source_target_pairs={{0,3},{1,0},{2,1},{3,2},{4,7},{5,4},{6,5},{7,6},{8,11},{9,8},{10,9... | collective-permute-start | bytes 786440 | tf_op jit(solution)/shard_map/ppermute | solution.py:314
  117.1 12.4 %collective-permute-start.18 = (bf16[128,1024]{1,0:T(8,128)(2,1)S(1)}, bf16[128,1024]{1,0:T(8,128)(2,1)S(1)}, u32[]{:S(2)}, u32[]{:S(2)}) collective-permute-start(bf16[128,1024]{1,0:T(8,128)(2,1)S(1)} %get-tuple-element.60), channel_id=1, source_target_pairs={{0,1},{1,2},{2,3},{3,0},{4,5},{5,6},{6,7},{7,4},{8,9},{9,10},{10,1... | collective-permute-start | bytes 786440 | tf_op jit(solution)/shard_map/ppermute | solution.py:314

commit v3 on v2

--- a/solution.py
+++ b/solution.py
@@ -87,34 +87,64 @@
             rows_ref[:, pair * PAIR : (pair + 1) * PAIR, n : n + 256] = rows.reshape(local, PAIR, 256)
 
 
-def backward_kernel(sources, local, *refs):
-    g_refs, refs = refs[:sources], refs[sources:]
-    a_ref, b_ref, pick_ref, place_ref, gate_ref, up_ref, down_ref = refs[:7]
-    out_refs, refs = refs[7 : 7 + sources], refs[7 + sources :]
-    rows_ref, back_ref = refs
-    tokens, width = g_refs[0].shape
-
-    pick_rows(g_refs, tokens, pick_ref, rows_ref)
+def pick_pieces(sources, pieces, piece_refs, pick_ref, rows_ref):
+    start = 0
+    for piece in range(pieces):
+        refs = [piece_refs[k * pieces + piece] for k in range(sources)]
+        tokens, width = refs[0].shape
+        pick_rows(refs, tokens, pick_ref, rows_ref.at[:, :, start : start + width])
+        start += width
+
+
+def row_piece(kept_ref, gate_grad_ref, up_grad_ref, place_ref, gate_ref, up_ref, out_refs, back_ref, columns):
+    local = gate_ref.shape[0]
+    pairs, double = place_ref.shape[0], place_ref.shape[1]
+    tokens = double // 2
     for e in range(local):
-        hidden = dot(rows_ref[e], down_ref[e], ((1,), (0,)))
-        gate_grad = (hidden * a_ref[e]).astype(BF16)
-        up_grad = (hidden * b_ref[e]).astype(BF16)
-        row = dot(gate_grad, gate_ref[e], ((1,), (0,))) + dot(up_grad, up_ref[e], ((1,), (0,)))
-        row = row.astype(BF16)
-        for pair in range(sources // 2):
+        row = dot(gate_grad_ref[e], gate_ref[e, :, columns], ((1,), (0,)))
+        row = (row + dot(up_grad_ref[e], up_ref[e, :, columns], ((1,), (0,)))).astype(BF16)
+        for pair in range(pairs):
             back_ref[pair, e] = row[pair * PAIR : (pair + 1) * PAIR]
-    for pair in range(sources // 2):
+    width = columns.stop - columns.start
+    for pair in range(pairs):
         for n in range(0, width, 256):
             rows = back_ref[pair, :, :, n : n + 256].reshape(local * PAIR, 256)
             total = dot(place_ref[pair], rows, ((1,), (0,)))
             for half in range(2):
                 out = out_refs[2 * pair + half]
-                out[:, n : n + 256] = total[half * tokens : (half + 1) * tokens].astype(out.dtype)
+                part = total[half * tokens : (half + 1) * tokens]
+                if pair == 0 and half == 0:
+                    first = columns.start if kept_ref.shape[1] > width else 0
+                    part = part + kept_ref[:, first + n : first + n + 256].astype(F32)
+                out[:, n : n + 256] = part.astype(out.dtype)
+
+
+def backward_kernel(sources, pieces, columns, *refs):
+    g_refs, refs = refs[: sources * pieces], refs[sources * pieces :]
+    a_ref, b_ref, pick_ref, place_ref, gate_ref, up_ref, down_ref = refs[:7]
+    out_refs, refs = refs[7 : 7 + sources], refs[7 + sources :]
+    gate_grad_ref, up_grad_ref, rows_ref, back_ref = refs
+    pick_pieces(sources, pieces, g_refs, pick_ref, rows_ref)
+    for e in range(rows_ref.shape[0]):
+        hidden = dot(rows_ref[e], down_ref[e], ((1,), (0,)))
+        gate_grad_ref[e] = (hidden * a_ref[e]).astype(BF16)
+        up_grad_ref[e] = (hidden * b_ref[e]).astype(BF16)
+    row_piece(g_refs[0], gate_grad_ref, up_grad_ref, place_ref, gate_ref, up_ref, out_refs, back_ref, columns)
+
+
+def rest_kernel(sources, columns, kept_ref, gate_grad_ref, up_grad_ref, place_ref, gate_ref, up_ref, *refs):
+    row_piece(
+        kept_ref, gate_grad_ref, up_grad_ref, place_ref, gate_ref, up_ref, refs[:sources], refs[sources], columns
+    )
+
+
+def hold_kernel(index, value_ref, *refs):
+    refs[-1][...] = value_ref[index]
 
 
 def turn_kernel(*refs):
     e = pl.program_id(0)
-    refs = refs[2:]
+    refs = refs[3:]
     count = len(refs) // 2
     for from_ref, to_ref in zip(refs[:count], refs[count:-1]):
         to_ref[e] = from_ref[0].T
@@ -141,8 +171,8 @@
         for part in (routes_ref[step].astype(F32), high, middle, weight - high - middle):
             rows.append(jnp.concatenate([part[k : k + 1] for k in range(part.shape[0])], axis=1))
     out_ref[tokens:] = jnp.concatenate(rows, axis=0).astype(BF16)
-    copies[2].wait()
-    copies[3].wait()
+    for copy in copies[2:]:
+        copy.wait()
 
 
 VMEM = pl.BlockSpec(memory_space=pltpu.VMEM)
@@ -159,19 +189,19 @@
     return pl.BlockSpec((1,) + shape[1:], lambda e: (e,) + (0,) * (len(shape) - 1))
 
 
-def turned(who, *weights):
+def turned(who, after, *weights):
     local = weights[0].shape[0]
     shapes = [(local, w.shape[2], w.shape[1]) for w in weights]
     return pl.pallas_call(
         turn_kernel,
         grid=(local,),
-        in_specs=[pl.BlockSpec(memory_space=pltpu.SMEM)] * 2 + [one(w.shape) for w in weights],
+        in_specs=[pl.BlockSpec(memory_space=pltpu.SMEM)] * 2 + [VMEM] + [one(w.shape) for w in weights],
         out_specs=(VMEM,) * (len(weights) + 1),
         out_shape=(*[pltpu.VMEM(shape, BF16) for shape in shapes], DONE),
         compiler_params=pltpu.CompilerParams(vmem_limit_bytes=10 * MIB),
         cost_estimate=SMALL,
         name="turn",
-    )(*who, *[pltpu.with_memory_space_constraint(w, pltpu.HBM) for w in weights])
+    )(*who, *near(after), *[pltpu.with_memory_space_constraint(w, pltpu.HBM) for w in weights])
 
 
 def first_blocks(saved, grad, routes, weights):
@@ -186,7 +216,7 @@
             pltpu.VMEM(weights.shape, weights.dtype),
             pltpu.SemaphoreType.DMA((4,)),
         ],
-        compiler_params=pltpu.CompilerParams(vmem_limit_bytes=4 * MIB),
+        compiler_params=pltpu.CompilerParams(vmem_limit_bytes=2 * MIB),
         cost_estimate=SMALL,
         name="first",
     )(*[pltpu.with_memory_space_constraint(v, pltpu.HBM) for v in (saved, grad, routes, weights)])
@@ -209,7 +239,7 @@
         in_specs=[pl.BlockSpec(memory_space=pltpu.SMEM)] + [VMEM] * 3,
         out_specs=VMEM,
         out_shape=pltpu.VMEM(left.shape, left.dtype),
-        compiler_params=pltpu.CompilerParams(vmem_limit_bytes=4 * MIB),
+        compiler_params=pltpu.CompilerParams(vmem_limit_bytes=2 * MIB),
         cost_estimate=SMALL,
         name="choose",
     )(who[1], *near(done, left, right))
@@ -236,29 +266,22 @@
         in_specs=[pl.BlockSpec(memory_space=pltpu.SMEM)] + [VMEM] * (3 + len(beside)),
         out_specs=(VMEM,) * 2,
         out_shape=(pltpu.VMEM(left.shape, left.dtype),) * 2,
-        compiler_params=pltpu.CompilerParams(vmem_limit_bytes=4 * MIB),
+        compiler_params=pltpu.CompilerParams(vmem_limit_bytes=2 * MIB),
         cost_estimate=SMALL,
         name="join",
     )(who[1], *near(far, left, right, *beside))
 
 
-def later_kernel(index, saved_ref, done_ref, out_ref, sem):
-    copy = pltpu.make_async_copy(saved_ref.at[index], out_ref, sem)
-    copy.start()
-    copy.wait()
-
-
-def later_block(saved, index, done):
-    return pl.pallas_call(
-        functools.partial(later_kernel, index),
-        in_specs=[pl.BlockSpec(memory_space=pl.ANY), VMEM],
+def held(value, index, *after):
+    return pl.pallas_call(
+        functools.partial(hold_kernel, index),
+        in_specs=[VMEM] * (1 + len(after)),
         out_specs=VMEM,
-        out_shape=pltpu.VMEM(saved.shape[1:], saved.dtype),
-        scratch_shapes=[pltpu.SemaphoreType.DMA],
-        compiler_params=pltpu.CompilerParams(vmem_limit_bytes=4 * MIB),
-        cost_estimate=SMALL,
-        name="later",
-    )(pltpu.with_memory_space_constraint(saved, pltpu.HBM), *near(done))
+        out_shape=pltpu.VMEM(value.shape[1:], value.dtype),
+        compiler_params=pltpu.CompilerParams(vmem_limit_bytes=2 * MIB),
+        cost_estimate=SMALL,
+        name="hold",
+    )(*near(value, *after))
 
 
 def forward(step, who, tokens, xs, metas, gate, up):
@@ -282,31 +305,43 @@
             pltpu.VMEM((local, rows, width), BF16),
             pltpu.VMEM((local, rows, 1), F32),
         ],
-        compiler_params=pltpu.CompilerParams(vmem_limit_bytes=11 * MIB),
+        compiler_params=pltpu.CompilerParams(vmem_limit_bytes=9 * MIB),
         cost_estimate=SMALL,
         name="forward",
     )(who[0], *near(*arrays))
 
 
-def backward(gs, a, b, pick, place, gate, up, down):
-    sources, local = len(gs), gate.shape[0]
-    tokens, width = gs[0].shape
-    hidden = gate.shape[1]
+def backward(gs, a, b, pick, place, gate, up, down, kept_type):
+    sources, pieces, local = len(gs), len(gs[0]), gate.shape[0]
+    tokens = gs[0][0].shape[0]
+    hidden, width = gate.shape[1:]
     rows = sources * MOST
-    outs = tuple(pltpu.VMEM((tokens, width), F32 if k == 0 else BF16) for k in range(sources))
-    return pl.pallas_call(
-        functools.partial(backward_kernel, sources, local),
-        in_specs=[VMEM] * (sources + 7),
+    half = width // 2
+    types = [kept_type] + [BF16] * (sources - 1)
+    outs = tuple(pltpu.VMEM((tokens, half), t) for t in types)
+    factor = pltpu.VMEM((local, rows, hidden), BF16)
+    back = pltpu.VMEM((sources // 2, local, PAIR, half), BF16)
+    *first, gate_grad, up_grad = pl.pallas_call(
+        functools.partial(backward_kernel, sources, pieces, slice(0, half)),
+        in_specs=[VMEM] * (sources * pieces + 7),
+        out_specs=(VMEM,) * (sources + 2),
+        out_shape=outs + (factor, factor),
+        scratch_shapes=[pltpu.VMEM((local, rows, width), BF16), back],
+        compiler_params=pltpu.CompilerParams(vmem_limit_bytes=11 * MIB),
+        cost_estimate=SMALL,
+        name="backward",
+    )(*near(*[g for block in gs for g in block], a, b, pick, place, gate, up, down))
+    rest = pl.pallas_call(
+        functools.partial(rest_kernel, sources, slice(half, width)),
+        in_specs=[VMEM] * 6,
         out_specs=(VMEM,) * sources,
         out_shape=outs,
-        scratch_shapes=[
-            pltpu.VMEM((local, rows, width), BF16),
-            pltpu.VMEM((sources // 2, local, PAIR, width), BF16),
-        ],
-        compiler_params=pltpu.CompilerParams(vmem_limit_bytes=13 * MIB),
-        cost_estimate=SMALL,
-        name="backward",
-    )(*near(*gs, a, b, pick, place, gate, up, down))
+        scratch_shapes=[back],
+        compiler_params=pltpu.CompilerParams(vmem_limit_bytes=6 * MIB),
+        cost_estimate=SMALL,
+        name="rest",
+    )(*near(gs[0][-1], gate_grad, up_grad, place, gate, up))
+    return first, rest
 
 
 def moved(value, by):
@@ -337,28 +372,26 @@
 
 def gathered_far(who, blocks, done):
     if blocks[2] is not None:
-        return blocks
+        return blocks, None
     value, left, _, right = blocks
-    return [value, left, swapped(chosen(who, done, left, right)), right]
-
-
-def scattered(who, parts, kept, move, beside, done):
-    count = lax.axis_size("expert")
-    if count != 4:
-        sent = [(parts[k], -k) for k in range(1, count)]
-    else:
-        own, left, far, right = parts
-        far = swapped(far)
-        to_left, to_right = joined(who, far, left, right, beside[1::2] if beside else ())
-        if beside is not None:
-            beside = gathered_far(who, beside, done)
-        sent = [(to_left, -1), (to_right, 1)]
-    total = kept + parts[0]
-    if move is moved_back:
-        total = moved_back(total.astype(BF16), 0).astype(F32)
+    passed = chosen(who, done, left, right)
+    return [value, left, swapped(passed), right], passed
+
+
+def joined_parts(who, parts, beside):
+    if lax.axis_size("expert") != 4:
+        return [(parts[k], -k) for k in range(1, len(parts))]
+    _, left, far, right = parts
+    to_left, to_right = joined(who, swapped(far), left, right, beside)
+    return [(to_left, -1), (to_right, 1)]
+
+
+def scattered(own, sent, last):
+    move = moved if last else moved_back
+    total = own if last else move(own, 0).astype(F32)
     for part, by in sent:
         total = total + move(part, by).astype(F32)
-    return total.astype(BF16), beside
+    return total.astype(BF16)
 
 
 def shards(grad_out, saved_inputs, routes, gate_weights, w_gate, w_up, w_down):
@@ -366,6 +399,7 @@
     local = gate.shape[0]
     tokens = grad_out.shape[1]
     steps = routes.shape[1]
+    ringed = lax.axis_size("expert") == 4
     place = lax.axis_index("expert").astype(jnp.int32)
     who = ((place * local).reshape(1), (place % 2).reshape(1))
     first, grad = first_blocks(
@@ -373,26 +407,27 @@
     )
     xs = gathered_near(first)
     gs = gathered_near(grad)
-    *back, done = turned(who, gate, up, down)
-    xs = gathered_far(who, xs, who[1])
+    xs, passed = gathered_far(who, xs, first)
     metas = xs
+    *back, done = turned(who, passed if ringed else first, gate, up, down)
+    gs = [[g] for g in gathered_far(who, gs, done)[0]]
     for step in range(steps):
         last = step + 1 == steps
-        if step == 0:
-            gs = gathered_far(who, gs, done)
         *factors, done = forward(step, who, tokens, xs, metas, back[0], back[1])
         if step:
-            gs = gathered_far(who, gs, done)
-        beside = None
+            gs = [list(block) for block in zip(*[gathered_far(who, g, done)[0] for g in gs])]
+        beside = ()
         if not last:
-            beside = gathered_near(later_block(saved_inputs[0], step + 1, done))
-        parts = backward(gs, *factors, *back)
-        grad, xs = scattered(
-            who, parts, grad.astype(F32), moved if last else moved_back, beside, done
-        )
+            following = held(saved_inputs[0], step + 1, gs[-2][0], done) if ringed else saved_inputs[0, step + 1]
+            xs = gathered_near(following)
+            beside = xs[1::2] if ringed else ()
+        halves = backward(gs, *factors, *back, F32 if last else BF16)
+        sent = [joined_parts(who, parts, beside) for parts in halves]
+        grads = [scattered(parts[0], pairs, last) for parts, pairs in zip(halves, sent)]
         if not last:
-            gs = gathered_near(grad)
-    return grad[None]
+            xs, _ = gathered_far(who, xs, done)
+            gs = [gathered_near(grad) for grad in grads]
+    return jnp.concatenate(grads, axis=1)[None]
 
 
 def solution(mesh):

time: 131 us -> 122 us (0.931)
  waiting for transfers between devices: 58.4 us -> 44.9 us
  starting transfers between devices: 29.9 us -> 37.6 us
  Pallas kernels: 40.9 us -> 38.5 us
    ppermute x10 -> x14, starting transfers between devices: 16.3 us -> 21.8 us  [moved(): lax.ppermute(value, 'expert', [(i, (i + by) % count) for i in range(count)])]
    ppermute x10 -> x14, waiting for transfers between devices: 27.7 us -> 22.8 us  [moved(): lax.ppermute(value, 'expert', [(i, (i + by) % count) for i in range(count)])]
    ppermute x3 -> x6, waiting for transfers between devices: 9.27 us -> 4.54 us  [moved_back(): return lax.ppermute(value, ('section', 'expert'), pairs)]
    ppermute x3 -> x6, starting transfers between devices: 3.74 us -> 7.89 us  [moved_back(): return lax.ppermute(value, ('section', 'expert'), pairs)]
    ppermute x6 -> x9, waiting for transfers between devices: 21.4 us -> 17.6 us  [swapped(): lax.ppermute(value, 'expert', [(i, i ^ 1) for i in range(lax.axis_size('e...]
    pallas_call x3 -> x5, Pallas kernels: 14.3 us -> 12.2 us  [the longest x2 8.21 us: backward(): pl.pallas_call(functools.partial(backward_kernel, sources, pieces, slice(...]
    ppermute x6 -> x9, starting transfers between devices: 9.78 us -> 7.92 us  [swapped(): lax.ppermute(value, 'expert', [(i, i ^ 1) for i in range(lax.axis_size('e...]
  transfers between devices with their start and end apart: 19 -> 29, of which waited for: 12 -> 19; matrix products, arithmetic and copies ran while one was open for 0% -> 0% of each run, Pallas kernels for 25% -> 27%
where the time goes in v3:
time: 122 us
  waiting for transfers between devices  44.9 us (37%)
  Pallas kernels  38.5 us (32%)
  starting transfers between devices  37.6 us (31%)
    ppermute x14, waiting for transfers between devices, moved(): lax.ppermute(value, 'expert', [(i, (i + by) % count) for i in range(count)])  22.8 us
    ppermute x14, starting transfers between devices, moved(): lax.ppermute(value, 'expert', [(i, (i + by) % count) for i in range(count)])  21.8 us
    ppermute x9, waiting for transfers between devices, swapped(): lax.ppermute(value, 'expert', [(i, i ^ 1) for i in range(lax.axis_size('e...  17.6 us
    pallas_call x1, Pallas kernels, turned(): pl.pallas_call(turn_kernel, grid=(local,), in_specs=[pl.BlockSpec(memory_...  12.6 us
    pallas_call x2, Pallas kernels, forward(): pl.pallas_call(functools.partial(forward_kernel, sources, local, tokens,...  12.4 us
    pallas_call x2, Pallas kernels, backward(): pl.pallas_call(functools.partial(backward_kernel, sources, pieces, slice(...  8.21 us
    ppermute x9, starting transfers between devices, swapped(): lax.ppermute(value, 'expert', [(i, i ^ 1) for i in range(lax.axis_size('e...  7.92 us
    ppermute x6, starting transfers between devices, moved_back(): return lax.ppermute(value, ('section', 'expert'), pairs)  7.89 us
  transfers between devices with their start and end apart: 29, of which 19 were waited for; matrix products, arithmetic and copies ran while one was open for 0% of the time, Pallas kernels for 27%

profile of v3, /device:TPU:0, one launch (start us, length us, event | category | flops | bytes accessed | tf_op | source)
XLA Modules:
  0.0 122.2 jit_solution(1741626770499038749)
XLA Ops:
  0.0 1.1 first.1
  1.1 5.1 %collective-permute-start.2 = (bf16[136,1024]{1,0:T(8,128)(2,1)S(1)}, bf16[136,1024]{1,0:T(8,128)(2,1)S(1)}, u32[]{:S(2)}, u32[]{:S(2)}) collective-permute-start(bf16[136,1024]{1,0:T(8,128)(2,1)S(1)} %get-tuple-element.50.done_ref.refs_0_.refs_4_), channel_id=1, source_target_pairs={{0,3},{1,0},{2,1},{3,2},{4,7},{5,4},{6,5},{7,6},{8,11},{9,8},{10,9... | collective-permute-start | bytes 835592 | tf_op jit(solution)/shard_map/ppermute | solution.py:349
  6.2 3.8 %collective-permute-start.3 = (bf16[128,1024]{1,0:T(8,128)(2,1)S(1)}, bf16[128,1024]{1,0:T(8,128)(2,1)S(1)}, u32[]{:S(2)}, u32[]{:S(2)}) collective-permute-start(bf16[128,1024]{1,0:T(8,128)(2,1)S(1)} %get-tuple-element.49.refs_0_.kept_ref), channel_id=1, source_target_pairs={{0,3},{1,0},{2,1},{3,2},{4,7},{5,4},{6,5},{7,6},{8,11},{9,8},{10,9... | collective-permute-start | bytes 786440 | tf_op jit(solution)/shard_map/ppermute | solution.py:349
  10.0 3.2 %collective-permute-done.2.right_ref.refs_3_.refs_7_ = bf16[136,1024]{1,0:T(8,128)(2,1)S(1)} collective-permute-done((bf16[136,1024]{1,0:T(8,128)(2,1)S(1)}, bf16[136,1024]{1,0:T(8,128)(2,1)S(1)}, u32[]{:S(2)}, u32[]{:S(2)}) %collective-permute-start.2) | collective-permute-done | bytes 278560 | tf_op jit(solution)/shard_map/ppermute | solution.py:349
  13.3 6.9 %collective-permute-done.1.left_ref.refs_1_.refs_5_ = bf16[136,1024]{1,0:T(8,128)(2,1)S(1)} collective-permute-done((bf16[136,1024]{1,0:T(8,128)(2,1)S(1)}, bf16[136,1024]{1,0:T(8,128)(2,1)S(1)}, u32[]{:S(2)}, u32[]{:S(2)}) %collective-permute-start.1) | collective-permute-done | bytes 278560 | tf_op jit(solution)/shard_map/ppermute | solution.py:349
  20.2 1.6 %collective-permute-start.5 = (bf16[136,1024]{1,0:T(8,128)(2,1)S(1)}, bf16[136,1024]{1,0:T(8,128)(2,1)S(1)}, u32[]{:S(2)}, u32[]{:S(2)}) collective-permute-start(bf16[136,1024]{1,0:T(8,128)(2,1)S(1)} %choose.5.refs_2_), channel_id=1, source_target_pairs={{0,1},{1,0},{2,3},{3,2},{4,5},{5,4},{6,7},{7,6},{8,9},{9,8},{10,11... | collective-permute-start | bytes 835592 | tf_op jit(solution)/shard_map/ppermute | solution.py:353
  21.8 12.6 %turn.1 = (bf16[8,512,1024]{2,1,0:T(8,128)(2,1)S(1)}, bf16[8,512,1024]{2,1,0:T(8,128)(2,1)S(1)}, bf16[8,1024,512]{2,1,0:T(8,128)(2,1)S(1)}, f32[8,128]{1,0:T(8,128)S(1)}) custom-call(s32[1]{0:T(128)} %bitcast.7.refs_0_.base_ref, s32[1]{0:T(128)} %bitcast.6.odd_ref.refs_1_, bf16[136,1024]{1,0:T(8,128)(2,1)S(1)} %choose.5.refs_2_, ...), custom_call_target="tpu_custom_call" | custom-call | bytes 1024 | tf_op jit(solution)/shard_map/turn/pallas_call | solution.py:195
  34.5 0.6 collective-permute-start.4
  35.1 1.4 %collective-permute-done.5.refs_2_.refs_6_ = bf16[136,1024]{1,0:T(8,128)(2,1)S(1)} collective-permute-done((bf16[136,1024]{1,0:T(8,128)(2,1)S(1)}, bf16[136,1024]{1,0:T(8,128)(2,1)S(1)}, u32[]{:S(2)}, u32[]{:S(2)}) %collective-permute-start.5) | collective-permute-done | bytes 278560 | tf_op jit(solution)/shard_map/ppermute | solution.py:353
  36.5 6.2 %forward.2 = (f32[8,160,512]{2,1,0:T(8,128)S(1)}, f32[8,160,512]{2,1,0:T(8,128)S(1)}, bf16[2,640,256]{2,1,0:T(8,128)(2,1)S(1)}, bf16[2,256,640]{2,1,0:T(8,128)(2,1)S(1)}, f32[8,128]{1,0:T(8,128)S(1)}) custom-call(s32[1]{0:T(128)} %bitcast.7.refs_0_.base_ref, bf16[136,1024]{1,0:T(8,128)(2,1)S(1)} %get-tuple-element.50.done_ref.refs_0_.refs_4_, ...), custom_call_target="tpu_custom_call" | custom-call | bytes 1024 | tf_op jit(solution)/shard_map/forward/pallas_call | solution.py:293
  42.7 3.0 %collective-permute-start.9 = (bf16[128,1024]{1,0:T(8,128)(2,1)S(1)}, bf16[128,1024]{1,0:T(8,128)(2,1)S(1)}, u32[]{:S(2)}, u32[]{:S(2)}) collective-permute-start(bf16[128,1024]{1,0:T(8,128)(2,1)S(1)} %hold.1.refs_0_), channel_id=1, source_target_pairs={{0,3},{1,0},{2,1},{3,2},{4,7},{5,4},{6,5},{7,6},{8,11},{9,8},{10,9... | collective-permute-start | bytes 786440 | tf_op jit(solution)/shard_map/ppermute | solution.py:349
  45.7 4.0 %backward.2 = (bf16[128,512]{1,0:T(8,128)(2,1)S(1)}, bf16[128,512]{1,0:T(8,128)(2,1)S(1)}, bf16[128,512]{1,0:T(8,128)(2,1)S(1)}, bf16[128,512]{1,0:T(8,128)(2,1)...) custom-call(bf16[128,1024]{1,0:T(8,128)(2,1)S(1)} %get-tuple-element.49.refs_0_.kept_ref, ...), custom_call_target="tpu_custom_call" | custom-call | bytes 1024 | tf_op jit(solution)/shard_map/backward/pallas_call | solution.py:324
  49.7 1.6 %collective-permute-start.7 = (bf16[128,512]{1,0:T(8,128)(2,1)S(1)}, bf16[128,512]{1,0:T(8,128)(2,1)S(1)}, u32[]{:S(2)}, u32[]{:S(2)}) collective-permute-start(bf16[128,512]{1,0:T(8,128)(2,1)S(1)} %get-tuple-element.60), channel_id=1, source_target_pairs={{0,1},{1,0},{2,3},{3,2},{4,5},{5,4},{6,7},{7,6},{8,9},{9,8},{10,11... | collective-permute-start | bytes 393224 | tf_op jit(solution)/shard_map/ppermute | solution.py:353
  51.4 2.0 %rest.2 = (bf16[128,512]{1,0:T(8,128)(2,1)S(1)}, bf16[128,512]{1,0:T(8,128)(2,1)S(1)}, bf16[128,512]{1,0:T(8,128)(2,1)S(1)}, bf16[128,512]{1,0:T(8,128)(2,1)S(1)}) custom-call(bf16[128,1024]{1,0:T(8,128)(2,1)S(1)} %get-tuple-element.49.refs_0_.kept_ref, bf16[8,160,512]{2,1,0:T(8,128)(2,1)S(1)} %get-tuple-element.66.gate_grad_ref, ...), custom_call_target="tpu_custom_call" | custom-call | bytes 1024 | tf_op jit(solution)/shard_map/rest/pallas_call | solution.py:334
  53.4 0.5 collective-permute-start.13
  53.9 5.5 %collective-permute-done.7.far_ref = bf16[128,512]{1,0:T(8,128)(2,1)S(1)} collective-permute-done((bf16[128,512]{1,0:T(8,128)(2,1)S(1)}, bf16[128,512]{1,0:T(8,128)(2,1)S(1)}, u32[]{:S(2)}, u32[]{:S(2)}) %collective-permute-start.7) | collective-permute-done | bytes 131104 | tf_op jit(solution)/shard_map/ppermute | solution.py:353
  59.4 2.2 %collective-permute-start.10 = (bf16[128,512]{1,0:T(8,128)(2,1)S(1)}, bf16[128,512]{1,0:T(8,128)(2,1)S(1)}, u32[]{:S(2)}, u32[]{:S(2)}) collective-permute-start(bf16[128,512]{1,0:T(8,128)(2,1)S(1)} %get-tuple-element.64), channel_id=1, source_target_pairs={{0,31},{1,28},{2,29},{3,30},{4,3},{5,0},{6,1},{7,2},{8,7},{9,4},{1... | collective-permute-start | bytes 393224 | tf_op jit(solution)/shard_map/ppermute | solution.py:363
  61.6 1.5 %collective-permute-start.11 = (bf16[128,512]{1,0:T(8,128)(2,1)S(1)}, bf16[128,512]{1,0:T(8,128)(2,1)S(1)}, u32[]{:S(2)}, u32[]{:S(2)}) collective-permute-start(bf16[128,512]{1,0:T(8,128)(2,1)S(1)} %get-tuple-element.65), channel_id=1, source_target_pairs={{0,29},{1,30},{2,31},{3,28},{4,1},{5,2},{6,3},{7,0},{8,5},{9,6},{1... | collective-permute-start | bytes 393224 | tf_op jit(solution)/shard_map/ppermute | solution.py:363
  63.1 0.7 collective-permute-start.12
  63.9 3.4 %collective-permute-start.14 = (bf16[128,512]{1,0:T(8,128)(2,1)S(1)}, bf16[128,512]{1,0:T(8,128)(2,1)S(1)}, u32[]{:S(2)}, u32[]{:S(2)}) collective-permute-start(bf16[128,512]{1,0:T(8,128)(2,1)S(1)} %get-tuple-element.72), channel_id=1, source_target_pairs={{0,31},{1,28},{2,29},{3,30},{4,3},{5,0},{6,1},{7,2},{8,7},{9,4},{1... | collective-permute-start | bytes 393224 | tf_op jit(solution)/shard_map/ppermute | solution.py:363
  67.5 0.4 collective-permute-done.11
  67.9 3.1 %collective-permute-start.19 = (bf16[128,512]{1,0:T(8,128)(2,1)S(1)}, bf16[128,512]{1,0:T(8,128)(2,1)S(1)}, u32[]{:S(2)}, u32[]{:S(2)}) collective-permute-start(bf16[128,512]{1,0:T(8,128)(2,1)S(1)} %add_convert_fusion.3.refs_0_), channel_id=1, source_target_pairs={{0,3},{1,0},{2,1},{3,2},{4,7},{5,4},{6,5},{7,6},{8,11},{9,8},{10,9... | collective-permute-start | bytes 393224 | tf_op jit(solution)/shard_map/ppermute | solution.py:349
  71.1 0.9 collective-permute-done.14
  72.0 3.2 %collective-permute-done.15 = bf16[128,512]{1,0:T(8,128)(2,1)S(1)} collective-permute-done((bf16[128,512]{1,0:T(8,128)(2,1)S(1)}, bf16[128,512]{1,0:T(8,128)(2,1)S(1)}, u32[]{:S(2)}, u32[]{:S(2)}) %collective-permute-start.15) | collective-permute-done | bytes 131104 | tf_op jit(solution)/shard_map/ppermute | solution.py:363
  75.2 0.8 collective-permute-start.21
  76.1 1.3 %collective-permute-start.17 = (bf16[128,512]{1,0:T(8,128)(2,1)S(1)}, bf16[128,512]{1,0:T(8,128)(2,1)S(1)}, u32[]{:S(2)}, u32[]{:S(2)}) collective-permute-start(bf16[128,512]{1,0:T(8,128)(2,1)S(1)} %add_convert_fusion.2.refs_1_.kept_ref), channel_id=1, source_target_pairs={{0,1},{1,2},{2,3},{3,0},{4,5},{5,6},{6,7},{7,4},{8,9},{9,10},{10,1... | collective-permute-start | bytes 393224 | tf_op jit(solution)/shard_map/ppermute | solution.py:349
  77.3 3.1 %collective-permute-done.18.refs_2_ = bf16[128,1024]{1,0:T(8,128)(2,1)S(1)} collective-permute-done((bf16[128,1024]{1,0:T(8,128)(2,1)S(1)}, bf16[128,1024]{1,0:T(8,128)(2,1)S(1)}, u32[]{:S(2)}, u32[]{:S(2)}) %collective-permute-start.18) | collective-permute-done | bytes 262176 | tf_op jit(solution)/shard_map/ppermute | solution.py:353
  80.4 6.2 %forward.3 = (f32[8,160,512]{2,1,0:T(8,128)S(1)}, f32[8,160,512]{2,1,0:T(8,128)S(1)}, bf16[2,640,256]{2,1,0:T(8,128)(2,1)S(1)}, bf16[2,256,640]{2,1,0:T(8,128)(2,1)S(1)}, f32[8,128]{1,0:T(8,128)S(1)}) custom-call(s32[1]{0:T(128)} %bitcast.7.refs_0_.base_ref, bf16[128,1024]{1,0:T(8,128)(2,1)S(1)} %hold.1.refs_0_, ...), custom_call_target="tpu_custom_call" | custom-call | bytes 1024 | tf_op jit(solution)/shard_map/forward/pallas_call | solution.py:293
  86.6 0.8 collective-permute-done.16.left_ref.refs_2_
  87.4 1.0 collective-permute-start.20
  88.4 0.5 collective-permute-done.21.right_ref.refs_7_
  88.9 4.2 %collective-permute-done.17.left_ref.refs_3_ = bf16[128,512]{1,0:T(8,128)(2,1)S(1)} collective-permute-done((bf16[128,512]{1,0:T(8,128)(2,1)S(1)}, bf16[128,512]{1,0:T(8,128)(2,1)S(1)}, u32[]{:S(2)}, u32[]{:S(2)}) %collective-permute-start.17) | collective-permute-done | bytes 131104 | tf_op jit(solution)/shard_map/ppermute | solution.py:349
  93.0 0.4 collective-permute-start.22
  93.5 1.6 %collective-permute-done.20.refs_4_ = bf16[128,512]{1,0:T(8,128)(2,1)S(1)} collective-permute-done((bf16[128,512]{1,0:T(8,128)(2,1)S(1)}, bf16[128,512]{1,0:T(8,128)(2,1)S(1)}, u32[]{:S(2)}, u32[]{:S(2)}) %collective-permute-start.20) | collective-permute-done | bytes 131104 | tf_op jit(solution)/shard_map/ppermute | solution.py:353
  95.0 3.1 %collective-permute-done.22.refs_5_ = bf16[128,512]{1,0:T(8,128)(2,1)S(1)} collective-permute-done((bf16[128,512]{1,0:T(8,128)(2,1)S(1)}, bf16[128,512]{1,0:T(8,128)(2,1)S(1)}, u32[]{:S(2)}, u32[]{:S(2)}) %collective-permute-start.22) | collective-permute-done | bytes 131104 | tf_op jit(solution)/shard_map/ppermute | solution.py:353
  98.1 4.2 %backward.3 = (f32[128,512]{1,0:T(8,128)S(1)}, bf16[128,512]{1,0:T(8,128)(2,1)S(1)}, bf16[128,512]{1,0:T(8,128)(2,1)S(1)}, bf16[128,512]{1,0:T(8,128)(2,1)S(1)},...) custom-call(bf16[128,512]{1,0:T(8,128)(2,1)S(1)} %add_convert_fusion.3.refs_0_, ...), custom_call_target="tpu_custom_call" | custom-call | bytes 1024 | tf_op jit(solution)/shard_map/backward/pallas_call | solution.py:324
  102.3 0.4 collective-permute-start.23
  102.7 2.0 %rest.3 = (f32[128,512]{1,0:T(8,128)S(1)}, bf16[128,512]{1,0:T(8,128)(2,1)S(1)}, bf16[128,512]{1,0:T(8,128)(2,1)S(1)}, bf16[128,512]{1,0:T(8,128)(2,1)S(1)}) custom-call(bf16[128,512]{1,0:T(8,128)(2,1)S(1)} %add_convert_fusion.2.refs_1_.kept_ref, bf16[8,160,512]{2,1,0:T(8,128)(2,1)S(1)} %get-tuple-element.85.gate_grad_ref, ...), custom_call_target="tpu_custom_call" | custom-call | bytes 1024 | tf_op jit(solution)/shard_map/rest/pallas_call | solution.py:334
  104.7 1.7 %collective-permute-start.26 = (bf16[128,512]{1,0:T(8,128)(2,1)S(1)}, bf16[128,512]{1,0:T(8,128)(2,1)S(1)}, u32[]{:S(2)}, u32[]{:S(2)}) collective-permute-start(bf16[128,512]{1,0:T(8,128)(2,1)S(1)} %get-tuple-element.88), channel_id=1, source_target_pairs={{0,1},{1,0},{2,3},{3,2},{4,5},{5,4},{6,7},{7,6},{8,9},{9,8},{10,11... | collective-permute-start | bytes 393224 | tf_op jit(solution)/shard_map/ppermute | solution.py:353
  106.4 2.2 %collective-permute-done.23.far_ref = bf16[128,512]{1,0:T(8,128)(2,1)S(1)} collective-permute-done((bf16[128,512]{1,0:T(8,128)(2,1)S(1)}, bf16[128,512]{1,0:T(8,128)(2,1)S(1)}, u32[]{:S(2)}, u32[]{:S(2)}) %collective-permute-start.23) | collective-permute-done | bytes 131104 | tf_op jit(solution)/shard_map/ppermute | solution.py:353
  108.7 2.0 %collective-permute-start.25 = (bf16[128,512]{1,0:T(8,128)(2,1)S(1)}, bf16[128,512]{1,0:T(8,128)(2,1)S(1)}, u32[]{:S(2)}, u32[]{:S(2)}) collective-permute-start(bf16[128,512]{1,0:T(8,128)(2,1)S(1)} %get-tuple-element.84), channel_id=1, source_target_pairs={{0,1},{1,2},{2,3},{3,0},{4,5},{5,6},{6,7},{7,4},{8,9},{9,10},{10,1... | collective-permute-start | bytes 393224 | tf_op jit(solution)/shard_map/ppermute | solution.py:349
  110.8 0.7 collective-permute-done.26.far_ref
  111.5 2.6 %collective-permute-start.27 = (bf16[128,512]{1,0:T(8,128)(2,1)S(1)}, bf16[128,512]{1,0:T(8,128)(2,1)S(1)}, u32[]{:S(2)}, u32[]{:S(2)}) collective-permute-start(bf16[128,512]{1,0:T(8,128)(2,1)S(1)} %get-tuple-element.91), channel_id=1, source_target_pairs={{0,3},{1,0},{2,1},{3,2},{4,7},{5,4},{6,5},{7,6},{8,11},{9,8},{10,9... | collective-permute-start | bytes 393224 | tf_op jit(solution)/shard_map/ppermute | solution.py:349
  114.1 1.8 %collective-permute-done.24 = bf16[128,512]{1,0:T(8,128)(2,1)S(1)} collective-permute-done((bf16[128,512]{1,0:T(8,128)(2,1)S(1)}, bf16[128,512]{1,0:T(8,128)(2,1)S(1)}, u32[]{:S(2)}, u32[]{:S(2)}) %collective-permute-start.24) | collective-permute-done | bytes 131104 | tf_op jit(solution)/shard_map/ppermute | solution.py:349
  115.9 1.7 %collective-permute-done.25 = bf16[128,512]{1,0:T(8,128)(2,1)S(1)} collective-permute-done((bf16[128,512]{1,0:T(8,128)(2,1)S(1)}, bf16[128,512]{1,0:T(8,128)(2,1)S(1)}, u32[]{:S(2)}, u32[]{:S(2)}) %collective-permute-start.25) | collective-permute-done | bytes 131104 | tf_op jit(solution)/shard_map/ppermute | solution.py:349
  117.7 1.7 %collective-permute-done.27 = bf16[128,512]{1,0:T(8,128)(2,1)S(1)} collective-permute-done((bf16[128,512]{1,0:T(8,128)(2,1)S(1)}, bf16[128,512]{1,0:T(8,128)(2,1)S(1)}, u32[]{:S(2)}, u32[]{:S(2)}) %collective-permute-start.27) | collective-permute-done | bytes 131104 | tf_op jit(solution)/shard_map/ppermute | solution.py:349
  119.4 2.0 %collective-permute-done.28 = bf16[128,512]{1,0:T(8,128)(2,1)S(1)} collective-permute-done((bf16[128,512]{1,0:T(8,128)(2,1)S(1)}, bf16[128,512]{1,0:T(8,128)(2,1)S(1)}, u32[]{:S(2)}, u32[]{:S(2)}) %collective-permute-start.28) | collective-permute-done | bytes 131104 | tf_op jit(solution)/shard_map/ppermute | solution.py:349
  121.4 0.7 maximum_bitcast_fusion
  (35 shorter events, 0.7 us)
Async XLA Ops:
  1.1 12.2 %collective-permute-start.2 = (bf16[136,1024]{1,0:T(8,128)(2,1)S(1)}, bf16[136,1024]{1,0:T(8,128)(2,1)S(1)}, u32[]{:S(2)}, u32[]{:S(2)}) collective-permute-start(bf16[136,1024]{1,0:T(8,128)(2,1)S(1)} %get-tuple-element.50.done_ref.refs_0_.refs_4_), channel_id=1, source_target_pairs={{0,3},{1,0},{2,1},{3,2},{4,7},{5,4},{6,5},{7,6},{8,11},{9,8},{10,9... | collective-permute-start | bytes 835592 | tf_op jit(solution)/shard_map/ppermute | solution.py:349
  6.2 14.0 %collective-permute-start.1 = (bf16[136,1024]{1,0:T(8,128)(2,1)S(1)}, bf16[136,1024]{1,0:T(8,128)(2,1)S(1)}, u32[]{:S(2)}, u32[]{:S(2)}) collective-permute-start(bf16[136,1024]{1,0:T(8,128)(2,1)S(1)} %get-tuple-element.50.done_ref.refs_0_.refs_4_), channel_id=1, source_target_pairs={{0,1},{1,2},{2,3},{3,0},{4,5},{5,6},{6,7},{7,4},{8,9},{9,10},{10,1... | collective-permute-start | bytes 835592 | tf_op jit(solution)/shard_map/ppermute | solution.py:349
  6.2 28.2 %collective-permute-start.3 = (bf16[128,1024]{1,0:T(8,128)(2,1)S(1)}, bf16[128,1024]{1,0:T(8,128)(2,1)S(1)}, u32[]{:S(2)}, u32[]{:S(2)}) collective-permute-start(bf16[128,1024]{1,0:T(8,128)(2,1)S(1)} %get-tuple-element.49.refs_0_.kept_ref), channel_id=1, source_target_pairs={{0,3},{1,0},{2,1},{3,2},{4,7},{5,4},{6,5},{7,6},{8,11},{9,8},{10,9... | collective-permute-start | bytes 786440 | tf_op jit(solution)/shard_map/ppermute | solution.py:349
  10.0 24.4 %collective-permute-start = (bf16[128,1024]{1,0:T(8,128)(2,1)S(1)}, bf16[128,1024]{1,0:T(8,128)(2,1)S(1)}, u32[]{:S(2)}, u32[]{:S(2)}) collective-permute-start(bf16[128,1024]{1,0:T(8,128)(2,1)S(1)} %get-tuple-element.49.refs_0_.kept_ref), channel_id=1, source_target_pairs={{0,1},{1,2},{2,3},{3,0},{4,5},{5,6},{6,7},{7,4},{8,9},{9,10},{10,1... | collective-permute-start | bytes 786440 | tf_op jit(solution)/shard_map/ppermute | solution.py:349
  20.2 16.3 %collective-permute-start.5 = (bf16[136,1024]{1,0:T(8,128)(2,1)S(1)}, bf16[136,1024]{1,0:T(8,128)(2,1)S(1)}, u32[]{:S(2)}, u32[]{:S(2)}) collective-permute-start(bf16[136,1024]{1,0:T(8,128)(2,1)S(1)} %choose.5.refs_2_), channel_id=1, source_target_pairs={{0,1},{1,0},{2,3},{3,2},{4,5},{5,4},{6,7},{7,6},{8,9},{9,8},{10,11... | collective-permute-start | bytes 835592 | tf_op jit(solution)/shard_map/ppermute | solution.py:353
  34.5 8.2 %collective-permute-start.4 = (bf16[128,1024]{1,0:T(8,128)(2,1)S(1)}, bf16[128,1024]{1,0:T(8,128)(2,1)S(1)}, u32[]{:S(2)}, u32[]{:S(2)}) collective-permute-start(bf16[128,1024]{1,0:T(8,128)(2,1)S(1)} %choose.6), channel_id=1, source_target_pairs={{0,1},{1,0},{2,3},{3,2},{4,5},{5,4},{6,7},{7,6},{8,9},{9,8},{10,11... | collective-permute-start | bytes 786440 | tf_op jit(solution)/shard_map/ppermute | solution.py:353
  36.5 6.2 %copy-start = (bf16[1,2,128,1024]{3,2,1,0:T(8,128)(2,1)S(1)}, bf16[1,2,128,1024]{3,2,1,0:T(8,128)(2,1)}, u32[]{:S(2)}) copy-start(bf16[1,2,128,1024]{3,2,1,0:T(8,128)(2,1)} %param.8) | copy-start | bytes 1572868
  42.7 16.6 %collective-permute-start.9 = (bf16[128,1024]{1,0:T(8,128)(2,1)S(1)}, bf16[128,1024]{1,0:T(8,128)(2,1)S(1)}, u32[]{:S(2)}, u32[]{:S(2)}) collective-permute-start(bf16[128,1024]{1,0:T(8,128)(2,1)S(1)} %hold.1.refs_0_), channel_id=1, source_target_pairs={{0,3},{1,0},{2,1},{3,2},{4,7},{5,4},{6,5},{7,6},{8,11},{9,8},{10,9... | collective-permute-start | bytes 786440 | tf_op jit(solution)/shard_map/ppermute | solution.py:349
  45.7 13.7 %collective-permute-start.8 = (bf16[128,1024]{1,0:T(8,128)(2,1)S(1)}, bf16[128,1024]{1,0:T(8,128)(2,1)S(1)}, u32[]{:S(2)}, u32[]{:S(2)}) collective-permute-start(bf16[128,1024]{1,0:T(8,128)(2,1)S(1)} %hold.1.refs_0_), channel_id=1, source_target_pairs={{0,1},{1,2},{2,3},{3,0},{4,5},{5,6},{6,7},{7,4},{8,9},{9,10},{10,1... | collective-permute-start | bytes 786440 | tf_op jit(solution)/shard_map/ppermute | solution.py:349
  49.7 9.6 %collective-permute-start.7 = (bf16[128,512]{1,0:T(8,128)(2,1)S(1)}, bf16[128,512]{1,0:T(8,128)(2,1)S(1)}, u32[]{:S(2)}, u32[]{:S(2)}) collective-permute-start(bf16[128,512]{1,0:T(8,128)(2,1)S(1)} %get-tuple-element.60), channel_id=1, source_target_pairs={{0,1},{1,0},{2,3},{3,2},{4,5},{5,4},{6,7},{7,6},{8,9},{9,8},{10,11... | collective-permute-start | bytes 393224 | tf_op jit(solution)/shard_map/ppermute | solution.py:353
  53.4 10.5 %collective-permute-start.13 = (bf16[128,512]{1,0:T(8,128)(2,1)S(1)}, bf16[128,512]{1,0:T(8,128)(2,1)S(1)}, u32[]{:S(2)}, u32[]{:S(2)}) collective-permute-start(bf16[128,512]{1,0:T(8,128)(2,1)S(1)} %get-tuple-element.69), channel_id=1, source_target_pairs={{0,1},{1,0},{2,3},{3,2},{4,5},{5,4},{6,7},{7,6},{8,9},{9,8},{10,11... | collective-permute-start | bytes 393224 | tf_op jit(solution)/shard_map/ppermute | solution.py:353
  53.9 13.4 %collective-permute-start.6 = (bf16[128,512]{1,0:T(8,128)(2,1)S(1)}, bf16[128,512]{1,0:T(8,128)(2,1)S(1)}, u32[]{:S(2)}, u32[]{:S(2)}) collective-permute-start(bf16[128,512]{1,0:T(8,128)(2,1)S(1)} %get-tuple-element.59), channel_id=1, source_target_pairs={{0,28},{1,29},{2,30},{3,31},{4,0},{5,1},{6,2},{7,3},{8,4},{9,5},{1... | collective-permute-start | bytes 393224 | tf_op jit(solution)/shard_map/ppermute | solution.py:363
  59.4 8.0 %collective-permute-start.10 = (bf16[128,512]{1,0:T(8,128)(2,1)S(1)}, bf16[128,512]{1,0:T(8,128)(2,1)S(1)}, u32[]{:S(2)}, u32[]{:S(2)}) collective-permute-start(bf16[128,512]{1,0:T(8,128)(2,1)S(1)} %get-tuple-element.64), channel_id=1, source_target_pairs={{0,31},{1,28},{2,29},{3,30},{4,3},{5,0},{6,1},{7,2},{8,7},{9,4},{1... | collective-permute-start | bytes 393224 | tf_op jit(solution)/shard_map/ppermute | solution.py:363
  61.6 6.3 %collective-permute-start.11 = (bf16[128,512]{1,0:T(8,128)(2,1)S(1)}, bf16[128,512]{1,0:T(8,128)(2,1)S(1)}, u32[]{:S(2)}, u32[]{:S(2)}) collective-permute-start(bf16[128,512]{1,0:T(8,128)(2,1)S(1)} %get-tuple-element.65), channel_id=1, source_target_pairs={{0,29},{1,30},{2,31},{3,28},{4,1},{5,2},{6,3},{7,0},{8,5},{9,6},{1... | collective-permute-start | bytes 393224 | tf_op jit(solution)/shard_map/ppermute | solution.py:363
  63.1 8.0 %collective-permute-start.12 = (bf16[128,512]{1,0:T(8,128)(2,1)S(1)}, bf16[128,512]{1,0:T(8,128)(2,1)S(1)}, u32[]{:S(2)}, u32[]{:S(2)}) collective-permute-start(bf16[128,512]{1,0:T(8,128)(2,1)S(1)} %get-tuple-element.68), channel_id=1, source_target_pairs={{0,28},{1,29},{2,30},{3,31},{4,0},{5,1},{6,2},{7,3},{8,4},{9,5},{1... | collective-permute-start | bytes 393224 | tf_op jit(solution)/shard_map/ppermute | solution.py:363
  63.9 8.1 %collective-permute-start.14 = (bf16[128,512]{1,0:T(8,128)(2,1)S(1)}, bf16[128,512]{1,0:T(8,128)(2,1)S(1)}, u32[]{:S(2)}, u32[]{:S(2)}) collective-permute-start(bf16[128,512]{1,0:T(8,128)(2,1)S(1)} %get-tuple-element.72), channel_id=1, source_target_pairs={{0,31},{1,28},{2,29},{3,30},{4,3},{5,0},{6,1},{7,2},{8,7},{9,4},{1... | collective-permute-start | bytes 393224 | tf_op jit(solution)/shard_map/ppermute | solution.py:363
  67.3 7.9 %collective-permute-start.15 = (bf16[128,512]{1,0:T(8,128)(2,1)S(1)}, bf16[128,512]{1,0:T(8,128)(2,1)S(1)}, u32[]{:S(2)}, u32[]{:S(2)}) collective-permute-start(bf16[128,512]{1,0:T(8,128)(2,1)S(1)} %get-tuple-element.73), channel_id=1, source_target_pairs={{0,29},{1,30},{2,31},{3,28},{4,1},{5,2},{6,3},{7,0},{8,5},{9,6},{1... | collective-permute-start | bytes 393224 | tf_op jit(solution)/shard_map/ppermute | solution.py:363
  67.4 13.0 %collective-permute-start.18 = (bf16[128,1024]{1,0:T(8,128)(2,1)S(1)}, bf16[128,1024]{1,0:T(8,128)(2,1)S(1)}, u32[]{:S(2)}, u32[]{:S(2)}) collective-permute-start(bf16[128,1024]{1,0:T(8,128)(2,1)S(1)} %choose.7), channel_id=1, source_target_pairs={{0,1},{1,0},{2,3},{3,2},{4,5},{5,4},{6,7},{7,6},{8,9},{9,8},{10,11... | collective-permute-start | bytes 786440 | tf_op jit(solution)/shard_map/ppermute | solution.py:353
  67.9 18.7 %collective-permute-start.19 = (bf16[128,512]{1,0:T(8,128)(2,1)S(1)}, bf16[128,512]{1,0:T(8,128)(2,1)S(1)}, u32[]{:S(2)}, u32[]{:S(2)}) collective-permute-start(bf16[128,512]{1,0:T(8,128)(2,1)S(1)} %add_convert_fusion.3.refs_0_), channel_id=1, source_target_pairs={{0,3},{1,0},{2,1},{3,2},{4,7},{5,4},{6,5},{7,6},{8,11},{9,8},{10,9... | collective-permute-start | bytes 393224 | tf_op jit(solution)/shard_map/ppermute | solution.py:349
  71.1 16.4 %collective-permute-start.16 = (bf16[128,512]{1,0:T(8,128)(2,1)S(1)}, bf16[128,512]{1,0:T(8,128)(2,1)S(1)}, u32[]{:S(2)}, u32[]{:S(2)}) collective-permute-start(bf16[128,512]{1,0:T(8,128)(2,1)S(1)} %add_convert_fusion.3.refs_0_), channel_id=1, source_target_pairs={{0,1},{1,2},{2,3},{3,0},{4,5},{5,6},{6,7},{7,4},{8,9},{9,10},{10,1... | collective-permute-start | bytes 393224 | tf_op jit(solution)/shard_map/ppermute | solution.py:349
  75.2 13.6 %collective-permute-start.21 = (bf16[128,512]{1,0:T(8,128)(2,1)S(1)}, bf16[128,512]{1,0:T(8,128)(2,1)S(1)}, u32[]{:S(2)}, u32[]{:S(2)}) collective-permute-start(bf16[128,512]{1,0:T(8,128)(2,1)S(1)} %add_convert_fusion.2.refs_1_.kept_ref), channel_id=1, source_target_pairs={{0,3},{1,0},{2,1},{3,2},{4,7},{5,4},{6,5},{7,6},{8,11},{9,8},{10,9... | collective-permute-start | bytes 393224 | tf_op jit(solution)/shard_map/ppermute | solution.py:349
  76.1 17.0 %collective-permute-start.17 = (bf16[128,512]{1,0:T(8,128)(2,1)S(1)}, bf16[128,512]{1,0:T(8,128)(2,1)S(1)}, u32[]{:S(2)}, u32[]{:S(2)}) collective-permute-start(bf16[128,512]{1,0:T(8,128)(2,1)S(1)} %add_convert_fusion.2.refs_1_.kept_ref), channel_id=1, source_target_pairs={{0,1},{1,2},{2,3},{3,0},{4,5},{5,6},{6,7},{7,4},{8,9},{9,10},{10,1... | collective-permute-start | bytes 393224 | tf_op jit(solution)/shard_map/ppermute | solution.py:349
  87.4 7.6 %collective-permute-start.20 = (bf16[128,512]{1,0:T(8,128)(2,1)S(1)}, bf16[128,512]{1,0:T(8,128)(2,1)S(1)}, u32[]{:S(2)}, u32[]{:S(2)}) collective-permute-start(bf16[128,512]{1,0:T(8,128)(2,1)S(1)} %choose.8), channel_id=1, source_target_pairs={{0,1},{1,0},{2,3},{3,2},{4,5},{5,4},{6,7},{7,6},{8,9},{9,8},{10,11... | collective-permute-start | bytes 393224 | tf_op jit(solution)/shard_map/ppermute | solution.py:353
  93.0 5.0 %collective-permute-start.22 = (bf16[128,512]{1,0:T(8,128)(2,1)S(1)}, bf16[128,512]{1,0:T(8,128)(2,1)S(1)}, u32[]{:S(2)}, u32[]{:S(2)}) collective-permute-start(bf16[128,512]{1,0:T(8,128)(2,1)S(1)} %choose.9), channel_id=1, source_target_pairs={{0,1},{1,0},{2,3},{3,2},{4,5},{5,4},{6,7},{7,6},{8,9},{9,8},{10,11... | collective-permute-start | bytes 393224 | tf_op jit(solution)/shard_map/ppermute | solution.py:353
  102.3 6.4 %collective-permute-start.23 = (bf16[128,512]{1,0:T(8,128)(2,1)S(1)}, bf16[128,512]{1,0:T(8,128)(2,1)S(1)}, u32[]{:S(2)}, u32[]{:S(2)}) collective-permute-start(bf16[128,512]{1,0:T(8,128)(2,1)S(1)} %get-tuple-element.80), channel_id=1, source_target_pairs={{0,1},{1,0},{2,3},{3,2},{4,5},{5,4},{6,7},{7,6},{8,9},{9,8},{10,11... | collective-permute-start | bytes 393224 | tf_op jit(solution)/shard_map/ppermute | solution.py:353
  104.7 6.8 %collective-permute-start.26 = (bf16[128,512]{1,0:T(8,128)(2,1)S(1)}, bf16[128,512]{1,0:T(8,128)(2,1)S(1)}, u32[]{:S(2)}, u32[]{:S(2)}) collective-permute-start(bf16[128,512]{1,0:T(8,128)(2,1)S(1)} %get-tuple-element.88), channel_id=1, source_target_pairs={{0,1},{1,0},{2,3},{3,2},{4,5},{5,4},{6,7},{7,6},{8,9},{9,8},{10,11... | collective-permute-start | bytes 393224 | tf_op jit(solution)/shard_map/ppermute | solution.py:353
  108.7 7.2 %collective-permute-start.24 = (bf16[128,512]{1,0:T(8,128)(2,1)S(1)}, bf16[128,512]{1,0:T(8,128)(2,1)S(1)}, u32[]{:S(2)}, u32[]{:S(2)}) collective-permute-start(bf16[128,512]{1,0:T(8,128)(2,1)S(1)} %get-tuple-element.83), channel_id=1, source_target_pairs={{0,3},{1,0},{2,1},{3,2},{4,7},{5,4},{6,5},{7,6},{8,11},{9,8},{10,9... | collective-permute-start | bytes 393224 | tf_op jit(solution)/shard_map/ppermute | solution.py:349
  108.7 8.9 %collective-permute-start.25 = (bf16[128,512]{1,0:T(8,128)(2,1)S(1)}, bf16[128,512]{1,0:T(8,128)(2,1)S(1)}, u32[]{:S(2)}, u32[]{:S(2)}) collective-permute-start(bf16[128,512]{1,0:T(8,128)(2,1)S(1)} %get-tuple-element.84), channel_id=1, source_target_pairs={{0,1},{1,2},{2,3},{3,0},{4,5},{5,6},{6,7},{7,4},{8,9},{9,10},{10,1... | collective-permute-start | bytes 393224 | tf_op jit(solution)/shard_map/ppermute | solution.py:349
  111.5 7.9 %collective-permute-start.27 = (bf16[128,512]{1,0:T(8,128)(2,1)S(1)}, bf16[128,512]{1,0:T(8,128)(2,1)S(1)}, u32[]{:S(2)}, u32[]{:S(2)}) collective-permute-start(bf16[128,512]{1,0:T(8,128)(2,1)S(1)} %get-tuple-element.91), channel_id=1, source_target_pairs={{0,3},{1,0},{2,1},{3,2},{4,7},{5,4},{6,5},{7,6},{8,11},{9,8},{10,9... | collective-permute-start | bytes 393224 | tf_op jit(solution)/shard_map/ppermute | solution.py:349
  114.1 7.3 %collective-permute-start.28 = (bf16[128,512]{1,0:T(8,128)(2,1)S(1)}, bf16[128,512]{1,0:T(8,128)(2,1)S(1)}, u32[]{:S(2)}, u32[]{:S(2)}) collective-permute-start(bf16[128,512]{1,0:T(8,128)(2,1)S(1)} %get-tuple-element.92), channel_id=1, source_target_pairs={{0,1},{1,2},{2,3},{3,0},{4,5},{5,6},{6,7},{7,4},{8,9},{9,10},{10,1... | collective-permute-start | bytes 393224 | tf_op jit(solution)/shard_map/ppermute | solution.py:349

commit v4 on v3

--- a/solution.py
+++ b/solution.py
@@ -142,13 +142,17 @@
     refs[-1][...] = value_ref[index]
 
 
-def turn_kernel(*refs):
+def turn_kernel(count, *refs):
     e = pl.program_id(0)
     refs = refs[3:]
-    count = len(refs) // 2
-    for from_ref, to_ref in zip(refs[:count], refs[count:-1]):
+    for from_ref, to_ref in zip(refs[:count], refs[count:]):
         to_ref[e] = from_ref[0].T
     refs[-1][...] = jnp.zeros_like(refs[-1])
+
+
+def turn_into_kernel(from_ref, after_ref, held_ref, to_ref, done_ref):
+    to_ref[pl.program_id(0)] = from_ref[0].T
+    done_ref[...] = jnp.zeros_like(done_ref)
 
 
 def first_kernel(saved_ref, grad_ref, routes_from, weights_from, out_ref, grad_out_ref, routes_ref, weights_ref, sems):
@@ -193,15 +197,29 @@
     local = weights[0].shape[0]
     shapes = [(local, w.shape[2], w.shape[1]) for w in weights]
     return pl.pallas_call(
-        turn_kernel,
+        functools.partial(turn_kernel, len(weights) - 1),
         grid=(local,),
-        in_specs=[pl.BlockSpec(memory_space=pltpu.SMEM)] * 2 + [VMEM] + [one(w.shape) for w in weights],
+        in_specs=[pl.BlockSpec(memory_space=pltpu.SMEM)] * 2 + [VMEM] + [one(w.shape) for w in weights[:-1]],
         out_specs=(VMEM,) * (len(weights) + 1),
         out_shape=(*[pltpu.VMEM(shape, BF16) for shape in shapes], DONE),
         compiler_params=pltpu.CompilerParams(vmem_limit_bytes=10 * MIB),
         cost_estimate=SMALL,
         name="turn",
-    )(*who, *near(after), *[pltpu.with_memory_space_constraint(w, pltpu.HBM) for w in weights])
+    )(*who, *near(after), *[pltpu.with_memory_space_constraint(w, pltpu.HBM) for w in weights[:-1]])
+
+
+def turned_into(place, after, weight):
+    return pl.pallas_call(
+        turn_into_kernel,
+        grid=(weight.shape[0],),
+        in_specs=[one(weight.shape), VMEM, VMEM],
+        out_specs=(VMEM, VMEM),
+        out_shape=(pltpu.VMEM(place.shape, BF16), DONE),
+        input_output_aliases={2: 0},
+        compiler_params=pltpu.CompilerParams(vmem_limit_bytes=6 * MIB),
+        cost_estimate=SMALL,
+        name="turn_into",
+    )(pltpu.with_memory_space_constraint(weight, pltpu.HBM), *near(after, place))
 
 
 def first_blocks(saved, grad, routes, weights):
@@ -386,12 +404,25 @@
     return [(to_left, -1), (to_right, 1)]
 
 
-def scattered(own, sent, last):
+def sum_kernel(count, *refs):
+    total = refs[0][...].astype(F32)
+    for ref in refs[1:count]:
+        total = total + ref[...].astype(F32)
+    refs[-1][...] = total.astype(BF16)
+
+
+def scattered(own, sent, last, after):
     move = moved if last else moved_back
-    total = own if last else move(own, 0).astype(F32)
-    for part, by in sent:
-        total = total + move(part, by).astype(F32)
-    return total.astype(BF16)
+    terms = [own if last else move(own, 0)] + [move(part, by) for part, by in sent]
+    return pl.pallas_call(
+        functools.partial(sum_kernel, len(terms)),
+        in_specs=[VMEM] * (len(terms) + len(after)),
+        out_specs=VMEM,
+        out_shape=pltpu.VMEM(own.shape, BF16),
+        compiler_params=pltpu.CompilerParams(vmem_limit_bytes=2 * MIB),
+        cost_estimate=SMALL,
+        name="sum",
+    )(*near(*terms, *after))
 
 
 def shards(grad_out, saved_inputs, routes, gate_weights, w_gate, w_up, w_down):
@@ -407,10 +438,12 @@
     )
     xs = gathered_near(first)
     gs = gathered_near(grad)
-    xs, passed = gathered_far(who, xs, first)
+    *back, done = turned(who, first, gate, up, down)
+    xs, passed = gathered_far(who, xs, done)
     metas = xs
-    *back, done = turned(who, passed if ringed else first, gate, up, down)
-    gs = [[g] for g in gathered_far(who, gs, done)[0]]
+    back[2], done = turned_into(back[2], passed if ringed else first, down)
+    gs, passed = gathered_far(who, gs, done)
+    gs = [[g] for g in gs]
     for step in range(steps):
         last = step + 1 == steps
         *factors, done = forward(step, who, tokens, xs, metas, back[0], back[1])
@@ -418,12 +451,14 @@
             gs = [list(block) for block in zip(*[gathered_far(who, g, done)[0] for g in gs])]
         beside = ()
         if not last:
-            following = held(saved_inputs[0], step + 1, gs[-2][0], done) if ringed else saved_inputs[0, step + 1]
+            following = held(saved_inputs[0], step + 1, passed) if ringed else saved_inputs[0, step + 1]
             xs = gathered_near(following)
             beside = xs[1::2] if ringed else ()
         halves = backward(gs, *factors, *back, F32 if last else BF16)
         sent = [joined_parts(who, parts, beside) for parts in halves]
-        grads = [scattered(parts[0], pairs, last) for parts, pairs in zip(halves, sent)]
+        grads = []
+        for parts, pairs in zip(halves, sent):
+            grads.append(scattered(parts[0], pairs, last, grads))
         if not last:
             xs, _ = gathered_far(who, xs, done)
             gs = [gathered_near(grad) for grad in grads]

time: 122 us -> 119 us (0.975)
  waiting for transfers between devices: 44.9 us -> 34.9 us
  Pallas kernels: 38.5 us -> 42.9 us
  starting transfers between devices: 37.6 us -> 40.2 us
    ppermute x14, waiting for transfers between devices: 22.8 us -> 12.7 us  [moved(): lax.ppermute(value, 'expert', [(i, (i + by) % count) for i in range(count)])]
    ppermute x6, waiting for transfers between devices: 4.54 us -> 9.05 us  [moved_back(): return lax.ppermute(value, ('section', 'expert'), pairs)]
    ppermute x9, waiting for transfers between devices: 17.6 us -> 13.2 us  [swapped(): lax.ppermute(value, 'expert', [(i, i ^ 1) for i in range(lax.axis_size('e...]
    pallas_call x1 -> x6, Pallas kernels: 12.6 us -> 16.9 us  [the longest x1 9.87 us: turned(): pl.pallas_call(functools.partial(turn_kernel, len(weights) - 1), grid=(lo...]
    ppermute x14, starting transfers between devices: 21.8 us -> 25.6 us  [moved(): lax.ppermute(value, 'expert', [(i, (i + by) % count) for i in range(count)])]
  transfers between devices with their start and end apart: 29 -> 29, of which waited for: 19 -> 16; matrix products, arithmetic and copies ran while one was open for 0% -> 0% of each run, Pallas kernels for 27% -> 32%
where the time goes in v4:
time: 119 us
  Pallas kernels  42.9 us (36%)
  starting transfers between devices  40.2 us (34%)
  waiting for transfers between devices  34.9 us (29%)
    ppermute x14, starting transfers between devices, moved(): lax.ppermute(value, 'expert', [(i, (i + by) % count) for i in range(count)])  25.6 us
    ppermute x9, waiting for transfers between devices, swapped(): lax.ppermute(value, 'expert', [(i, i ^ 1) for i in range(lax.axis_size('e...  13.2 us
    ppermute x14, waiting for transfers between devices, moved(): lax.ppermute(value, 'expert', [(i, (i + by) % count) for i in range(count)])  12.7 us
    pallas_call x2, Pallas kernels, forward(): pl.pallas_call(functools.partial(forward_kernel, sources, local, tokens,...  12.4 us
    pallas_call x1, Pallas kernels, turned(): pl.pallas_call(functools.partial(turn_kernel, len(weights) - 1), grid=(lo...  9.87 us
    ppermute x6, waiting for transfers between devices, moved_back(): return lax.ppermute(value, ('section', 'expert'), pairs)  9.05 us
    pallas_call x2, Pallas kernels, backward(): pl.pallas_call(functools.partial(backward_kernel, sources, pieces, slice(...  8.33 us
    ppermute x6, starting transfers between devices, moved_back(): return lax.ppermute(value, ('section', 'expert'), pairs)  7.63 us
  transfers between devices with their start and end apart: 29, of which 16 were waited for; matrix products, arithmetic and copies ran while one was open for 0% of the time, Pallas kernels for 32%

profile of v4, /device:TPU:0, one launch (start us, length us, event | category | flops | bytes accessed | tf_op | source)
XLA Modules:
  0.0 119.1 jit_solution(5792555520198741038)
XLA Ops:
  0.0 1.1 first.1
  1.1 3.1 %collective-permute-start.1 = (bf16[136,1024]{1,0:T(8,128)(2,1)S(1)}, bf16[136,1024]{1,0:T(8,128)(2,1)S(1)}, u32[]{:S(2)}, u32[]{:S(2)}) collective-permute-start(bf16[136,1024]{1,0:T(8,128)(2,1)S(1)} %get-tuple-element.52.refs_2_.refs_0_.refs_4_), channel_id=1, source_target_pairs={{0,1},{1,2},{2,3},{3,0},{4,5},{5,6},{6,7},{7,4},{8,9},{9,10},{10,1... | collective-permute-start | bytes 835592 | tf_op jit(solution)/shard_map/ppermute | solution.py:367
  4.2 2.1 %collective-permute-start.2 = (bf16[136,1024]{1,0:T(8,128)(2,1)S(1)}, bf16[136,1024]{1,0:T(8,128)(2,1)S(1)}, u32[]{:S(2)}, u32[]{:S(2)}) collective-permute-start(bf16[136,1024]{1,0:T(8,128)(2,1)S(1)} %get-tuple-element.52.refs_2_.refs_0_.refs_4_), channel_id=1, source_target_pairs={{0,3},{1,0},{2,1},{3,2},{4,7},{5,4},{6,5},{7,6},{8,11},{9,8},{10,9... | collective-permute-start | bytes 835592 | tf_op jit(solution)/shard_map/ppermute | solution.py:367
  6.3 3.8 %collective-permute-start.3 = (bf16[128,1024]{1,0:T(8,128)(2,1)S(1)}, bf16[128,1024]{1,0:T(8,128)(2,1)S(1)}, u32[]{:S(2)}, u32[]{:S(2)}) collective-permute-start(bf16[128,1024]{1,0:T(8,128)(2,1)S(1)} %get-tuple-element.51.refs_0_.kept_ref), channel_id=1, source_target_pairs={{0,3},{1,0},{2,1},{3,2},{4,7},{5,4},{6,5},{7,6},{8,11},{9,8},{10,9... | collective-permute-start | bytes 786440 | tf_op jit(solution)/shard_map/ppermute | solution.py:367
  10.1 9.9 %turn.1 = (bf16[8,512,1024]{2,1,0:T(8,128)(2,1)S(1)}, bf16[8,512,1024]{2,1,0:T(8,128)(2,1)S(1)}, bf16[8,1024,512]{2,1,0:T(8,128)(2,1)S(1)}, f32[8,128]{1,0:T(8,128)S(1)}) custom-call(s32[1]{0:T(128)} %bitcast.8.refs_0_.base_ref, s32[1]{0:T(128)} %bitcast.6.refs_1_.odd_ref, bf16[136,1024]{1,0:T(8,128)(2,1)S(1)} %get-tuple-element.52.refs_2_.refs_0_.refs_4_, ...), custom_call_target="tpu_custom_call" | custom-call | bytes 1024 | tf_op jit(solution)/shard_map/turn/pallas_call | solution.py:199
  20.0 0.4 collective-permute-start.5
  20.4 6.9 %turn_into.1 = (bf16[8,1024,512]{2,1,0:T(8,128)(2,1)S(1)}, f32[8,128]{1,0:T(8,128)S(1)}) custom-call(bf16[8,512,1024]{2,1,0:T(8,128)(2,1)} %bitcast.21, bf16[136,1024]{1,0:T(8,128)(2,1)S(1)} %choose.5.after_ref, bf16[8,1024,512]{2,1,0:T(8,128)(2,1)S(1)} %get-tuple-element.54.held_ref), custom_call_target="tpu_custom_call", output_to_operand_aliasing={{0}: (2, {})} | custom-call | bytes 1024 | tf_op jit(solution)/shard_map/turn_into/pallas_call | solution.py:212
  27.3 2.9 %collective-permute-done.3.right_ref.refs_3_ = bf16[128,1024]{1,0:T(8,128)(2,1)S(1)} collective-permute-done((bf16[128,1024]{1,0:T(8,128)(2,1)S(1)}, bf16[128,1024]{1,0:T(8,128)(2,1)S(1)}, u32[]{:S(2)}, u32[]{:S(2)}) %collective-permute-start.3) | collective-permute-done | bytes 262176 | tf_op jit(solution)/shard_map/ppermute | solution.py:367
  30.2 0.5 collective-permute-start.4
  30.8 1.7 %collective-permute-start.8 = (bf16[128,1024]{1,0:T(8,128)(2,1)S(1)}, bf16[128,1024]{1,0:T(8,128)(2,1)S(1)}, u32[]{:S(2)}, u32[]{:S(2)}) collective-permute-start(bf16[128,1024]{1,0:T(8,128)(2,1)S(1)} %hold.1.refs_0_), channel_id=1, source_target_pairs={{0,1},{1,2},{2,3},{3,0},{4,5},{5,6},{6,7},{7,4},{8,9},{9,10},{10,1... | collective-permute-start | bytes 786440 | tf_op jit(solution)/shard_map/ppermute | solution.py:367
  32.4 2.2 %collective-permute-start.9 = (bf16[128,1024]{1,0:T(8,128)(2,1)S(1)}, bf16[128,1024]{1,0:T(8,128)(2,1)S(1)}, u32[]{:S(2)}, u32[]{:S(2)}) collective-permute-start(bf16[128,1024]{1,0:T(8,128)(2,1)S(1)} %hold.1.refs_0_), channel_id=1, source_target_pairs={{0,3},{1,0},{2,1},{3,2},{4,7},{5,4},{6,5},{7,6},{8,11},{9,8},{10,9... | collective-permute-start | bytes 786440 | tf_op jit(solution)/shard_map/ppermute | solution.py:367
  34.6 1.6 %collective-permute-done.5.refs_2_.refs_6_ = bf16[136,1024]{1,0:T(8,128)(2,1)S(1)} collective-permute-done((bf16[136,1024]{1,0:T(8,128)(2,1)S(1)}, bf16[136,1024]{1,0:T(8,128)(2,1)S(1)}, u32[]{:S(2)}, u32[]{:S(2)}) %collective-permute-start.5) | collective-permute-done | bytes 278560 | tf_op jit(solution)/shard_map/ppermute | solution.py:371
  36.2 6.2 %forward.2 = (f32[8,160,512]{2,1,0:T(8,128)S(1)}, f32[8,160,512]{2,1,0:T(8,128)S(1)}, bf16[2,640,256]{2,1,0:T(8,128)(2,1)S(1)}, bf16[2,256,640]{2,1,0:T(8,128)(2,1)S(1)}, f32[8,128]{1,0:T(8,128)S(1)}) custom-call(s32[1]{0:T(128)} %bitcast.8.refs_0_.base_ref, bf16[136,1024]{1,0:T(8,128)(2,1)S(1)} %get-tuple-element.52.refs_2_.refs_0_.refs_4_, ...), custom_call_target="tpu_custom_call" | custom-call | bytes 1024 | tf_op jit(solution)/shard_map/forward/pallas_call | solution.py:311
  42.4 0.3 collective-permute-done.4.refs_2_
  42.6 4.1 %backward.2 = (bf16[128,512]{1,0:T(8,128)(2,1)S(1)}, bf16[128,512]{1,0:T(8,128)(2,1)S(1)}, bf16[128,512]{1,0:T(8,128)(2,1)S(1)}, bf16[128,512]{1,0:T(8,128)(2,1)...) custom-call(bf16[128,1024]{1,0:T(8,128)(2,1)S(1)} %get-tuple-element.51.refs_0_.kept_ref, ...), custom_call_target="tpu_custom_call" | custom-call | bytes 1024 | tf_op jit(solution)/shard_map/backward/pallas_call | solution.py:342
  46.8 0.6 collective-permute-start.7
  47.4 2.0 %rest.2 = (bf16[128,512]{1,0:T(8,128)(2,1)S(1)}, bf16[128,512]{1,0:T(8,128)(2,1)S(1)}, bf16[128,512]{1,0:T(8,128)(2,1)S(1)}, bf16[128,512]{1,0:T(8,128)(2,1)S(1)}) custom-call(bf16[128,1024]{1,0:T(8,128)(2,1)S(1)} %get-tuple-element.51.refs_0_.kept_ref, bf16[8,160,512]{2,1,0:T(8,128)(2,1)S(1)} %get-tuple-element.69.gate_grad_ref, ...), custom_call_target="tpu_custom_call" | custom-call | bytes 1024 | tf_op jit(solution)/shard_map/rest/pallas_call | solution.py:352
  49.3 1.6 %collective-permute-start.13 = (bf16[128,512]{1,0:T(8,128)(2,1)S(1)}, bf16[128,512]{1,0:T(8,128)(2,1)S(1)}, u32[]{:S(2)}, u32[]{:S(2)}) collective-permute-start(bf16[128,512]{1,0:T(8,128)(2,1)S(1)} %get-tuple-element.72), channel_id=1, source_target_pairs={{0,1},{1,0},{2,3},{3,2},{4,5},{5,4},{6,7},{7,6},{8,9},{9,8},{10,11... | collective-permute-start | bytes 393224 | tf_op jit(solution)/shard_map/ppermute | solution.py:371
  50.9 2.1 %collective-permute-done.9.refs_1_.right_ref.refs_3_ = bf16[128,1024]{1,0:T(8,128)(2,1)S(1)} collective-permute-done((bf16[128,1024]{1,0:T(8,128)(2,1)S(1)}, bf16[128,1024]{1,0:T(8,128)(2,1)S(1)}, u32[]{:S(2)}, u32[]{:S(2)}) %collective-permute-start.9) | collective-permute-done | bytes 262176 | tf_op jit(solution)/shard_map/ppermute | solution.py:367
  53.0 2.8 %collective-permute-done.7.far_ref = bf16[128,512]{1,0:T(8,128)(2,1)S(1)} collective-permute-done((bf16[128,512]{1,0:T(8,128)(2,1)S(1)}, bf16[128,512]{1,0:T(8,128)(2,1)S(1)}, u32[]{:S(2)}, u32[]{:S(2)}) %collective-permute-start.7) | collective-permute-done | bytes 131104 | tf_op jit(solution)/shard_map/ppermute | solution.py:371
  55.9 3.0 %collective-permute-start.10 = (bf16[128,512]{1,0:T(8,128)(2,1)S(1)}, bf16[128,512]{1,0:T(8,128)(2,1)S(1)}, u32[]{:S(2)}, u32[]{:S(2)}) collective-permute-start(bf16[128,512]{1,0:T(8,128)(2,1)S(1)} %get-tuple-element.67), channel_id=1, source_target_pairs={{0,31},{1,28},{2,29},{3,30},{4,3},{5,0},{6,1},{7,2},{8,7},{9,4},{1... | collective-permute-start | bytes 393224 | tf_op jit(solution)/shard_map/ppermute | solution.py:381
  58.9 1.0 collective-permute-start.12
  60.0 0.3 collective-permute-start.18
  60.2 1.0 collective-permute-start.11
  61.3 2.6 %collective-permute-start.14 = (bf16[128,512]{1,0:T(8,128)(2,1)S(1)}, bf16[128,512]{1,0:T(8,128)(2,1)S(1)}, u32[]{:S(2)}, u32[]{:S(2)}) collective-permute-start(bf16[128,512]{1,0:T(8,128)(2,1)S(1)} %get-tuple-element.75), channel_id=1, source_target_pairs={{0,31},{1,28},{2,29},{3,30},{4,3},{5,0},{6,1},{7,2},{8,7},{9,4},{1... | collective-permute-start | bytes 393224 | tf_op jit(solution)/shard_map/ppermute | solution.py:381
  63.9 7.4 %collective-permute-done.11.refs_2_ = bf16[128,512]{1,0:T(8,128)(2,1)S(1)} collective-permute-done((bf16[128,512]{1,0:T(8,128)(2,1)S(1)}, bf16[128,512]{1,0:T(8,128)(2,1)S(1)}, u32[]{:S(2)}, u32[]{:S(2)}) %collective-permute-start.11) | collective-permute-done | bytes 131104 | tf_op jit(solution)/shard_map/ppermute | solution.py:381
  71.4 3.8 %collective-permute-start.19 = (bf16[128,512]{1,0:T(8,128)(2,1)S(1)}, bf16[128,512]{1,0:T(8,128)(2,1)S(1)}, u32[]{:S(2)}, u32[]{:S(2)}) collective-permute-start(bf16[128,512]{1,0:T(8,128)(2,1)S(1)} %sum.4.refs_3_.refs_0_), channel_id=1, source_target_pairs={{0,3},{1,0},{2,1},{3,2},{4,7},{5,4},{6,5},{7,6},{8,11},{9,8},{10,9... | collective-permute-start | bytes 393224 | tf_op jit(solution)/shard_map/ppermute | solution.py:367
  75.2 1.7 %collective-permute-done.15.refs_2_ = bf16[128,512]{1,0:T(8,128)(2,1)S(1)} collective-permute-done((bf16[128,512]{1,0:T(8,128)(2,1)S(1)}, bf16[128,512]{1,0:T(8,128)(2,1)S(1)}, u32[]{:S(2)}, u32[]{:S(2)}) %collective-permute-start.15) | collective-permute-done | bytes 131104 | tf_op jit(solution)/shard_map/ppermute | solution.py:381
  77.0 3.8 %collective-permute-start.21 = (bf16[128,512]{1,0:T(8,128)(2,1)S(1)}, bf16[128,512]{1,0:T(8,128)(2,1)S(1)}, u32[]{:S(2)}, u32[]{:S(2)}) collective-permute-start(bf16[128,512]{1,0:T(8,128)(2,1)S(1)} %sum.5.refs_1_.kept_ref), channel_id=1, source_target_pairs={{0,3},{1,0},{2,1},{3,2},{4,7},{5,4},{6,5},{7,6},{8,11},{9,8},{10,9... | collective-permute-start | bytes 393224 | tf_op jit(solution)/shard_map/ppermute | solution.py:367
  80.8 6.2 %forward.3 = (f32[8,160,512]{2,1,0:T(8,128)S(1)}, f32[8,160,512]{2,1,0:T(8,128)S(1)}, bf16[2,640,256]{2,1,0:T(8,128)(2,1)S(1)}, bf16[2,256,640]{2,1,0:T(8,128)(2,1)S(1)}, f32[8,128]{1,0:T(8,128)S(1)}) custom-call(s32[1]{0:T(128)} %bitcast.8.refs_0_.base_ref, bf16[128,1024]{1,0:T(8,128)(2,1)S(1)} %hold.1.refs_0_, ...), custom_call_target="tpu_custom_call" | custom-call | bytes 1024 | tf_op jit(solution)/shard_map/forward/pallas_call | solution.py:311
  87.1 0.6 collective-permute-done.21.right_ref.refs_7_
  87.8 1.4 %collective-permute-start.22 = (bf16[128,512]{1,0:T(8,128)(2,1)S(1)}, bf16[128,512]{1,0:T(8,128)(2,1)S(1)}, u32[]{:S(2)}, u32[]{:S(2)}) collective-permute-start(bf16[128,512]{1,0:T(8,128)(2,1)S(1)} %choose.9), channel_id=1, source_target_pairs={{0,1},{1,0},{2,3},{3,2},{4,5},{5,4},{6,7},{7,6},{8,9},{9,8},{10,11... | collective-permute-start | bytes 393224 | tf_op jit(solution)/shard_map/ppermute | solution.py:371
  89.2 4.0 %collective-permute-done.20.refs_4_ = bf16[128,512]{1,0:T(8,128)(2,1)S(1)} collective-permute-done((bf16[128,512]{1,0:T(8,128)(2,1)S(1)}, bf16[128,512]{1,0:T(8,128)(2,1)S(1)}, u32[]{:S(2)}, u32[]{:S(2)}) %collective-permute-start.20) | collective-permute-done | bytes 131104 | tf_op jit(solution)/shard_map/ppermute | solution.py:371
  93.3 1.4 %collective-permute-done.22.refs_5_ = bf16[128,512]{1,0:T(8,128)(2,1)S(1)} collective-permute-done((bf16[128,512]{1,0:T(8,128)(2,1)S(1)}, bf16[128,512]{1,0:T(8,128)(2,1)S(1)}, u32[]{:S(2)}, u32[]{:S(2)}) %collective-permute-start.22) | collective-permute-done | bytes 131104 | tf_op jit(solution)/shard_map/ppermute | solution.py:371
  94.7 4.2 %backward.3 = (f32[128,512]{1,0:T(8,128)S(1)}, bf16[128,512]{1,0:T(8,128)(2,1)S(1)}, bf16[128,512]{1,0:T(8,128)(2,1)S(1)}, bf16[128,512]{1,0:T(8,128)(2,1)S(1)},...) custom-call(bf16[128,512]{1,0:T(8,128)(2,1)S(1)} %sum.4.refs_3_.refs_0_, ...), custom_call_target="tpu_custom_call" | custom-call | bytes 1024 | tf_op jit(solution)/shard_map/backward/pallas_call | solution.py:342
  98.9 0.3 collective-permute-start.23
  99.2 2.0 %rest.3 = (f32[128,512]{1,0:T(8,128)S(1)}, bf16[128,512]{1,0:T(8,128)(2,1)S(1)}, bf16[128,512]{1,0:T(8,128)(2,1)S(1)}, bf16[128,512]{1,0:T(8,128)(2,1)S(1)}) custom-call(bf16[128,512]{1,0:T(8,128)(2,1)S(1)} %sum.5.refs_1_.kept_ref, bf16[8,160,512]{2,1,0:T(8,128)(2,1)S(1)} %get-tuple-element.89.gate_grad_ref, ...), custom_call_target="tpu_custom_call" | custom-call | bytes 1024 | tf_op jit(solution)/shard_map/rest/pallas_call | solution.py:352
  101.1 1.9 %collective-permute-start.26 = (bf16[128,512]{1,0:T(8,128)(2,1)S(1)}, bf16[128,512]{1,0:T(8,128)(2,1)S(1)}, u32[]{:S(2)}, u32[]{:S(2)}) collective-permute-start(bf16[128,512]{1,0:T(8,128)(2,1)S(1)} %get-tuple-element.92), channel_id=1, source_target_pairs={{0,1},{1,0},{2,3},{3,2},{4,5},{5,4},{6,7},{7,6},{8,9},{9,8},{10,11... | collective-permute-start | bytes 393224 | tf_op jit(solution)/shard_map/ppermute | solution.py:371
  103.0 2.3 %collective-permute-done.23.far_ref = bf16[128,512]{1,0:T(8,128)(2,1)S(1)} collective-permute-done((bf16[128,512]{1,0:T(8,128)(2,1)S(1)}, bf16[128,512]{1,0:T(8,128)(2,1)S(1)}, u32[]{:S(2)}, u32[]{:S(2)}) %collective-permute-start.23) | collective-permute-done | bytes 131104 | tf_op jit(solution)/shard_map/ppermute | solution.py:371
  105.4 1.7 %collective-permute-start.24 = (bf16[128,512]{1,0:T(8,128)(2,1)S(1)}, bf16[128,512]{1,0:T(8,128)(2,1)S(1)}, u32[]{:S(2)}, u32[]{:S(2)}) collective-permute-start(bf16[128,512]{1,0:T(8,128)(2,1)S(1)} %get-tuple-element.87), channel_id=1, source_target_pairs={{0,3},{1,0},{2,1},{3,2},{4,7},{5,4},{6,5},{7,6},{8,11},{9,8},{10,9... | collective-permute-start | bytes 393224 | tf_op jit(solution)/shard_map/ppermute | solution.py:367
  107.1 0.4 collective-permute-start.25
  107.5 0.8 collective-permute-done.26.far_ref
  108.3 3.0 %collective-permute-start.27 = (bf16[128,512]{1,0:T(8,128)(2,1)S(1)}, bf16[128,512]{1,0:T(8,128)(2,1)S(1)}, u32[]{:S(2)}, u32[]{:S(2)}) collective-permute-start(bf16[128,512]{1,0:T(8,128)(2,1)S(1)} %get-tuple-element.95), channel_id=1, source_target_pairs={{0,3},{1,0},{2,1},{3,2},{4,7},{5,4},{6,5},{7,6},{8,11},{9,8},{10,9... | collective-permute-start | bytes 393224 | tf_op jit(solution)/shard_map/ppermute | solution.py:367
  111.3 1.0 collective-permute-done.24.refs_1_
  112.3 3.1 %collective-permute-done.25.refs_2_ = bf16[128,512]{1,0:T(8,128)(2,1)S(1)} collective-permute-done((bf16[128,512]{1,0:T(8,128)(2,1)S(1)}, bf16[128,512]{1,0:T(8,128)(2,1)S(1)}, u32[]{:S(2)}, u32[]{:S(2)}) %collective-permute-start.25) | collective-permute-done | bytes 131104 | tf_op jit(solution)/shard_map/ppermute | solution.py:367
  115.5 1.0 collective-permute-done.27.refs_1_
  116.5 1.8 %collective-permute-done.28.refs_2_ = bf16[128,512]{1,0:T(8,128)(2,1)S(1)} collective-permute-done((bf16[128,512]{1,0:T(8,128)(2,1)S(1)}, bf16[128,512]{1,0:T(8,128)(2,1)S(1)}, u32[]{:S(2)}, u32[]{:S(2)}) %collective-permute-start.28) | collective-permute-done | bytes 131104 | tf_op jit(solution)/shard_map/ppermute | solution.py:367
  118.4 0.7 maximum_bitcast_fusion
  (43 shorter events, 0.7 us)
Async XLA Ops:
  1.1 18.9 %collective-permute-start.1 = (bf16[136,1024]{1,0:T(8,128)(2,1)S(1)}, bf16[136,1024]{1,0:T(8,128)(2,1)S(1)}, u32[]{:S(2)}, u32[]{:S(2)}) collective-permute-start(bf16[136,1024]{1,0:T(8,128)(2,1)S(1)} %get-tuple-element.52.refs_2_.refs_0_.refs_4_), channel_id=1, source_target_pairs={{0,1},{1,2},{2,3},{3,0},{4,5},{5,6},{6,7},{7,4},{8,9},{9,10},{10,1... | collective-permute-start | bytes 835592 | tf_op jit(solution)/shard_map/ppermute | solution.py:367
  4.2 15.8 %collective-permute-start.2 = (bf16[136,1024]{1,0:T(8,128)(2,1)S(1)}, bf16[136,1024]{1,0:T(8,128)(2,1)S(1)}, u32[]{:S(2)}, u32[]{:S(2)}) collective-permute-start(bf16[136,1024]{1,0:T(8,128)(2,1)S(1)} %get-tuple-element.52.refs_2_.refs_0_.refs_4_), channel_id=1, source_target_pairs={{0,3},{1,0},{2,1},{3,2},{4,7},{5,4},{6,5},{7,6},{8,11},{9,8},{10,9... | collective-permute-start | bytes 835592 | tf_op jit(solution)/shard_map/ppermute | solution.py:367
  6.3 21.0 %collective-permute-start = (bf16[128,1024]{1,0:T(8,128)(2,1)S(1)}, bf16[128,1024]{1,0:T(8,128)(2,1)S(1)}, u32[]{:S(2)}, u32[]{:S(2)}) collective-permute-start(bf16[128,1024]{1,0:T(8,128)(2,1)S(1)} %get-tuple-element.51.refs_0_.kept_ref), channel_id=1, source_target_pairs={{0,1},{1,2},{2,3},{3,0},{4,5},{5,6},{6,7},{7,4},{8,9},{9,10},{10,1... | collective-permute-start | bytes 786440 | tf_op jit(solution)/shard_map/ppermute | solution.py:367
  6.3 23.9 %collective-permute-start.3 = (bf16[128,1024]{1,0:T(8,128)(2,1)S(1)}, bf16[128,1024]{1,0:T(8,128)(2,1)S(1)}, u32[]{:S(2)}, u32[]{:S(2)}) collective-permute-start(bf16[128,1024]{1,0:T(8,128)(2,1)S(1)} %get-tuple-element.51.refs_0_.kept_ref), channel_id=1, source_target_pairs={{0,3},{1,0},{2,1},{3,2},{4,7},{5,4},{6,5},{7,6},{8,11},{9,8},{10,9... | collective-permute-start | bytes 786440 | tf_op jit(solution)/shard_map/ppermute | solution.py:367
  20.0 16.2 %collective-permute-start.5 = (bf16[136,1024]{1,0:T(8,128)(2,1)S(1)}, bf16[136,1024]{1,0:T(8,128)(2,1)S(1)}, u32[]{:S(2)}, u32[]{:S(2)}) collective-permute-start(bf16[136,1024]{1,0:T(8,128)(2,1)S(1)} %choose.5.after_ref), channel_id=1, source_target_pairs={{0,1},{1,0},{2,3},{3,2},{4,5},{5,4},{6,7},{7,6},{8,9},{9,8},{10,11... | collective-permute-start | bytes 835592 | tf_op jit(solution)/shard_map/ppermute | solution.py:371
  20.4 10.3 %copy-start.1 = (bf16[1,2,128,1024]{3,2,1,0:T(8,128)(2,1)S(1)}, bf16[1,2,128,1024]{3,2,1,0:T(8,128)(2,1)}, u32[]{:S(2)}) copy-start(bf16[1,2,128,1024]{3,2,1,0:T(8,128)(2,1)} %param.8) | copy-start | bytes 1572868
  27.3 15.4 %copy-start = (bf16[8,1024,512]{2,1,0:T(8,128)(2,1)}, bf16[8,1024,512]{2,1,0:T(8,128)(2,1)S(1)}, u32[]{:S(2)}) copy-start(bf16[8,1024,512]{2,1,0:T(8,128)(2,1)S(1)} %get-tuple-element.62.refs_10_.refs_14_) | copy-start | bytes 25165828
  30.2 12.4 %collective-permute-start.4 = (bf16[128,1024]{1,0:T(8,128)(2,1)S(1)}, bf16[128,1024]{1,0:T(8,128)(2,1)S(1)}, u32[]{:S(2)}, u32[]{:S(2)}) collective-permute-start(bf16[128,1024]{1,0:T(8,128)(2,1)S(1)} %choose.6.refs_0_), channel_id=1, source_target_pairs={{0,1},{1,0},{2,3},{3,2},{4,5},{5,4},{6,7},{7,6},{8,9},{9,8},{10,11... | collective-permute-start | bytes 786440 | tf_op jit(solution)/shard_map/ppermute | solution.py:371
  30.8 20.2 %collective-permute-start.8 = (bf16[128,1024]{1,0:T(8,128)(2,1)S(1)}, bf16[128,1024]{1,0:T(8,128)(2,1)S(1)}, u32[]{:S(2)}, u32[]{:S(2)}) collective-permute-start(bf16[128,1024]{1,0:T(8,128)(2,1)S(1)} %hold.1.refs_0_), channel_id=1, source_target_pairs={{0,1},{1,2},{2,3},{3,0},{4,5},{5,6},{6,7},{7,4},{8,9},{9,10},{10,1... | collective-permute-start | bytes 786440 | tf_op jit(solution)/shard_map/ppermute | solution.py:367
  32.4 20.6 %collective-permute-start.9 = (bf16[128,1024]{1,0:T(8,128)(2,1)S(1)}, bf16[128,1024]{1,0:T(8,128)(2,1)S(1)}, u32[]{:S(2)}, u32[]{:S(2)}) collective-permute-start(bf16[128,1024]{1,0:T(8,128)(2,1)S(1)} %hold.1.refs_0_), channel_id=1, source_target_pairs={{0,3},{1,0},{2,1},{3,2},{4,7},{5,4},{6,5},{7,6},{8,11},{9,8},{10,9... | collective-permute-start | bytes 786440 | tf_op jit(solution)/shard_map/ppermute | solution.py:367
  46.8 9.1 %collective-permute-start.7 = (bf16[128,512]{1,0:T(8,128)(2,1)S(1)}, bf16[128,512]{1,0:T(8,128)(2,1)S(1)}, u32[]{:S(2)}, u32[]{:S(2)}) collective-permute-start(bf16[128,512]{1,0:T(8,128)(2,1)S(1)} %get-tuple-element.64), channel_id=1, source_target_pairs={{0,1},{1,0},{2,3},{3,2},{4,5},{5,4},{6,7},{7,6},{8,9},{9,8},{10,11... | collective-permute-start | bytes 393224 | tf_op jit(solution)/shard_map/ppermute | solution.py:371
  49.3 10.9 %collective-permute-start.13 = (bf16[128,512]{1,0:T(8,128)(2,1)S(1)}, bf16[128,512]{1,0:T(8,128)(2,1)S(1)}, u32[]{:S(2)}, u32[]{:S(2)}) collective-permute-start(bf16[128,512]{1,0:T(8,128)(2,1)S(1)} %get-tuple-element.72), channel_id=1, source_target_pairs={{0,1},{1,0},{2,3},{3,2},{4,5},{5,4},{6,7},{7,6},{8,9},{9,8},{10,11... | collective-permute-start | bytes 393224 | tf_op jit(solution)/shard_map/ppermute | solution.py:371
  50.9 10.3 %collective-permute-start.6 = (bf16[128,512]{1,0:T(8,128)(2,1)S(1)}, bf16[128,512]{1,0:T(8,128)(2,1)S(1)}, u32[]{:S(2)}, u32[]{:S(2)}) collective-permute-start(bf16[128,512]{1,0:T(8,128)(2,1)S(1)} %get-tuple-element.63), channel_id=1, source_target_pairs={{0,28},{1,29},{2,30},{3,31},{4,0},{5,1},{6,2},{7,3},{8,4},{9,5},{1... | collective-permute-start | bytes 393224 | tf_op jit(solution)/shard_map/ppermute | solution.py:381
  55.9 8.0 %collective-permute-start.10 = (bf16[128,512]{1,0:T(8,128)(2,1)S(1)}, bf16[128,512]{1,0:T(8,128)(2,1)S(1)}, u32[]{:S(2)}, u32[]{:S(2)}) collective-permute-start(bf16[128,512]{1,0:T(8,128)(2,1)S(1)} %get-tuple-element.67), channel_id=1, source_target_pairs={{0,31},{1,28},{2,29},{3,30},{4,3},{5,0},{6,1},{7,2},{8,7},{9,4},{1... | collective-permute-start | bytes 393224 | tf_op jit(solution)/shard_map/ppermute | solution.py:381
  58.9 12.4 %collective-permute-start.12 = (bf16[128,512]{1,0:T(8,128)(2,1)S(1)}, bf16[128,512]{1,0:T(8,128)(2,1)S(1)}, u32[]{:S(2)}, u32[]{:S(2)}) collective-permute-start(bf16[128,512]{1,0:T(8,128)(2,1)S(1)} %get-tuple-element.71), channel_id=1, source_target_pairs={{0,28},{1,29},{2,30},{3,31},{4,0},{5,1},{6,2},{7,3},{8,4},{9,5},{1... | collective-permute-start | bytes 393224 | tf_op jit(solution)/shard_map/ppermute | solution.py:381
  60.0 20.8 %collective-permute-start.18 = (bf16[128,1024]{1,0:T(8,128)(2,1)S(1)}, bf16[128,1024]{1,0:T(8,128)(2,1)S(1)}, u32[]{:S(2)}, u32[]{:S(2)}) collective-permute-start(bf16[128,1024]{1,0:T(8,128)(2,1)S(1)} %choose.7), channel_id=1, source_target_pairs={{0,1},{1,0},{2,3},{3,2},{4,5},{5,4},{6,7},{7,6},{8,9},{9,8},{10,11... | collective-permute-start | bytes 786440 | tf_op jit(solution)/shard_map/ppermute | solution.py:371
  60.2 11.0 %collective-permute-start.11 = (bf16[128,512]{1,0:T(8,128)(2,1)S(1)}, bf16[128,512]{1,0:T(8,128)(2,1)S(1)}, u32[]{:S(2)}, u32[]{:S(2)}) collective-permute-start(bf16[128,512]{1,0:T(8,128)(2,1)S(1)} %get-tuple-element.68), channel_id=1, source_target_pairs={{0,29},{1,30},{2,31},{3,28},{4,1},{5,2},{6,3},{7,0},{8,5},{9,6},{1... | collective-permute-start | bytes 393224 | tf_op jit(solution)/shard_map/ppermute | solution.py:381
  61.3 13.9 %collective-permute-start.14 = (bf16[128,512]{1,0:T(8,128)(2,1)S(1)}, bf16[128,512]{1,0:T(8,128)(2,1)S(1)}, u32[]{:S(2)}, u32[]{:S(2)}) collective-permute-start(bf16[128,512]{1,0:T(8,128)(2,1)S(1)} %get-tuple-element.75), channel_id=1, source_target_pairs={{0,31},{1,28},{2,29},{3,30},{4,3},{5,0},{6,1},{7,2},{8,7},{9,4},{1... | collective-permute-start | bytes 393224 | tf_op jit(solution)/shard_map/ppermute | solution.py:381
  63.9 13.0 %collective-permute-start.15 = (bf16[128,512]{1,0:T(8,128)(2,1)S(1)}, bf16[128,512]{1,0:T(8,128)(2,1)S(1)}, u32[]{:S(2)}, u32[]{:S(2)}) collective-permute-start(bf16[128,512]{1,0:T(8,128)(2,1)S(1)} %get-tuple-element.76), channel_id=1, source_target_pairs={{0,29},{1,30},{2,31},{3,28},{4,1},{5,2},{6,3},{7,0},{8,5},{9,6},{1... | collective-permute-start | bytes 393224 | tf_op jit(solution)/shard_map/ppermute | solution.py:381
  71.3 15.7 %collective-permute-start.16 = (bf16[128,512]{1,0:T(8,128)(2,1)S(1)}, bf16[128,512]{1,0:T(8,128)(2,1)S(1)}, u32[]{:S(2)}, u32[]{:S(2)}) collective-permute-start(bf16[128,512]{1,0:T(8,128)(2,1)S(1)} %sum.4.refs_3_.refs_0_), channel_id=1, source_target_pairs={{0,1},{1,2},{2,3},{3,0},{4,5},{5,6},{6,7},{7,4},{8,9},{9,10},{10,1... | collective-permute-start | bytes 393224 | tf_op jit(solution)/shard_map/ppermute | solution.py:367
  71.4 15.6 %collective-permute-start.19 = (bf16[128,512]{1,0:T(8,128)(2,1)S(1)}, bf16[128,512]{1,0:T(8,128)(2,1)S(1)}, u32[]{:S(2)}, u32[]{:S(2)}) collective-permute-start(bf16[128,512]{1,0:T(8,128)(2,1)S(1)} %sum.4.refs_3_.refs_0_), channel_id=1, source_target_pairs={{0,3},{1,0},{2,1},{3,2},{4,7},{5,4},{6,5},{7,6},{8,11},{9,8},{10,9... | collective-permute-start | bytes 393224 | tf_op jit(solution)/shard_map/ppermute | solution.py:367
  76.9 17.8 %slice-start = ((s8[8388608]{0:T(1024)(128)(4,1)}), s8[4194304]{0:T(1024)(128)(4,1)S(1)}, s32[]{:S(2)}) async-start(s8[8388608]{0:T(1024)(128)(4,1)} %bitcast.15), calls=%async_computation | async-start | bytes 8388608
  76.9 17.8 %slice-start.1 = ((s8[8388608]{0:T(1024)(128)(4,1)}), s8[4194304]{0:T(1024)(128)(4,1)S(1)}, s32[]{:S(2)}) async-start(s8[8388608]{0:T(1024)(128)(4,1)} %bitcast.15), calls=%async_computation.1 | async-start | bytes 8388608
  76.9 10.2 %collective-permute-start.17 = (bf16[128,512]{1,0:T(8,128)(2,1)S(1)}, bf16[128,512]{1,0:T(8,128)(2,1)S(1)}, u32[]{:S(2)}, u32[]{:S(2)}) collective-permute-start(bf16[128,512]{1,0:T(8,128)(2,1)S(1)} %sum.5.refs_1_.kept_ref), channel_id=1, source_target_pairs={{0,1},{1,2},{2,3},{3,0},{4,5},{5,6},{6,7},{7,4},{8,9},{9,10},{10,1... | collective-permute-start | bytes 393224 | tf_op jit(solution)/shard_map/ppermute | solution.py:367
  77.0 10.8 %collective-permute-start.21 = (bf16[128,512]{1,0:T(8,128)(2,1)S(1)}, bf16[128,512]{1,0:T(8,128)(2,1)S(1)}, u32[]{:S(2)}, u32[]{:S(2)}) collective-permute-start(bf16[128,512]{1,0:T(8,128)(2,1)S(1)} %sum.5.refs_1_.kept_ref), channel_id=1, source_target_pairs={{0,3},{1,0},{2,1},{3,2},{4,7},{5,4},{6,5},{7,6},{8,11},{9,8},{10,9... | collective-permute-start | bytes 393224 | tf_op jit(solution)/shard_map/ppermute | solution.py:367
  87.0 6.2 %collective-permute-start.20 = (bf16[128,512]{1,0:T(8,128)(2,1)S(1)}, bf16[128,512]{1,0:T(8,128)(2,1)S(1)}, u32[]{:S(2)}, u32[]{:S(2)}) collective-permute-start(bf16[128,512]{1,0:T(8,128)(2,1)S(1)} %choose.8), channel_id=1, source_target_pairs={{0,1},{1,0},{2,3},{3,2},{4,5},{5,4},{6,7},{7,6},{8,9},{9,8},{10,11... | collective-permute-start | bytes 393224 | tf_op jit(solution)/shard_map/ppermute | solution.py:371
  87.8 6.9 %collective-permute-start.22 = (bf16[128,512]{1,0:T(8,128)(2,1)S(1)}, bf16[128,512]{1,0:T(8,128)(2,1)S(1)}, u32[]{:S(2)}, u32[]{:S(2)}) collective-permute-start(bf16[128,512]{1,0:T(8,128)(2,1)S(1)} %choose.9), channel_id=1, source_target_pairs={{0,1},{1,0},{2,3},{3,2},{4,5},{5,4},{6,7},{7,6},{8,9},{9,8},{10,11... | collective-permute-start | bytes 393224 | tf_op jit(solution)/shard_map/ppermute | solution.py:371
  98.9 6.4 %collective-permute-start.23 = (bf16[128,512]{1,0:T(8,128)(2,1)S(1)}, bf16[128,512]{1,0:T(8,128)(2,1)S(1)}, u32[]{:S(2)}, u32[]{:S(2)}) collective-permute-start(bf16[128,512]{1,0:T(8,128)(2,1)S(1)} %get-tuple-element.84), channel_id=1, source_target_pairs={{0,1},{1,0},{2,3},{3,2},{4,5},{5,4},{6,7},{7,6},{8,9},{9,8},{10,11... | collective-permute-start | bytes 393224 | tf_op jit(solution)/shard_map/ppermute | solution.py:371
  101.1 7.2 %collective-permute-start.26 = (bf16[128,512]{1,0:T(8,128)(2,1)S(1)}, bf16[128,512]{1,0:T(8,128)(2,1)S(1)}, u32[]{:S(2)}, u32[]{:S(2)}) collective-permute-start(bf16[128,512]{1,0:T(8,128)(2,1)S(1)} %get-tuple-element.92), channel_id=1, source_target_pairs={{0,1},{1,0},{2,3},{3,2},{4,5},{5,4},{6,7},{7,6},{8,9},{9,8},{10,11... | collective-permute-start | bytes 393224 | tf_op jit(solution)/shard_map/ppermute | solution.py:371
  105.4 6.9 %collective-permute-start.24 = (bf16[128,512]{1,0:T(8,128)(2,1)S(1)}, bf16[128,512]{1,0:T(8,128)(2,1)S(1)}, u32[]{:S(2)}, u32[]{:S(2)}) collective-permute-start(bf16[128,512]{1,0:T(8,128)(2,1)S(1)} %get-tuple-element.87), channel_id=1, source_target_pairs={{0,3},{1,0},{2,1},{3,2},{4,7},{5,4},{6,5},{7,6},{8,11},{9,8},{10,9... | collective-permute-start | bytes 393224 | tf_op jit(solution)/shard_map/ppermute | solution.py:367
  107.1 8.4 %collective-permute-start.25 = (bf16[128,512]{1,0:T(8,128)(2,1)S(1)}, bf16[128,512]{1,0:T(8,128)(2,1)S(1)}, u32[]{:S(2)}, u32[]{:S(2)}) collective-permute-start(bf16[128,512]{1,0:T(8,128)(2,1)S(1)} %get-tuple-element.88), channel_id=1, source_target_pairs={{0,1},{1,2},{2,3},{3,0},{4,5},{5,6},{6,7},{7,4},{8,9},{9,10},{10,1... | collective-permute-start | bytes 393224 | tf_op jit(solution)/shard_map/ppermute | solution.py:367
  108.3 8.2 %collective-permute-start.27 = (bf16[128,512]{1,0:T(8,128)(2,1)S(1)}, bf16[128,512]{1,0:T(8,128)(2,1)S(1)}, u32[]{:S(2)}, u32[]{:S(2)}) collective-permute-start(bf16[128,512]{1,0:T(8,128)(2,1)S(1)} %get-tuple-element.95), channel_id=1, source_target_pairs={{0,3},{1,0},{2,1},{3,2},{4,7},{5,4},{6,5},{7,6},{8,11},{9,8},{10,9... | collective-permute-start | bytes 393224 | tf_op jit(solution)/shard_map/ppermute | solution.py:367
  111.3 7.0 %collective-permute-start.28 = (bf16[128,512]{1,0:T(8,128)(2,1)S(1)}, bf16[128,512]{1,0:T(8,128)(2,1)S(1)}, u32[]{:S(2)}, u32[]{:S(2)}) collective-permute-start(bf16[128,512]{1,0:T(8,128)(2,1)S(1)} %get-tuple-element.96), channel_id=1, source_target_pairs={{0,1},{1,2},{2,3},{3,0},{4,5},{5,6},{6,7},{7,4},{8,9},{9,10},{10,1... | collective-permute-start | bytes 393224 | tf_op jit(solution)/shard_map/ppermute | solution.py:367

commit v5 on v4

--- a/solution.py
+++ b/solution.py
@@ -9,6 +9,7 @@
 
 MOST = 40
 PAIR = 2 * MOST
+CUTS = (512, 512)
 F32 = jnp.float32
 BF16 = jnp.bfloat16
 
@@ -83,8 +84,9 @@
     for pair in range(len(source_refs) // 2):
         source = jnp.concatenate([ref[:tokens] for ref in source_refs[2 * pair : 2 * pair + 2]], axis=0)
         for n in range(0, width, 256):
-            rows = dot(pick_ref[pair], source[:, n : n + 256], ((1,), (0,))).astype(BF16)
-            rows_ref[:, pair * PAIR : (pair + 1) * PAIR, n : n + 256] = rows.reshape(local, PAIR, 256)
+            stop = min(n + 256, width)
+            rows = dot(pick_ref[pair], source[:, n:stop], ((1,), (0,))).astype(BF16)
+            rows_ref[:, pair * PAIR : (pair + 1) * PAIR, n:stop] = rows.reshape(local, PAIR, stop - n)
 
 
 def pick_pieces(sources, pieces, piece_refs, pick_ref, rows_ref):
@@ -96,7 +98,17 @@
         start += width
 
 
-def row_piece(kept_ref, gate_grad_ref, up_grad_ref, place_ref, gate_ref, up_ref, out_refs, back_ref, columns):
+def columns_of(refs, start, stop):
+    parts, first = [], 0
+    for ref in refs:
+        last = first + ref.shape[1]
+        if first < stop and start < last:
+            parts.append(ref[:, max(start - first, 0) : min(stop, last) - first])
+        first = last
+    return jnp.concatenate(parts, axis=1)
+
+
+def row_piece(kept_refs, gate_grad_ref, up_grad_ref, place_ref, gate_ref, up_ref, out_refs, back_ref, columns):
     local = gate_ref.shape[0]
     pairs, double = place_ref.shape[0], place_ref.shape[1]
     tokens = double // 2
@@ -108,15 +120,15 @@
     width = columns.stop - columns.start
     for pair in range(pairs):
         for n in range(0, width, 256):
-            rows = back_ref[pair, :, :, n : n + 256].reshape(local * PAIR, 256)
+            stop = min(n + 256, width)
+            rows = back_ref[pair, :, :, n:stop].reshape(local * PAIR, stop - n)
             total = dot(place_ref[pair], rows, ((1,), (0,)))
             for half in range(2):
                 out = out_refs[2 * pair + half]
                 part = total[half * tokens : (half + 1) * tokens]
                 if pair == 0 and half == 0:
-                    first = columns.start if kept_ref.shape[1] > width else 0
-                    part = part + kept_ref[:, first + n : first + n + 256].astype(F32)
-                out[:, n : n + 256] = part.astype(out.dtype)
+                    part = part + columns_of(kept_refs, columns.start + n, columns.start + stop).astype(F32)
+                out[:, n:stop] = part.astype(out.dtype)
 
 
 def backward_kernel(sources, pieces, columns, *refs):
@@ -129,12 +141,14 @@
         hidden = dot(rows_ref[e], down_ref[e], ((1,), (0,)))
         gate_grad_ref[e] = (hidden * a_ref[e]).astype(BF16)
         up_grad_ref[e] = (hidden * b_ref[e]).astype(BF16)
-    row_piece(g_refs[0], gate_grad_ref, up_grad_ref, place_ref, gate_ref, up_ref, out_refs, back_ref, columns)
-
-
-def rest_kernel(sources, columns, kept_ref, gate_grad_ref, up_grad_ref, place_ref, gate_ref, up_ref, *refs):
+    row_piece(g_refs[:pieces], gate_grad_ref, up_grad_ref, place_ref, gate_ref, up_ref, out_refs, back_ref, columns)
+
+
+def rest_kernel(sources, pieces, columns, *refs):
+    kept_refs, refs = refs[:pieces], refs[pieces:]
+    gate_grad_ref, up_grad_ref, place_ref, gate_ref, up_ref, *refs = refs
     row_piece(
-        kept_ref, gate_grad_ref, up_grad_ref, place_ref, gate_ref, up_ref, refs[:sources], refs[sources], columns
+        kept_refs, gate_grad_ref, up_grad_ref, place_ref, gate_ref, up_ref, refs[:sources], refs[sources], columns
     )
 
 
@@ -329,36 +343,35 @@
     )(who[0], *near(*arrays))
 
 
-def backward(gs, a, b, pick, place, gate, up, down, kept_type):
+def backward(cut, kept_type, gs, a, b, pick, place, gate, up, down):
     sources, pieces, local = len(gs), len(gs[0]), gate.shape[0]
     tokens = gs[0][0].shape[0]
     hidden, width = gate.shape[1:]
     rows = sources * MOST
-    half = width // 2
     types = [kept_type] + [BF16] * (sources - 1)
-    outs = tuple(pltpu.VMEM((tokens, half), t) for t in types)
+    outs = [tuple(pltpu.VMEM((tokens, w), t) for t in types) for w in (cut, width - cut)]
     factor = pltpu.VMEM((local, rows, hidden), BF16)
-    back = pltpu.VMEM((sources // 2, local, PAIR, half), BF16)
+    backs = [pltpu.VMEM((sources // 2, local, PAIR, w), BF16) for w in (cut, width - cut)]
     *first, gate_grad, up_grad = pl.pallas_call(
-        functools.partial(backward_kernel, sources, pieces, slice(0, half)),
+        functools.partial(backward_kernel, sources, pieces, slice(0, cut)),
         in_specs=[VMEM] * (sources * pieces + 7),
         out_specs=(VMEM,) * (sources + 2),
-        out_shape=outs + (factor, factor),
-        scratch_shapes=[pltpu.VMEM((local, rows, width), BF16), back],
+        out_shape=outs[0] + (factor, factor),
+        scratch_shapes=[pltpu.VMEM((local, rows, width), BF16), backs[0]],
         compiler_params=pltpu.CompilerParams(vmem_limit_bytes=11 * MIB),
         cost_estimate=SMALL,
         name="backward",
     )(*near(*[g for block in gs for g in block], a, b, pick, place, gate, up, down))
     rest = pl.pallas_call(
-        functools.partial(rest_kernel, sources, slice(half, width)),
-        in_specs=[VMEM] * 6,
+        functools.partial(rest_kernel, sources, pieces, slice(cut, width)),
+        in_specs=[VMEM] * (pieces + 5),
         out_specs=(VMEM,) * sources,
-        out_shape=outs,
-        scratch_shapes=[back],
-        compiler_params=pltpu.CompilerParams(vmem_limit_bytes=6 * MIB),
+        out_shape=outs[1],
+        scratch_shapes=[backs[1]],
+        compiler_params=pltpu.CompilerParams(vmem_limit_bytes=7 * MIB),
         cost_estimate=SMALL,
         name="rest",
-    )(*near(gs[0][-1], gate_grad, up_grad, place, gate, up))
+    )(*near(*gs[0], gate_grad, up_grad, place, gate, up))
     return first, rest
 
 
@@ -413,7 +426,7 @@
 
 def scattered(own, sent, last, after):
     move = moved if last else moved_back
-    terms = [own if last else move(own, 0)] + [move(part, by) for part, by in sent]
+    terms = [own] + [move(part, by) for part, by in sent]
     return pl.pallas_call(
         functools.partial(sum_kernel, len(terms)),
         in_specs=[VMEM] * (len(terms) + len(after)),
@@ -454,11 +467,14 @@
             following = held(saved_inputs[0], step + 1, passed) if ringed else saved_inputs[0, step + 1]
             xs = gathered_near(following)
             beside = xs[1::2] if ringed else ()
-        halves = backward(gs, *factors, *back, F32 if last else BF16)
-        sent = [joined_parts(who, parts, beside) for parts in halves]
+        halves = backward(CUTS[last], F32 if last else BF16, gs, *factors, *back)
+        owns = [parts[0] if last else moved_back(parts[0], 0) for parts in halves]
+        sent = []
+        for own, parts in zip(owns, halves):
+            sent.append(joined_parts(who, parts, (*beside, own)))
         grads = []
-        for parts, pairs in zip(halves, sent):
-            grads.append(scattered(parts[0], pairs, last, grads))
+        for own, pairs in zip(owns, sent):
+            grads.append(scattered(own, pairs, last, grads))
         if not last:
             xs, _ = gathered_far(who, xs, done)
             gs = [gathered_near(grad) for grad in grads]

time: 119 us -> 118 us (level)
  waiting for transfers between devices: 34.9 us -> 32.2 us
    ppermute x6, starting transfers between devices: 7.63 us -> 9.83 us  [moved_back(): return lax.ppermute(value, ('section', 'expert'), pairs)]
    ppermute x6, waiting for transfers between devices: 9.05 us -> 6.91 us  [moved_back(): return lax.ppermute(value, ('section', 'expert'), pairs)]
    ppermute x9, waiting for transfers between devices: 13.2 us -> 11.8 us  [swapped(): lax.ppermute(value, 'expert', [(i, i ^ 1) for i in range(lax.axis_size('e...]
  transfers between devices with their start and end apart: 29 -> 29, of which waited for: 16 -> 14; matrix products, arithmetic and copies ran while one was open for 0% -> 0% of each run, Pallas kernels for 32% -> 32%
where the time goes in v5:
time: 118 us
  Pallas kernels  43.3 us (37%)
  starting transfers between devices  41 us (35%)
  waiting for transfers between devices  32.2 us (27%)
    ppermute x14, starting transfers between devices, moved(): lax.ppermute(value, 'expert', [(i, (i + by) % count) for i in range(count)])  24.8 us
    ppermute x14, waiting for transfers between devices, moved(): lax.ppermute(value, 'expert', [(i, (i + by) % count) for i in range(count)])  13.5 us
    pallas_call x2, Pallas kernels, forward(): pl.pallas_call(functools.partial(forward_kernel, sources, local, tokens,...  12.4 us
    ppermute x9, waiting for transfers between devices, swapped(): lax.ppermute(value, 'expert', [(i, i ^ 1) for i in range(lax.axis_size('e...  11.8 us
    pallas_call x1, Pallas kernels, turned(): pl.pallas_call(functools.partial(turn_kernel, len(weights) - 1), grid=(lo...  9.87 us
    ppermute x6, starting transfers between devices, moved_back(): return lax.ppermute(value, ('section', 'expert'), pairs)  9.83 us
    pallas_call x2, Pallas kernels, backward(): pl.pallas_call(functools.partial(backward_kernel, sources, pieces, slice(...  8.52 us
    ppermute x6, waiting for transfers between devices, moved_back(): return lax.ppermute(value, ('section', 'expert'), pairs)  6.91 us
  transfers between devices with their start and end apart: 29, of which 14 were waited for; matrix products, arithmetic and copies ran while one was open for 0% of the time, Pallas kernels for 32%

profile of v5, /device:TPU:0, one launch (start us, length us, event | category | flops | bytes accessed | tf_op | source)
XLA Modules:
  0.0 117.5 jit_solution(722076391011386404)
XLA Ops:
  0.0 1.1 first.1
  1.1 3.1 %collective-permute-start.1 = (bf16[136,1024]{1,0:T(8,128)(2,1)S(1)}, bf16[136,1024]{1,0:T(8,128)(2,1)S(1)}, u32[]{:S(2)}, u32[]{:S(2)}) collective-permute-start(bf16[136,1024]{1,0:T(8,128)(2,1)S(1)} %get-tuple-element.52.refs_2_.refs_0_.refs_4_), channel_id=1, source_target_pairs={{0,1},{1,2},{2,3},{3,0},{4,5},{5,6},{6,7},{7,4},{8,9},{9,10},{10,1... | collective-permute-start | bytes 835592 | tf_op jit(solution)/shard_map/ppermute | solution.py:380
  4.2 2.1 %collective-permute-start.2 = (bf16[136,1024]{1,0:T(8,128)(2,1)S(1)}, bf16[136,1024]{1,0:T(8,128)(2,1)S(1)}, u32[]{:S(2)}, u32[]{:S(2)}) collective-permute-start(bf16[136,1024]{1,0:T(8,128)(2,1)S(1)} %get-tuple-element.52.refs_2_.refs_0_.refs_4_), channel_id=1, source_target_pairs={{0,3},{1,0},{2,1},{3,2},{4,7},{5,4},{6,5},{7,6},{8,11},{9,8},{10,9... | collective-permute-start | bytes 835592 | tf_op jit(solution)/shard_map/ppermute | solution.py:380
  6.3 3.8 %collective-permute-start.3 = (bf16[128,1024]{1,0:T(8,128)(2,1)S(1)}, bf16[128,1024]{1,0:T(8,128)(2,1)S(1)}, u32[]{:S(2)}, u32[]{:S(2)}) collective-permute-start(bf16[128,1024]{1,0:T(8,128)(2,1)S(1)} %get-tuple-element.51.refs_0_), channel_id=1, source_target_pairs={{0,3},{1,0},{2,1},{3,2},{4,7},{5,4},{6,5},{7,6},{8,11},{9,8},{10,9... | collective-permute-start | bytes 786440 | tf_op jit(solution)/shard_map/ppermute | solution.py:380
  10.1 9.9 %turn.1 = (bf16[8,512,1024]{2,1,0:T(8,128)(2,1)S(1)}, bf16[8,512,1024]{2,1,0:T(8,128)(2,1)S(1)}, bf16[8,1024,512]{2,1,0:T(8,128)(2,1)S(1)}, f32[8,128]{1,0:T(8,128)S(1)}) custom-call(s32[1]{0:T(128)} %bitcast.8.refs_0_.base_ref, s32[1]{0:T(128)} %bitcast.6.refs_1_.odd_ref, bf16[136,1024]{1,0:T(8,128)(2,1)S(1)} %get-tuple-element.52.refs_2_.refs_0_.refs_4_, ...), custom_call_target="tpu_custom_call" | custom-call | bytes 1024 | tf_op jit(solution)/shard_map/turn/pallas_call | solution.py:213
  20.0 0.4 collective-permute-start.5
  20.4 6.9 %turn_into.1 = (bf16[8,1024,512]{2,1,0:T(8,128)(2,1)S(1)}, f32[8,128]{1,0:T(8,128)S(1)}) custom-call(bf16[8,512,1024]{2,1,0:T(8,128)(2,1)} %bitcast.19, bf16[136,1024]{1,0:T(8,128)(2,1)S(1)} %choose.5.after_ref, bf16[8,1024,512]{2,1,0:T(8,128)(2,1)S(1)} %get-tuple-element.54.held_ref), custom_call_target="tpu_custom_call", output_to_operand_aliasing={{0}: (2, {})} | custom-call | bytes 1024 | tf_op jit(solution)/shard_map/turn_into/pallas_call | solution.py:226
  27.3 2.9 %collective-permute-done.3.right_ref.refs_3_ = bf16[128,1024]{1,0:T(8,128)(2,1)S(1)} collective-permute-done((bf16[128,1024]{1,0:T(8,128)(2,1)S(1)}, bf16[128,1024]{1,0:T(8,128)(2,1)S(1)}, u32[]{:S(2)}, u32[]{:S(2)}) %collective-permute-start.3) | collective-permute-done | bytes 262176 | tf_op jit(solution)/shard_map/ppermute | solution.py:380
  30.2 0.5 collective-permute-start.4
  30.8 1.7 %collective-permute-start.8 = (bf16[128,1024]{1,0:T(8,128)(2,1)S(1)}, bf16[128,1024]{1,0:T(8,128)(2,1)S(1)}, u32[]{:S(2)}, u32[]{:S(2)}) collective-permute-start(bf16[128,1024]{1,0:T(8,128)(2,1)S(1)} %hold.1.refs_0_), channel_id=1, source_target_pairs={{0,1},{1,2},{2,3},{3,0},{4,5},{5,6},{6,7},{7,4},{8,9},{9,10},{10,1... | collective-permute-start | bytes 786440 | tf_op jit(solution)/shard_map/ppermute | solution.py:380
  32.4 2.2 %collective-permute-start.9 = (bf16[128,1024]{1,0:T(8,128)(2,1)S(1)}, bf16[128,1024]{1,0:T(8,128)(2,1)S(1)}, u32[]{:S(2)}, u32[]{:S(2)}) collective-permute-start(bf16[128,1024]{1,0:T(8,128)(2,1)S(1)} %hold.1.refs_0_), channel_id=1, source_target_pairs={{0,3},{1,0},{2,1},{3,2},{4,7},{5,4},{6,5},{7,6},{8,11},{9,8},{10,9... | collective-permute-start | bytes 786440 | tf_op jit(solution)/shard_map/ppermute | solution.py:380
  34.6 1.6 %collective-permute-done.5.refs_2_.refs_6_ = bf16[136,1024]{1,0:T(8,128)(2,1)S(1)} collective-permute-done((bf16[136,1024]{1,0:T(8,128)(2,1)S(1)}, bf16[136,1024]{1,0:T(8,128)(2,1)S(1)}, u32[]{:S(2)}, u32[]{:S(2)}) %collective-permute-start.5) | collective-permute-done | bytes 278560 | tf_op jit(solution)/shard_map/ppermute | solution.py:384
  36.2 6.2 %forward.2 = (f32[8,160,512]{2,1,0:T(8,128)S(1)}, f32[8,160,512]{2,1,0:T(8,128)S(1)}, bf16[2,640,256]{2,1,0:T(8,128)(2,1)S(1)}, bf16[2,256,640]{2,1,0:T(8,128)(2,1)S(1)}, f32[8,128]{1,0:T(8,128)S(1)}) custom-call(s32[1]{0:T(128)} %bitcast.8.refs_0_.base_ref, bf16[136,1024]{1,0:T(8,128)(2,1)S(1)} %get-tuple-element.52.refs_2_.refs_0_.refs_4_, ...), custom_call_target="tpu_custom_call" | custom-call | bytes 1024 | tf_op jit(solution)/shard_map/forward/pallas_call | solution.py:325
  42.4 0.3 collective-permute-done.4.refs_2_
  42.6 4.3 %backward.2 = (bf16[128,512]{1,0:T(8,128)(2,1)S(1)}, bf16[128,512]{1,0:T(8,128)(2,1)S(1)}, bf16[128,512]{1,0:T(8,128)(2,1)S(1)}, bf16[128,512]{1,0:T(8,128)(2,1)...) custom-call(bf16[128,1024]{1,0:T(8,128)(2,1)S(1)} %get-tuple-element.51.refs_0_, ...), custom_call_target="tpu_custom_call" | custom-call | bytes 1024 | tf_op jit(solution)/shard_map/backward/pallas_call | solution.py:355
  46.9 0.7 collective-permute-start.6
  47.8 2.0 %rest.2 = (bf16[128,512]{1,0:T(8,128)(2,1)S(1)}, bf16[128,512]{1,0:T(8,128)(2,1)S(1)}, bf16[128,512]{1,0:T(8,128)(2,1)S(1)}, bf16[128,512]{1,0:T(8,128)(2,1)S(1)}) custom-call(bf16[128,1024]{1,0:T(8,128)(2,1)S(1)} %get-tuple-element.51.refs_0_, bf16[8,160,512]{2,1,0:T(8,128)(2,1)S(1)} %get-tuple-element.69.refs_1_, ...), custom_call_target="tpu_custom_call" | custom-call | bytes 1024 | tf_op jit(solution)/shard_map/rest/pallas_call | solution.py:365
  49.7 2.3 %collective-permute-start.12 = (bf16[128,512]{1,0:T(8,128)(2,1)S(1)}, bf16[128,512]{1,0:T(8,128)(2,1)S(1)}, u32[]{:S(2)}, u32[]{:S(2)}) collective-permute-start(bf16[128,512]{1,0:T(8,128)(2,1)S(1)} %get-tuple-element.71), channel_id=1, source_target_pairs={{0,28},{1,29},{2,30},{3,31},{4,0},{5,1},{6,2},{7,3},{8,4},{9,5},{1... | collective-permute-start | bytes 393224 | tf_op jit(solution)/shard_map/ppermute | solution.py:394
  52.0 1.8 %collective-permute-start.13 = (bf16[128,512]{1,0:T(8,128)(2,1)S(1)}, bf16[128,512]{1,0:T(8,128)(2,1)S(1)}, u32[]{:S(2)}, u32[]{:S(2)}) collective-permute-start(bf16[128,512]{1,0:T(8,128)(2,1)S(1)} %get-tuple-element.72), channel_id=1, source_target_pairs={{0,1},{1,0},{2,3},{3,2},{4,5},{5,4},{6,7},{7,6},{8,9},{9,8},{10,11... | collective-permute-start | bytes 393224 | tf_op jit(solution)/shard_map/ppermute | solution.py:384
  53.8 0.3 collective-permute-start.18
  54.1 1.7 %collective-permute-done.7.far_ref = bf16[128,512]{1,0:T(8,128)(2,1)S(1)} collective-permute-done((bf16[128,512]{1,0:T(8,128)(2,1)S(1)}, bf16[128,512]{1,0:T(8,128)(2,1)S(1)}, u32[]{:S(2)}, u32[]{:S(2)}) %collective-permute-start.7) | collective-permute-done | bytes 131104 | tf_op jit(solution)/shard_map/ppermute | solution.py:384
  55.9 3.3 %collective-permute-start.10 = (bf16[128,512]{1,0:T(8,128)(2,1)S(1)}, bf16[128,512]{1,0:T(8,128)(2,1)S(1)}, u32[]{:S(2)}, u32[]{:S(2)}) collective-permute-start(bf16[128,512]{1,0:T(8,128)(2,1)S(1)} %get-tuple-element.67), channel_id=1, source_target_pairs={{0,31},{1,28},{2,29},{3,30},{4,3},{5,0},{6,1},{7,2},{8,7},{9,4},{1... | collective-permute-start | bytes 393224 | tf_op jit(solution)/shard_map/ppermute | solution.py:394
  59.1 0.4 collective-permute-start.11
  59.6 3.2 %collective-permute-start.14 = (bf16[128,512]{1,0:T(8,128)(2,1)S(1)}, bf16[128,512]{1,0:T(8,128)(2,1)S(1)}, u32[]{:S(2)}, u32[]{:S(2)}) collective-permute-start(bf16[128,512]{1,0:T(8,128)(2,1)S(1)} %get-tuple-element.75), channel_id=1, source_target_pairs={{0,31},{1,28},{2,29},{3,30},{4,3},{5,0},{6,1},{7,2},{8,7},{9,4},{1... | collective-permute-start | bytes 393224 | tf_op jit(solution)/shard_map/ppermute | solution.py:394
  62.8 3.4 %collective-permute-done.10.refs_1_ = bf16[128,512]{1,0:T(8,128)(2,1)S(1)} collective-permute-done((bf16[128,512]{1,0:T(8,128)(2,1)S(1)}, bf16[128,512]{1,0:T(8,128)(2,1)S(1)}, u32[]{:S(2)}, u32[]{:S(2)}) %collective-permute-start.10) | collective-permute-done | bytes 131104 | tf_op jit(solution)/shard_map/ppermute | solution.py:394
  66.2 2.8 %collective-permute-done.11.refs_2_ = bf16[128,512]{1,0:T(8,128)(2,1)S(1)} collective-permute-done((bf16[128,512]{1,0:T(8,128)(2,1)S(1)}, bf16[128,512]{1,0:T(8,128)(2,1)S(1)}, u32[]{:S(2)}, u32[]{:S(2)}) %collective-permute-start.11) | collective-permute-done | bytes 131104 | tf_op jit(solution)/shard_map/ppermute | solution.py:394
  69.1 3.8 %collective-permute-start.19 = (bf16[128,512]{1,0:T(8,128)(2,1)S(1)}, bf16[128,512]{1,0:T(8,128)(2,1)S(1)}, u32[]{:S(2)}, u32[]{:S(2)}) collective-permute-start(bf16[128,512]{1,0:T(8,128)(2,1)S(1)} %sum.4.refs_3_.refs_0_), channel_id=1, source_target_pairs={{0,3},{1,0},{2,1},{3,2},{4,7},{5,4},{6,5},{7,6},{8,11},{9,8},{10,9... | collective-permute-start | bytes 393224 | tf_op jit(solution)/shard_map/ppermute | solution.py:380
  72.9 0.7 collective-permute-done.15.refs_2_
  73.7 3.8 %collective-permute-start.21 = (bf16[128,512]{1,0:T(8,128)(2,1)S(1)}, bf16[128,512]{1,0:T(8,128)(2,1)S(1)}, u32[]{:S(2)}, u32[]{:S(2)}) collective-permute-start(bf16[128,512]{1,0:T(8,128)(2,1)S(1)} %sum.5.refs_1_), channel_id=1, source_target_pairs={{0,3},{1,0},{2,1},{3,2},{4,7},{5,4},{6,5},{7,6},{8,11},{9,8},{10,9... | collective-permute-start | bytes 393224 | tf_op jit(solution)/shard_map/ppermute | solution.py:380
  77.6 6.2 %forward.3 = (f32[8,160,512]{2,1,0:T(8,128)S(1)}, f32[8,160,512]{2,1,0:T(8,128)S(1)}, bf16[2,640,256]{2,1,0:T(8,128)(2,1)S(1)}, bf16[2,256,640]{2,1,0:T(8,128)(2,1)S(1)}, f32[8,128]{1,0:T(8,128)S(1)}) custom-call(s32[1]{0:T(128)} %bitcast.8.refs_0_.base_ref, bf16[128,1024]{1,0:T(8,128)(2,1)S(1)} %hold.1.refs_0_, ...), custom_call_target="tpu_custom_call" | custom-call | bytes 1024 | tf_op jit(solution)/shard_map/forward/pallas_call | solution.py:325
  83.9 2.3 %collective-permute-done.21.right_ref.refs_7_ = bf16[128,512]{1,0:T(8,128)(2,1)S(1)} collective-permute-done((bf16[128,512]{1,0:T(8,128)(2,1)S(1)}, bf16[128,512]{1,0:T(8,128)(2,1)S(1)}, u32[]{:S(2)}, u32[]{:S(2)}) %collective-permute-start.21) | collective-permute-done | bytes 131104 | tf_op jit(solution)/shard_map/ppermute | solution.py:380
  86.2 0.2 choose.9
  86.4 1.1 collective-permute-start.22
  87.5 1.6 %collective-permute-done.20.refs_4_ = bf16[128,512]{1,0:T(8,128)(2,1)S(1)} collective-permute-done((bf16[128,512]{1,0:T(8,128)(2,1)S(1)}, bf16[128,512]{1,0:T(8,128)(2,1)S(1)}, u32[]{:S(2)}, u32[]{:S(2)}) %collective-permute-start.20) | collective-permute-done | bytes 131104 | tf_op jit(solution)/shard_map/ppermute | solution.py:384
  89.1 3.8 %collective-permute-done.22.refs_5_ = bf16[128,512]{1,0:T(8,128)(2,1)S(1)} collective-permute-done((bf16[128,512]{1,0:T(8,128)(2,1)S(1)}, bf16[128,512]{1,0:T(8,128)(2,1)S(1)}, u32[]{:S(2)}, u32[]{:S(2)}) %collective-permute-start.22) | collective-permute-done | bytes 131104 | tf_op jit(solution)/shard_map/ppermute | solution.py:384
  92.9 4.2 %backward.3 = (f32[128,512]{1,0:T(8,128)S(1)}, bf16[128,512]{1,0:T(8,128)(2,1)S(1)}, bf16[128,512]{1,0:T(8,128)(2,1)S(1)}, bf16[128,512]{1,0:T(8,128)(2,1)S(1)},...) custom-call(bf16[128,512]{1,0:T(8,128)(2,1)S(1)} %sum.4.refs_3_.refs_0_, ...), custom_call_target="tpu_custom_call" | custom-call | bytes 1024 | tf_op jit(solution)/shard_map/backward/pallas_call | solution.py:355
  97.1 0.6 collective-permute-start.23
  97.7 2.0 %rest.3 = (f32[128,512]{1,0:T(8,128)S(1)}, bf16[128,512]{1,0:T(8,128)(2,1)S(1)}, bf16[128,512]{1,0:T(8,128)(2,1)S(1)}, bf16[128,512]{1,0:T(8,128)(2,1)S(1)}) custom-call(bf16[128,512]{1,0:T(8,128)(2,1)S(1)} %sum.4.refs_3_.refs_0_, bf16[128,512]{1,0:T(8,128)(2,1)S(1)} %sum.5.refs_1_, bf16[8,160,512]{2,1,0:T(8,128)(2,1)S(1)} %get-tuple-element.89.refs_2_, ...), custom_call_target="tpu_custom_call" | custom-call | bytes 1024 | tf_op jit(solution)/shard_map/rest/pallas_call | solution.py:365
  99.7 1.6 %collective-permute-start.26 = (bf16[128,512]{1,0:T(8,128)(2,1)S(1)}, bf16[128,512]{1,0:T(8,128)(2,1)S(1)}, u32[]{:S(2)}, u32[]{:S(2)}) collective-permute-start(bf16[128,512]{1,0:T(8,128)(2,1)S(1)} %get-tuple-element.92), channel_id=1, source_target_pairs={{0,1},{1,0},{2,3},{3,2},{4,5},{5,4},{6,7},{7,6},{8,9},{9,8},{10,11... | collective-permute-start | bytes 393224 | tf_op jit(solution)/shard_map/ppermute | solution.py:384
  101.3 2.2 %collective-permute-done.23.far_ref = bf16[128,512]{1,0:T(8,128)(2,1)S(1)} collective-permute-done((bf16[128,512]{1,0:T(8,128)(2,1)S(1)}, bf16[128,512]{1,0:T(8,128)(2,1)S(1)}, u32[]{:S(2)}, u32[]{:S(2)}) %collective-permute-start.23) | collective-permute-done | bytes 131104 | tf_op jit(solution)/shard_map/ppermute | solution.py:384
  103.5 0.5 collective-permute-start.24
  104.0 1.6 %collective-permute-start.25 = (bf16[128,512]{1,0:T(8,128)(2,1)S(1)}, bf16[128,512]{1,0:T(8,128)(2,1)S(1)}, u32[]{:S(2)}, u32[]{:S(2)}) collective-permute-start(bf16[128,512]{1,0:T(8,128)(2,1)S(1)} %get-tuple-element.88), channel_id=1, source_target_pairs={{0,1},{1,2},{2,3},{3,0},{4,5},{5,6},{6,7},{7,4},{8,9},{9,10},{10,1... | collective-permute-start | bytes 393224 | tf_op jit(solution)/shard_map/ppermute | solution.py:380
  105.6 0.7 collective-permute-done.26.far_ref
  106.3 1.6 %collective-permute-start.27 = (bf16[128,512]{1,0:T(8,128)(2,1)S(1)}, bf16[128,512]{1,0:T(8,128)(2,1)S(1)}, u32[]{:S(2)}, u32[]{:S(2)}) collective-permute-start(bf16[128,512]{1,0:T(8,128)(2,1)S(1)} %get-tuple-element.95), channel_id=1, source_target_pairs={{0,3},{1,0},{2,1},{3,2},{4,7},{5,4},{6,5},{7,6},{8,11},{9,8},{10,9... | collective-permute-start | bytes 393224 | tf_op jit(solution)/shard_map/ppermute | solution.py:380
  107.9 0.4 collective-permute-start.28
  108.4 4.1 %collective-permute-done.24.refs_1_ = bf16[128,512]{1,0:T(8,128)(2,1)S(1)} collective-permute-done((bf16[128,512]{1,0:T(8,128)(2,1)S(1)}, bf16[128,512]{1,0:T(8,128)(2,1)S(1)}, u32[]{:S(2)}, u32[]{:S(2)}) %collective-permute-start.24) | collective-permute-done | bytes 131104 | tf_op jit(solution)/shard_map/ppermute | solution.py:380
  112.6 4.2 %collective-permute-done.27.refs_1_ = bf16[128,512]{1,0:T(8,128)(2,1)S(1)} collective-permute-done((bf16[128,512]{1,0:T(8,128)(2,1)S(1)}, bf16[128,512]{1,0:T(8,128)(2,1)S(1)}, u32[]{:S(2)}, u32[]{:S(2)}) %collective-permute-start.27) | collective-permute-done | bytes 131104 | tf_op jit(solution)/shard_map/ppermute | solution.py:380
  116.8 0.7 maximum_bitcast_fusion
  (36 shorter events, 0.8 us)
Async XLA Ops:
  1.1 18.9 %collective-permute-start.1 = (bf16[136,1024]{1,0:T(8,128)(2,1)S(1)}, bf16[136,1024]{1,0:T(8,128)(2,1)S(1)}, u32[]{:S(2)}, u32[]{:S(2)}) collective-permute-start(bf16[136,1024]{1,0:T(8,128)(2,1)S(1)} %get-tuple-element.52.refs_2_.refs_0_.refs_4_), channel_id=1, source_target_pairs={{0,1},{1,2},{2,3},{3,0},{4,5},{5,6},{6,7},{7,4},{8,9},{9,10},{10,1... | collective-permute-start | bytes 835592 | tf_op jit(solution)/shard_map/ppermute | solution.py:380
  4.2 15.8 %collective-permute-start.2 = (bf16[136,1024]{1,0:T(8,128)(2,1)S(1)}, bf16[136,1024]{1,0:T(8,128)(2,1)S(1)}, u32[]{:S(2)}, u32[]{:S(2)}) collective-permute-start(bf16[136,1024]{1,0:T(8,128)(2,1)S(1)} %get-tuple-element.52.refs_2_.refs_0_.refs_4_), channel_id=1, source_target_pairs={{0,3},{1,0},{2,1},{3,2},{4,7},{5,4},{6,5},{7,6},{8,11},{9,8},{10,9... | collective-permute-start | bytes 835592 | tf_op jit(solution)/shard_map/ppermute | solution.py:380
  6.3 21.0 %collective-permute-start = (bf16[128,1024]{1,0:T(8,128)(2,1)S(1)}, bf16[128,1024]{1,0:T(8,128)(2,1)S(1)}, u32[]{:S(2)}, u32[]{:S(2)}) collective-permute-start(bf16[128,1024]{1,0:T(8,128)(2,1)S(1)} %get-tuple-element.51.refs_0_), channel_id=1, source_target_pairs={{0,1},{1,2},{2,3},{3,0},{4,5},{5,6},{6,7},{7,4},{8,9},{9,10},{10,1... | collective-permute-start | bytes 786440 | tf_op jit(solution)/shard_map/ppermute | solution.py:380
  6.3 23.9 %collective-permute-start.3 = (bf16[128,1024]{1,0:T(8,128)(2,1)S(1)}, bf16[128,1024]{1,0:T(8,128)(2,1)S(1)}, u32[]{:S(2)}, u32[]{:S(2)}) collective-permute-start(bf16[128,1024]{1,0:T(8,128)(2,1)S(1)} %get-tuple-element.51.refs_0_), channel_id=1, source_target_pairs={{0,3},{1,0},{2,1},{3,2},{4,7},{5,4},{6,5},{7,6},{8,11},{9,8},{10,9... | collective-permute-start | bytes 786440 | tf_op jit(solution)/shard_map/ppermute | solution.py:380
  20.0 16.2 %collective-permute-start.5 = (bf16[136,1024]{1,0:T(8,128)(2,1)S(1)}, bf16[136,1024]{1,0:T(8,128)(2,1)S(1)}, u32[]{:S(2)}, u32[]{:S(2)}) collective-permute-start(bf16[136,1024]{1,0:T(8,128)(2,1)S(1)} %choose.5.after_ref), channel_id=1, source_target_pairs={{0,1},{1,0},{2,3},{3,2},{4,5},{5,4},{6,7},{7,6},{8,9},{9,8},{10,11... | collective-permute-start | bytes 835592 | tf_op jit(solution)/shard_map/ppermute | solution.py:384
  20.4 10.3 %copy-start = (bf16[1,2,128,1024]{3,2,1,0:T(8,128)(2,1)S(1)}, bf16[1,2,128,1024]{3,2,1,0:T(8,128)(2,1)}, u32[]{:S(2)}) copy-start(bf16[1,2,128,1024]{3,2,1,0:T(8,128)(2,1)} %param.8) | copy-start | bytes 1572868
  30.2 12.4 %collective-permute-start.4 = (bf16[128,1024]{1,0:T(8,128)(2,1)S(1)}, bf16[128,1024]{1,0:T(8,128)(2,1)S(1)}, u32[]{:S(2)}, u32[]{:S(2)}) collective-permute-start(bf16[128,1024]{1,0:T(8,128)(2,1)S(1)} %choose.6.refs_0_), channel_id=1, source_target_pairs={{0,1},{1,0},{2,3},{3,2},{4,5},{5,4},{6,7},{7,6},{8,9},{9,8},{10,11... | collective-permute-start | bytes 786440 | tf_op jit(solution)/shard_map/ppermute | solution.py:384
  30.8 21.3 %collective-permute-start.8 = (bf16[128,1024]{1,0:T(8,128)(2,1)S(1)}, bf16[128,1024]{1,0:T(8,128)(2,1)S(1)}, u32[]{:S(2)}, u32[]{:S(2)}) collective-permute-start(bf16[128,1024]{1,0:T(8,128)(2,1)S(1)} %hold.1.refs_0_), channel_id=1, source_target_pairs={{0,1},{1,2},{2,3},{3,0},{4,5},{5,6},{6,7},{7,4},{8,9},{9,10},{10,1... | collective-permute-start | bytes 786440 | tf_op jit(solution)/shard_map/ppermute | solution.py:380
  32.4 21.4 %collective-permute-start.9 = (bf16[128,1024]{1,0:T(8,128)(2,1)S(1)}, bf16[128,1024]{1,0:T(8,128)(2,1)S(1)}, u32[]{:S(2)}, u32[]{:S(2)}) collective-permute-start(bf16[128,1024]{1,0:T(8,128)(2,1)S(1)} %hold.1.refs_0_), channel_id=1, source_target_pairs={{0,3},{1,0},{2,1},{3,2},{4,7},{5,4},{6,5},{7,6},{8,11},{9,8},{10,9... | collective-permute-start | bytes 786440 | tf_op jit(solution)/shard_map/ppermute | solution.py:380
  46.9 7.2 %collective-permute-start.6 = (bf16[128,512]{1,0:T(8,128)(2,1)S(1)}, bf16[128,512]{1,0:T(8,128)(2,1)S(1)}, u32[]{:S(2)}, u32[]{:S(2)}) collective-permute-start(bf16[128,512]{1,0:T(8,128)(2,1)S(1)} %get-tuple-element.63), channel_id=1, source_target_pairs={{0,28},{1,29},{2,30},{3,31},{4,0},{5,1},{6,2},{7,3},{8,4},{9,5},{1... | collective-permute-start | bytes 393224 | tf_op jit(solution)/shard_map/ppermute | solution.py:394
  47.7 8.2 %collective-permute-start.7 = (bf16[128,512]{1,0:T(8,128)(2,1)S(1)}, bf16[128,512]{1,0:T(8,128)(2,1)S(1)}, u32[]{:S(2)}, u32[]{:S(2)}) collective-permute-start(bf16[128,512]{1,0:T(8,128)(2,1)S(1)} %get-tuple-element.64), channel_id=1, source_target_pairs={{0,1},{1,0},{2,3},{3,2},{4,5},{5,4},{6,7},{7,6},{8,9},{9,8},{10,11... | collective-permute-start | bytes 393224 | tf_op jit(solution)/shard_map/ppermute | solution.py:384
  49.7 9.8 %collective-permute-start.12 = (bf16[128,512]{1,0:T(8,128)(2,1)S(1)}, bf16[128,512]{1,0:T(8,128)(2,1)S(1)}, u32[]{:S(2)}, u32[]{:S(2)}) collective-permute-start(bf16[128,512]{1,0:T(8,128)(2,1)S(1)} %get-tuple-element.71), channel_id=1, source_target_pairs={{0,28},{1,29},{2,30},{3,31},{4,0},{5,1},{6,2},{7,3},{8,4},{9,5},{1... | collective-permute-start | bytes 393224 | tf_op jit(solution)/shard_map/ppermute | solution.py:394
  52.0 7.6 %collective-permute-start.13 = (bf16[128,512]{1,0:T(8,128)(2,1)S(1)}, bf16[128,512]{1,0:T(8,128)(2,1)S(1)}, u32[]{:S(2)}, u32[]{:S(2)}) collective-permute-start(bf16[128,512]{1,0:T(8,128)(2,1)S(1)} %get-tuple-element.72), channel_id=1, source_target_pairs={{0,1},{1,0},{2,3},{3,2},{4,5},{5,4},{6,7},{7,6},{8,9},{9,8},{10,11... | collective-permute-start | bytes 393224 | tf_op jit(solution)/shard_map/ppermute | solution.py:384
  53.8 23.8 %collective-permute-start.18 = (bf16[128,1024]{1,0:T(8,128)(2,1)S(1)}, bf16[128,1024]{1,0:T(8,128)(2,1)S(1)}, u32[]{:S(2)}, u32[]{:S(2)}) collective-permute-start(bf16[128,1024]{1,0:T(8,128)(2,1)S(1)} %choose.7), channel_id=1, source_target_pairs={{0,1},{1,0},{2,3},{3,2},{4,5},{5,4},{6,7},{7,6},{8,9},{9,8},{10,11... | collective-permute-start | bytes 786440 | tf_op jit(solution)/shard_map/ppermute | solution.py:384
  55.9 10.3 %collective-permute-start.10 = (bf16[128,512]{1,0:T(8,128)(2,1)S(1)}, bf16[128,512]{1,0:T(8,128)(2,1)S(1)}, u32[]{:S(2)}, u32[]{:S(2)}) collective-permute-start(bf16[128,512]{1,0:T(8,128)(2,1)S(1)} %get-tuple-element.67), channel_id=1, source_target_pairs={{0,31},{1,28},{2,29},{3,30},{4,3},{5,0},{6,1},{7,2},{8,7},{9,4},{1... | collective-permute-start | bytes 393224 | tf_op jit(solution)/shard_map/ppermute | solution.py:394
  59.1 9.9 %collective-permute-start.11 = (bf16[128,512]{1,0:T(8,128)(2,1)S(1)}, bf16[128,512]{1,0:T(8,128)(2,1)S(1)}, u32[]{:S(2)}, u32[]{:S(2)}) collective-permute-start(bf16[128,512]{1,0:T(8,128)(2,1)S(1)} %get-tuple-element.68), channel_id=1, source_target_pairs={{0,29},{1,30},{2,31},{3,28},{4,1},{5,2},{6,3},{7,0},{8,5},{9,6},{1... | collective-permute-start | bytes 393224 | tf_op jit(solution)/shard_map/ppermute | solution.py:394
  59.6 13.3 %collective-permute-start.14 = (bf16[128,512]{1,0:T(8,128)(2,1)S(1)}, bf16[128,512]{1,0:T(8,128)(2,1)S(1)}, u32[]{:S(2)}, u32[]{:S(2)}) collective-permute-start(bf16[128,512]{1,0:T(8,128)(2,1)S(1)} %get-tuple-element.75), channel_id=1, source_target_pairs={{0,31},{1,28},{2,29},{3,30},{4,3},{5,0},{6,1},{7,2},{8,7},{9,4},{1... | collective-permute-start | bytes 393224 | tf_op jit(solution)/shard_map/ppermute | solution.py:394
  62.8 10.8 %collective-permute-start.15 = (bf16[128,512]{1,0:T(8,128)(2,1)S(1)}, bf16[128,512]{1,0:T(8,128)(2,1)S(1)}, u32[]{:S(2)}, u32[]{:S(2)}) collective-permute-start(bf16[128,512]{1,0:T(8,128)(2,1)S(1)} %get-tuple-element.76), channel_id=1, source_target_pairs={{0,29},{1,30},{2,31},{3,28},{4,1},{5,2},{6,3},{7,0},{8,5},{9,6},{1... | collective-permute-start | bytes 393224 | tf_op jit(solution)/shard_map/ppermute | solution.py:394
  69.1 14.7 %collective-permute-start.16 = (bf16[128,512]{1,0:T(8,128)(2,1)S(1)}, bf16[128,512]{1,0:T(8,128)(2,1)S(1)}, u32[]{:S(2)}, u32[]{:S(2)}) collective-permute-start(bf16[128,512]{1,0:T(8,128)(2,1)S(1)} %sum.4.refs_3_.refs_0_), channel_id=1, source_target_pairs={{0,1},{1,2},{2,3},{3,0},{4,5},{5,6},{6,7},{7,4},{8,9},{9,10},{10,1... | collective-permute-start | bytes 393224 | tf_op jit(solution)/shard_map/ppermute | solution.py:380
  69.1 14.6 %collective-permute-start.19 = (bf16[128,512]{1,0:T(8,128)(2,1)S(1)}, bf16[128,512]{1,0:T(8,128)(2,1)S(1)}, u32[]{:S(2)}, u32[]{:S(2)}) collective-permute-start(bf16[128,512]{1,0:T(8,128)(2,1)S(1)} %sum.4.refs_3_.refs_0_), channel_id=1, source_target_pairs={{0,3},{1,0},{2,1},{3,2},{4,7},{5,4},{6,5},{7,6},{8,11},{9,8},{10,9... | collective-permute-start | bytes 393224 | tf_op jit(solution)/shard_map/ppermute | solution.py:380
  73.7 10.2 %collective-permute-start.17 = (bf16[128,512]{1,0:T(8,128)(2,1)S(1)}, bf16[128,512]{1,0:T(8,128)(2,1)S(1)}, u32[]{:S(2)}, u32[]{:S(2)}) collective-permute-start(bf16[128,512]{1,0:T(8,128)(2,1)S(1)} %sum.5.refs_1_), channel_id=1, source_target_pairs={{0,1},{1,2},{2,3},{3,0},{4,5},{5,6},{6,7},{7,4},{8,9},{9,10},{10,1... | collective-permute-start | bytes 393224 | tf_op jit(solution)/shard_map/ppermute | solution.py:380
  73.7 12.4 %collective-permute-start.21 = (bf16[128,512]{1,0:T(8,128)(2,1)S(1)}, bf16[128,512]{1,0:T(8,128)(2,1)S(1)}, u32[]{:S(2)}, u32[]{:S(2)}) collective-permute-start(bf16[128,512]{1,0:T(8,128)(2,1)S(1)} %sum.5.refs_1_), channel_id=1, source_target_pairs={{0,3},{1,0},{2,1},{3,2},{4,7},{5,4},{6,5},{7,6},{8,11},{9,8},{10,9... | collective-permute-start | bytes 393224 | tf_op jit(solution)/shard_map/ppermute | solution.py:380
  83.8 5.3 %collective-permute-start.20 = (bf16[128,512]{1,0:T(8,128)(2,1)S(1)}, bf16[128,512]{1,0:T(8,128)(2,1)S(1)}, u32[]{:S(2)}, u32[]{:S(2)}) collective-permute-start(bf16[128,512]{1,0:T(8,128)(2,1)S(1)} %choose.8), channel_id=1, source_target_pairs={{0,1},{1,0},{2,3},{3,2},{4,5},{5,4},{6,7},{7,6},{8,9},{9,8},{10,11... | collective-permute-start | bytes 393224 | tf_op jit(solution)/shard_map/ppermute | solution.py:384
  86.4 6.5 %collective-permute-start.22 = (bf16[128,512]{1,0:T(8,128)(2,1)S(1)}, bf16[128,512]{1,0:T(8,128)(2,1)S(1)}, u32[]{:S(2)}, u32[]{:S(2)}) collective-permute-start(bf16[128,512]{1,0:T(8,128)(2,1)S(1)} %choose.9), channel_id=1, source_target_pairs={{0,1},{1,0},{2,3},{3,2},{4,5},{5,4},{6,7},{7,6},{8,9},{9,8},{10,11... | collective-permute-start | bytes 393224 | tf_op jit(solution)/shard_map/ppermute | solution.py:384
  97.1 6.3 %collective-permute-start.23 = (bf16[128,512]{1,0:T(8,128)(2,1)S(1)}, bf16[128,512]{1,0:T(8,128)(2,1)S(1)}, u32[]{:S(2)}, u32[]{:S(2)}) collective-permute-start(bf16[128,512]{1,0:T(8,128)(2,1)S(1)} %get-tuple-element.84), channel_id=1, source_target_pairs={{0,1},{1,0},{2,3},{3,2},{4,5},{5,4},{6,7},{7,6},{8,9},{9,8},{10,11... | collective-permute-start | bytes 393224 | tf_op jit(solution)/shard_map/ppermute | solution.py:384
  99.7 6.6 %collective-permute-start.26 = (bf16[128,512]{1,0:T(8,128)(2,1)S(1)}, bf16[128,512]{1,0:T(8,128)(2,1)S(1)}, u32[]{:S(2)}, u32[]{:S(2)}) collective-permute-start(bf16[128,512]{1,0:T(8,128)(2,1)S(1)} %get-tuple-element.92), channel_id=1, source_target_pairs={{0,1},{1,0},{2,3},{3,2},{4,5},{5,4},{6,7},{7,6},{8,9},{9,8},{10,11... | collective-permute-start | bytes 393224 | tf_op jit(solution)/shard_map/ppermute | solution.py:384
  103.5 9.0 %collective-permute-start.24 = (bf16[128,512]{1,0:T(8,128)(2,1)S(1)}, bf16[128,512]{1,0:T(8,128)(2,1)S(1)}, u32[]{:S(2)}, u32[]{:S(2)}) collective-permute-start(bf16[128,512]{1,0:T(8,128)(2,1)S(1)} %get-tuple-element.87), channel_id=1, source_target_pairs={{0,3},{1,0},{2,1},{3,2},{4,7},{5,4},{6,5},{7,6},{8,11},{9,8},{10,9... | collective-permute-start | bytes 393224 | tf_op jit(solution)/shard_map/ppermute | solution.py:380
  104.0 8.5 %collective-permute-start.25 = (bf16[128,512]{1,0:T(8,128)(2,1)S(1)}, bf16[128,512]{1,0:T(8,128)(2,1)S(1)}, u32[]{:S(2)}, u32[]{:S(2)}) collective-permute-start(bf16[128,512]{1,0:T(8,128)(2,1)S(1)} %get-tuple-element.88), channel_id=1, source_target_pairs={{0,1},{1,2},{2,3},{3,0},{4,5},{5,6},{6,7},{7,4},{8,9},{9,10},{10,1... | collective-permute-start | bytes 393224 | tf_op jit(solution)/shard_map/ppermute | solution.py:380
  106.3 10.5 %collective-permute-start.27 = (bf16[128,512]{1,0:T(8,128)(2,1)S(1)}, bf16[128,512]{1,0:T(8,128)(2,1)S(1)}, u32[]{:S(2)}, u32[]{:S(2)}) collective-permute-start(bf16[128,512]{1,0:T(8,128)(2,1)S(1)} %get-tuple-element.95), channel_id=1, source_target_pairs={{0,3},{1,0},{2,1},{3,2},{4,7},{5,4},{6,5},{7,6},{8,11},{9,8},{10,9... | collective-permute-start | bytes 393224 | tf_op jit(solution)/shard_map/ppermute | solution.py:380
  107.9 8.8 %collective-permute-start.28 = (bf16[128,512]{1,0:T(8,128)(2,1)S(1)}, bf16[128,512]{1,0:T(8,128)(2,1)S(1)}, u32[]{:S(2)}, u32[]{:S(2)}) collective-permute-start(bf16[128,512]{1,0:T(8,128)(2,1)S(1)} %get-tuple-element.96), channel_id=1, source_target_pairs={{0,1},{1,2},{2,3},{3,0},{4,5},{5,6},{6,7},{7,4},{8,9},{9,10},{10,1... | collective-permute-start | bytes 393224 | tf_op jit(solution)/shard_map/ppermute | solution.py:380

commit v6 on v5

--- a/solution.py
+++ b/solution.py
@@ -424,6 +424,30 @@
     refs[-1][...] = total.astype(BF16)
 
 
+def write_kernel(count, start, *refs):
+    out_ref, total_ref, sem = refs[-3:]
+    sum_kernel(count, *refs[:count], total_ref)
+    copy = pltpu.make_async_copy(total_ref, out_ref.at[:, start : start + total_ref.shape[1]], sem)
+    copy.start()
+    copy.wait()
+
+
+def written(own, sent, start, width, result):
+    terms = [own] + [moved(part, by) for part, by in sent]
+    anywhere = pl.BlockSpec(memory_space=pl.ANY)
+    return pl.pallas_call(
+        functools.partial(write_kernel, len(terms), start),
+        in_specs=[VMEM] * len(terms) + [anywhere] * len(result),
+        out_specs=anywhere,
+        out_shape=jax.ShapeDtypeStruct((own.shape[0], width), BF16),
+        scratch_shapes=[pltpu.VMEM(own.shape, BF16), pltpu.SemaphoreType.DMA],
+        input_output_aliases={len(terms): 0} if result else {},
+        compiler_params=pltpu.CompilerParams(vmem_limit_bytes=2 * MIB),
+        cost_estimate=SMALL,
+        name="write",
+    )(*near(*terms), *result)
+
+
 def scattered(own, sent, last, after):
     move = moved if last else moved_back
     terms = [own] + [move(part, by) for part, by in sent]
@@ -472,13 +496,18 @@
         sent = []
         for own, parts in zip(owns, halves):
             sent.append(joined_parts(who, parts, (*beside, own)))
+        if last:
+            result, start = (), 0
+            for own, pairs in zip(owns, sent):
+                result = (written(own, pairs, start, grad_out.shape[2], result),)
+                start += own.shape[1]
+            return result[0][None]
         grads = []
         for own, pairs in zip(owns, sent):
             grads.append(scattered(own, pairs, last, grads))
         if not last:
             xs, _ = gathered_far(who, xs, done)
             gs = [gathered_near(grad) for grad in grads]
-    return jnp.concatenate(grads, axis=1)[None]
 
 
 def solution(mesh):

time: 118 us -> 118 us (level)
  Pallas kernels: 43.3 us -> 44.6 us
    pallas_call x0 -> x2, Pallas kernels: none -> 1.41 us  [written(): pl.pallas_call(functools.partial(write_kernel, len(terms), start), in_spe...]
  transfers between devices with their start and end apart: 29 -> 29, of which waited for: 14 -> 14; matrix products, arithmetic and copies ran while one was open for 0% -> 0% of each run, Pallas kernels for 32% -> 33%
where the time goes in v6:
time: 118 us
  Pallas kernels  44.6 us (38%)
  starting transfers between devices  41 us (35%)
  waiting for transfers between devices  31.6 us (27%)
    ppermute x14, starting transfers between devices, moved(): lax.ppermute(value, 'expert', [(i, (i + by) % count) for i in range(count)])  24.8 us
    ppermute x14, waiting for transfers between devices, moved(): lax.ppermute(value, 'expert', [(i, (i + by) % count) for i in range(count)])  12.9 us
    pallas_call x2, Pallas kernels, forward(): pl.pallas_call(functools.partial(forward_kernel, sources, local, tokens,...  12.4 us
    ppermute x9, waiting for transfers between devices, swapped(): lax.ppermute(value, 'expert', [(i, i ^ 1) for i in range(lax.axis_size('e...  11.8 us
    pallas_call x1, Pallas kernels, turned(): pl.pallas_call(functools.partial(turn_kernel, len(weights) - 1), grid=(lo...  9.87 us
    ppermute x6, starting transfers between devices, moved_back(): return lax.ppermute(value, ('section', 'expert'), pairs)  9.83 us
    pallas_call x2, Pallas kernels, backward(): pl.pallas_call(functools.partial(backward_kernel, sources, pieces, slice(...  8.52 us
    ppermute x6, waiting for transfers between devices, moved_back(): return lax.ppermute(value, ('section', 'expert'), pairs)  6.91 us
  transfers between devices with their start and end apart: 29, of which 14 were waited for; matrix products, arithmetic and copies ran while one was open for 0% of the time, Pallas kernels for 33%

profile of v6, /device:TPU:0, one launch (start us, length us, event | category | flops | bytes accessed | tf_op | source)
XLA Modules:
  0.0 117.6 jit_solution(2238730778883888723)
XLA Ops:
  0.0 1.1 first.1
  1.1 3.1 %collective-permute-start.1 = (bf16[136,1024]{1,0:T(8,128)(2,1)S(1)}, bf16[136,1024]{1,0:T(8,128)(2,1)S(1)}, u32[]{:S(2)}, u32[]{:S(2)}) collective-permute-start(bf16[136,1024]{1,0:T(8,128)(2,1)S(1)} %get-tuple-element.52.refs_2_.refs_0_.refs_4_), channel_id=1, source_target_pairs={{0,1},{1,2},{2,3},{3,0},{4,5},{5,6},{6,7},{7,4},{8,9},{9,10},{10,1... | collective-permute-start | bytes 835592 | tf_op jit(solution)/shard_map/ppermute | solution.py:380
  4.2 2.1 %collective-permute-start.2 = (bf16[136,1024]{1,0:T(8,128)(2,1)S(1)}, bf16[136,1024]{1,0:T(8,128)(2,1)S(1)}, u32[]{:S(2)}, u32[]{:S(2)}) collective-permute-start(bf16[136,1024]{1,0:T(8,128)(2,1)S(1)} %get-tuple-element.52.refs_2_.refs_0_.refs_4_), channel_id=1, source_target_pairs={{0,3},{1,0},{2,1},{3,2},{4,7},{5,4},{6,5},{7,6},{8,11},{9,8},{10,9... | collective-permute-start | bytes 835592 | tf_op jit(solution)/shard_map/ppermute | solution.py:380
  6.3 3.8 %collective-permute-start.3 = (bf16[128,1024]{1,0:T(8,128)(2,1)S(1)}, bf16[128,1024]{1,0:T(8,128)(2,1)S(1)}, u32[]{:S(2)}, u32[]{:S(2)}) collective-permute-start(bf16[128,1024]{1,0:T(8,128)(2,1)S(1)} %get-tuple-element.51.refs_0_), channel_id=1, source_target_pairs={{0,3},{1,0},{2,1},{3,2},{4,7},{5,4},{6,5},{7,6},{8,11},{9,8},{10,9... | collective-permute-start | bytes 786440 | tf_op jit(solution)/shard_map/ppermute | solution.py:380
  10.1 9.9 %turn.1 = (bf16[8,512,1024]{2,1,0:T(8,128)(2,1)S(1)}, bf16[8,512,1024]{2,1,0:T(8,128)(2,1)S(1)}, bf16[8,1024,512]{2,1,0:T(8,128)(2,1)S(1)}, f32[8,128]{1,0:T(8,128)S(1)}) custom-call(s32[1]{0:T(128)} %bitcast.8.refs_0_.base_ref, s32[1]{0:T(128)} %bitcast.6.refs_1_.odd_ref, bf16[136,1024]{1,0:T(8,128)(2,1)S(1)} %get-tuple-element.52.refs_2_.refs_0_.refs_4_, ...), custom_call_target="tpu_custom_call" | custom-call | bytes 1024 | tf_op jit(solution)/shard_map/turn/pallas_call | solution.py:213
  20.0 0.4 collective-permute-start.5
  20.4 6.9 %turn_into.1 = (bf16[8,1024,512]{2,1,0:T(8,128)(2,1)S(1)}, f32[8,128]{1,0:T(8,128)S(1)}) custom-call(bf16[8,512,1024]{2,1,0:T(8,128)(2,1)} %bitcast.18, bf16[136,1024]{1,0:T(8,128)(2,1)S(1)} %choose.5.after_ref, bf16[8,1024,512]{2,1,0:T(8,128)(2,1)S(1)} %get-tuple-element.54.held_ref), custom_call_target="tpu_custom_call", output_to_operand_aliasing={{0}: (2, {})} | custom-call | bytes 1024 | tf_op jit(solution)/shard_map/turn_into/pallas_call | solution.py:226
  27.3 2.9 %collective-permute-done.3.right_ref.refs_3_ = bf16[128,1024]{1,0:T(8,128)(2,1)S(1)} collective-permute-done((bf16[128,1024]{1,0:T(8,128)(2,1)S(1)}, bf16[128,1024]{1,0:T(8,128)(2,1)S(1)}, u32[]{:S(2)}, u32[]{:S(2)}) %collective-permute-start.3) | collective-permute-done | bytes 262176 | tf_op jit(solution)/shard_map/ppermute | solution.py:380
  30.2 0.5 collective-permute-start.4
  30.8 1.7 %collective-permute-start.8 = (bf16[128,1024]{1,0:T(8,128)(2,1)S(1)}, bf16[128,1024]{1,0:T(8,128)(2,1)S(1)}, u32[]{:S(2)}, u32[]{:S(2)}) collective-permute-start(bf16[128,1024]{1,0:T(8,128)(2,1)S(1)} %hold.1.refs_0_), channel_id=1, source_target_pairs={{0,1},{1,2},{2,3},{3,0},{4,5},{5,6},{6,7},{7,4},{8,9},{9,10},{10,1... | collective-permute-start | bytes 786440 | tf_op jit(solution)/shard_map/ppermute | solution.py:380
  32.4 2.2 %collective-permute-start.9 = (bf16[128,1024]{1,0:T(8,128)(2,1)S(1)}, bf16[128,1024]{1,0:T(8,128)(2,1)S(1)}, u32[]{:S(2)}, u32[]{:S(2)}) collective-permute-start(bf16[128,1024]{1,0:T(8,128)(2,1)S(1)} %hold.1.refs_0_), channel_id=1, source_target_pairs={{0,3},{1,0},{2,1},{3,2},{4,7},{5,4},{6,5},{7,6},{8,11},{9,8},{10,9... | collective-permute-start | bytes 786440 | tf_op jit(solution)/shard_map/ppermute | solution.py:380
  34.6 1.6 %collective-permute-done.5.refs_2_.refs_6_ = bf16[136,1024]{1,0:T(8,128)(2,1)S(1)} collective-permute-done((bf16[136,1024]{1,0:T(8,128)(2,1)S(1)}, bf16[136,1024]{1,0:T(8,128)(2,1)S(1)}, u32[]{:S(2)}, u32[]{:S(2)}) %collective-permute-start.5) | collective-permute-done | bytes 278560 | tf_op jit(solution)/shard_map/ppermute | solution.py:384
  36.2 6.2 %forward.2 = (f32[8,160,512]{2,1,0:T(8,128)S(1)}, f32[8,160,512]{2,1,0:T(8,128)S(1)}, bf16[2,640,256]{2,1,0:T(8,128)(2,1)S(1)}, bf16[2,256,640]{2,1,0:T(8,128)(2,1)S(1)}, f32[8,128]{1,0:T(8,128)S(1)}) custom-call(s32[1]{0:T(128)} %bitcast.8.refs_0_.base_ref, bf16[136,1024]{1,0:T(8,128)(2,1)S(1)} %get-tuple-element.52.refs_2_.refs_0_.refs_4_, ...), custom_call_target="tpu_custom_call" | custom-call | bytes 1024 | tf_op jit(solution)/shard_map/forward/pallas_call | solution.py:325
  42.4 0.3 collective-permute-done.4.refs_2_
  42.6 4.3 %backward.2 = (bf16[128,512]{1,0:T(8,128)(2,1)S(1)}, bf16[128,512]{1,0:T(8,128)(2,1)S(1)}, bf16[128,512]{1,0:T(8,128)(2,1)S(1)}, bf16[128,512]{1,0:T(8,128)(2,1)...) custom-call(bf16[128,1024]{1,0:T(8,128)(2,1)S(1)} %get-tuple-element.51.refs_0_, ...), custom_call_target="tpu_custom_call" | custom-call | bytes 1024 | tf_op jit(solution)/shard_map/backward/pallas_call | solution.py:355
  46.9 0.7 collective-permute-start.6
  47.8 2.0 %rest.2 = (bf16[128,512]{1,0:T(8,128)(2,1)S(1)}, bf16[128,512]{1,0:T(8,128)(2,1)S(1)}, bf16[128,512]{1,0:T(8,128)(2,1)S(1)}, bf16[128,512]{1,0:T(8,128)(2,1)S(1)}) custom-call(bf16[128,1024]{1,0:T(8,128)(2,1)S(1)} %get-tuple-element.51.refs_0_, bf16[8,160,512]{2,1,0:T(8,128)(2,1)S(1)} %get-tuple-element.69.refs_1_, ...), custom_call_target="tpu_custom_call" | custom-call | bytes 1024 | tf_op jit(solution)/shard_map/rest/pallas_call | solution.py:365
  49.7 2.3 %collective-permute-start.12 = (bf16[128,512]{1,0:T(8,128)(2,1)S(1)}, bf16[128,512]{1,0:T(8,128)(2,1)S(1)}, u32[]{:S(2)}, u32[]{:S(2)}) collective-permute-start(bf16[128,512]{1,0:T(8,128)(2,1)S(1)} %get-tuple-element.71), channel_id=1, source_target_pairs={{0,28},{1,29},{2,30},{3,31},{4,0},{5,1},{6,2},{7,3},{8,4},{9,5},{1... | collective-permute-start | bytes 393224 | tf_op jit(solution)/shard_map/ppermute | solution.py:394
  52.0 1.8 %collective-permute-start.13 = (bf16[128,512]{1,0:T(8,128)(2,1)S(1)}, bf16[128,512]{1,0:T(8,128)(2,1)S(1)}, u32[]{:S(2)}, u32[]{:S(2)}) collective-permute-start(bf16[128,512]{1,0:T(8,128)(2,1)S(1)} %get-tuple-element.72), channel_id=1, source_target_pairs={{0,1},{1,0},{2,3},{3,2},{4,5},{5,4},{6,7},{7,6},{8,9},{9,8},{10,11... | collective-permute-start | bytes 393224 | tf_op jit(solution)/shard_map/ppermute | solution.py:384
  53.8 0.3 collective-permute-start.18
  54.1 1.7 %collective-permute-done.7.far_ref = bf16[128,512]{1,0:T(8,128)(2,1)S(1)} collective-permute-done((bf16[128,512]{1,0:T(8,128)(2,1)S(1)}, bf16[128,512]{1,0:T(8,128)(2,1)S(1)}, u32[]{:S(2)}, u32[]{:S(2)}) %collective-permute-start.7) | collective-permute-done | bytes 131104 | tf_op jit(solution)/shard_map/ppermute | solution.py:384
  55.9 3.3 %collective-permute-start.10 = (bf16[128,512]{1,0:T(8,128)(2,1)S(1)}, bf16[128,512]{1,0:T(8,128)(2,1)S(1)}, u32[]{:S(2)}, u32[]{:S(2)}) collective-permute-start(bf16[128,512]{1,0:T(8,128)(2,1)S(1)} %get-tuple-element.67), channel_id=1, source_target_pairs={{0,31},{1,28},{2,29},{3,30},{4,3},{5,0},{6,1},{7,2},{8,7},{9,4},{1... | collective-permute-start | bytes 393224 | tf_op jit(solution)/shard_map/ppermute | solution.py:394
  59.1 0.4 collective-permute-start.11
  59.6 3.2 %collective-permute-start.14 = (bf16[128,512]{1,0:T(8,128)(2,1)S(1)}, bf16[128,512]{1,0:T(8,128)(2,1)S(1)}, u32[]{:S(2)}, u32[]{:S(2)}) collective-permute-start(bf16[128,512]{1,0:T(8,128)(2,1)S(1)} %get-tuple-element.75), channel_id=1, source_target_pairs={{0,31},{1,28},{2,29},{3,30},{4,3},{5,0},{6,1},{7,2},{8,7},{9,4},{1... | collective-permute-start | bytes 393224 | tf_op jit(solution)/shard_map/ppermute | solution.py:394
  62.8 3.4 %collective-permute-done.10.refs_1_ = bf16[128,512]{1,0:T(8,128)(2,1)S(1)} collective-permute-done((bf16[128,512]{1,0:T(8,128)(2,1)S(1)}, bf16[128,512]{1,0:T(8,128)(2,1)S(1)}, u32[]{:S(2)}, u32[]{:S(2)}) %collective-permute-start.10) | collective-permute-done | bytes 131104 | tf_op jit(solution)/shard_map/ppermute | solution.py:394
  66.2 2.8 %collective-permute-done.11.refs_2_ = bf16[128,512]{1,0:T(8,128)(2,1)S(1)} collective-permute-done((bf16[128,512]{1,0:T(8,128)(2,1)S(1)}, bf16[128,512]{1,0:T(8,128)(2,1)S(1)}, u32[]{:S(2)}, u32[]{:S(2)}) %collective-permute-start.11) | collective-permute-done | bytes 131104 | tf_op jit(solution)/shard_map/ppermute | solution.py:394
  69.1 3.8 %collective-permute-start.19 = (bf16[128,512]{1,0:T(8,128)(2,1)S(1)}, bf16[128,512]{1,0:T(8,128)(2,1)S(1)}, u32[]{:S(2)}, u32[]{:S(2)}) collective-permute-start(bf16[128,512]{1,0:T(8,128)(2,1)S(1)} %sum.2.refs_3_.refs_0_), channel_id=1, source_target_pairs={{0,3},{1,0},{2,1},{3,2},{4,7},{5,4},{6,5},{7,6},{8,11},{9,8},{10,9... | collective-permute-start | bytes 393224 | tf_op jit(solution)/shard_map/ppermute | solution.py:380
  72.9 0.7 collective-permute-done.15.refs_2_
  73.7 3.8 %collective-permute-start.21 = (bf16[128,512]{1,0:T(8,128)(2,1)S(1)}, bf16[128,512]{1,0:T(8,128)(2,1)S(1)}, u32[]{:S(2)}, u32[]{:S(2)}) collective-permute-start(bf16[128,512]{1,0:T(8,128)(2,1)S(1)} %sum.3.refs_1_), channel_id=1, source_target_pairs={{0,3},{1,0},{2,1},{3,2},{4,7},{5,4},{6,5},{7,6},{8,11},{9,8},{10,9... | collective-permute-start | bytes 393224 | tf_op jit(solution)/shard_map/ppermute | solution.py:380
  77.6 6.2 %forward.3 = (f32[8,160,512]{2,1,0:T(8,128)S(1)}, f32[8,160,512]{2,1,0:T(8,128)S(1)}, bf16[2,640,256]{2,1,0:T(8,128)(2,1)S(1)}, bf16[2,256,640]{2,1,0:T(8,128)(2,1)S(1)}, f32[8,128]{1,0:T(8,128)S(1)}) custom-call(s32[1]{0:T(128)} %bitcast.8.refs_0_.base_ref, bf16[128,1024]{1,0:T(8,128)(2,1)S(1)} %hold.1.refs_0_, ...), custom_call_target="tpu_custom_call" | custom-call | bytes 1024 | tf_op jit(solution)/shard_map/forward/pallas_call | solution.py:325
  83.9 2.3 %collective-permute-done.21.right_ref.refs_7_ = bf16[128,512]{1,0:T(8,128)(2,1)S(1)} collective-permute-done((bf16[128,512]{1,0:T(8,128)(2,1)S(1)}, bf16[128,512]{1,0:T(8,128)(2,1)S(1)}, u32[]{:S(2)}, u32[]{:S(2)}) %collective-permute-start.21) | collective-permute-done | bytes 131104 | tf_op jit(solution)/shard_map/ppermute | solution.py:380
  86.4 1.1 collective-permute-start.22
  87.5 1.6 %collective-permute-done.20.refs_4_ = bf16[128,512]{1,0:T(8,128)(2,1)S(1)} collective-permute-done((bf16[128,512]{1,0:T(8,128)(2,1)S(1)}, bf16[128,512]{1,0:T(8,128)(2,1)S(1)}, u32[]{:S(2)}, u32[]{:S(2)}) %collective-permute-start.20) | collective-permute-done | bytes 131104 | tf_op jit(solution)/shard_map/ppermute | solution.py:384
  89.1 3.8 %collective-permute-done.22.refs_5_ = bf16[128,512]{1,0:T(8,128)(2,1)S(1)} collective-permute-done((bf16[128,512]{1,0:T(8,128)(2,1)S(1)}, bf16[128,512]{1,0:T(8,128)(2,1)S(1)}, u32[]{:S(2)}, u32[]{:S(2)}) %collective-permute-start.22) | collective-permute-done | bytes 131104 | tf_op jit(solution)/shard_map/ppermute | solution.py:384
  92.9 4.2 %backward.3 = (f32[128,512]{1,0:T(8,128)S(1)}, bf16[128,512]{1,0:T(8,128)(2,1)S(1)}, bf16[128,512]{1,0:T(8,128)(2,1)S(1)}, bf16[128,512]{1,0:T(8,128)(2,1)S(1)},...) custom-call(bf16[128,512]{1,0:T(8,128)(2,1)S(1)} %sum.2.refs_3_.refs_0_, ...), custom_call_target="tpu_custom_call" | custom-call | bytes 1024 | tf_op jit(solution)/shard_map/backward/pallas_call | solution.py:355
  97.1 0.6 collective-permute-start.26
  97.7 2.0 %rest.3 = (f32[128,512]{1,0:T(8,128)S(1)}, bf16[128,512]{1,0:T(8,128)(2,1)S(1)}, bf16[128,512]{1,0:T(8,128)(2,1)S(1)}, bf16[128,512]{1,0:T(8,128)(2,1)S(1)}) custom-call(bf16[128,512]{1,0:T(8,128)(2,1)S(1)} %sum.2.refs_3_.refs_0_, bf16[128,512]{1,0:T(8,128)(2,1)S(1)} %sum.3.refs_1_, bf16[8,160,512]{2,1,0:T(8,128)(2,1)S(1)} %get-tuple-element.83.refs_2_, ...), custom_call_target="tpu_custom_call" | custom-call | bytes 1024 | tf_op jit(solution)/shard_map/rest/pallas_call | solution.py:365
  99.7 1.6 %collective-permute-start.23 = (bf16[128,512]{1,0:T(8,128)(2,1)S(1)}, bf16[128,512]{1,0:T(8,128)(2,1)S(1)}, u32[]{:S(2)}, u32[]{:S(2)}) collective-permute-start(bf16[128,512]{1,0:T(8,128)(2,1)S(1)} %get-tuple-element.86), channel_id=1, source_target_pairs={{0,1},{1,0},{2,3},{3,2},{4,5},{5,4},{6,7},{7,6},{8,9},{9,8},{10,11... | collective-permute-start | bytes 393224 | tf_op jit(solution)/shard_map/ppermute | solution.py:384
  101.3 2.2 %collective-permute-done.26.far_ref = bf16[128,512]{1,0:T(8,128)(2,1)S(1)} collective-permute-done((bf16[128,512]{1,0:T(8,128)(2,1)S(1)}, bf16[128,512]{1,0:T(8,128)(2,1)S(1)}, u32[]{:S(2)}, u32[]{:S(2)}) %collective-permute-start.26) | collective-permute-done | bytes 131104 | tf_op jit(solution)/shard_map/ppermute | solution.py:384
  103.5 0.5 collective-permute-start.27
  104.0 1.6 %collective-permute-start.28 = (bf16[128,512]{1,0:T(8,128)(2,1)S(1)}, bf16[128,512]{1,0:T(8,128)(2,1)S(1)}, u32[]{:S(2)}, u32[]{:S(2)}) collective-permute-start(bf16[128,512]{1,0:T(8,128)(2,1)S(1)} %get-tuple-element.96), channel_id=1, source_target_pairs={{0,1},{1,2},{2,3},{3,0},{4,5},{5,6},{6,7},{7,4},{8,9},{9,10},{10,1... | collective-permute-start | bytes 393224 | tf_op jit(solution)/shard_map/ppermute | solution.py:380
  105.6 0.7 collective-permute-done.23.far_ref
  106.3 1.6 %collective-permute-start.24 = (bf16[128,512]{1,0:T(8,128)(2,1)S(1)}, bf16[128,512]{1,0:T(8,128)(2,1)S(1)}, u32[]{:S(2)}, u32[]{:S(2)}) collective-permute-start(bf16[128,512]{1,0:T(8,128)(2,1)S(1)} %get-tuple-element.89), channel_id=1, source_target_pairs={{0,3},{1,0},{2,1},{3,2},{4,7},{5,4},{6,5},{7,6},{8,11},{9,8},{10,9... | collective-permute-start | bytes 393224 | tf_op jit(solution)/shard_map/ppermute | solution.py:380
  107.9 0.4 collective-permute-start.25
  108.4 4.1 %collective-permute-done.27.refs_1_ = bf16[128,512]{1,0:T(8,128)(2,1)S(1)} collective-permute-done((bf16[128,512]{1,0:T(8,128)(2,1)S(1)}, bf16[128,512]{1,0:T(8,128)(2,1)S(1)}, u32[]{:S(2)}, u32[]{:S(2)}) %collective-permute-start.27) | collective-permute-done | bytes 131104 | tf_op jit(solution)/shard_map/ppermute | solution.py:380
  112.5 0.7 write.2.refs_3_
  113.2 3.5 %collective-permute-done.24.refs_1_ = bf16[128,512]{1,0:T(8,128)(2,1)S(1)} collective-permute-done((bf16[128,512]{1,0:T(8,128)(2,1)S(1)}, bf16[128,512]{1,0:T(8,128)(2,1)S(1)}, u32[]{:S(2)}, u32[]{:S(2)}) %collective-permute-start.24) | collective-permute-done | bytes 131104 | tf_op jit(solution)/shard_map/ppermute | solution.py:380
  116.8 0.7 write.3
  (35 shorter events, 0.9 us)
Async XLA Ops:
  1.1 18.9 %collective-permute-start.1 = (bf16[136,1024]{1,0:T(8,128)(2,1)S(1)}, bf16[136,1024]{1,0:T(8,128)(2,1)S(1)}, u32[]{:S(2)}, u32[]{:S(2)}) collective-permute-start(bf16[136,1024]{1,0:T(8,128)(2,1)S(1)} %get-tuple-element.52.refs_2_.refs_0_.refs_4_), channel_id=1, source_target_pairs={{0,1},{1,2},{2,3},{3,0},{4,5},{5,6},{6,7},{7,4},{8,9},{9,10},{10,1... | collective-permute-start | bytes 835592 | tf_op jit(solution)/shard_map/ppermute | solution.py:380
  4.2 15.8 %collective-permute-start.2 = (bf16[136,1024]{1,0:T(8,128)(2,1)S(1)}, bf16[136,1024]{1,0:T(8,128)(2,1)S(1)}, u32[]{:S(2)}, u32[]{:S(2)}) collective-permute-start(bf16[136,1024]{1,0:T(8,128)(2,1)S(1)} %get-tuple-element.52.refs_2_.refs_0_.refs_4_), channel_id=1, source_target_pairs={{0,3},{1,0},{2,1},{3,2},{4,7},{5,4},{6,5},{7,6},{8,11},{9,8},{10,9... | collective-permute-start | bytes 835592 | tf_op jit(solution)/shard_map/ppermute | solution.py:380
  6.3 21.0 %collective-permute-start = (bf16[128,1024]{1,0:T(8,128)(2,1)S(1)}, bf16[128,1024]{1,0:T(8,128)(2,1)S(1)}, u32[]{:S(2)}, u32[]{:S(2)}) collective-permute-start(bf16[128,1024]{1,0:T(8,128)(2,1)S(1)} %get-tuple-element.51.refs_0_), channel_id=1, source_target_pairs={{0,1},{1,2},{2,3},{3,0},{4,5},{5,6},{6,7},{7,4},{8,9},{9,10},{10,1... | collective-permute-start | bytes 786440 | tf_op jit(solution)/shard_map/ppermute | solution.py:380
  6.3 23.9 %collective-permute-start.3 = (bf16[128,1024]{1,0:T(8,128)(2,1)S(1)}, bf16[128,1024]{1,0:T(8,128)(2,1)S(1)}, u32[]{:S(2)}, u32[]{:S(2)}) collective-permute-start(bf16[128,1024]{1,0:T(8,128)(2,1)S(1)} %get-tuple-element.51.refs_0_), channel_id=1, source_target_pairs={{0,3},{1,0},{2,1},{3,2},{4,7},{5,4},{6,5},{7,6},{8,11},{9,8},{10,9... | collective-permute-start | bytes 786440 | tf_op jit(solution)/shard_map/ppermute | solution.py:380
  20.0 16.2 %collective-permute-start.5 = (bf16[136,1024]{1,0:T(8,128)(2,1)S(1)}, bf16[136,1024]{1,0:T(8,128)(2,1)S(1)}, u32[]{:S(2)}, u32[]{:S(2)}) collective-permute-start(bf16[136,1024]{1,0:T(8,128)(2,1)S(1)} %choose.5.after_ref), channel_id=1, source_target_pairs={{0,1},{1,0},{2,3},{3,2},{4,5},{5,4},{6,7},{7,6},{8,9},{9,8},{10,11... | collective-permute-start | bytes 835592 | tf_op jit(solution)/shard_map/ppermute | solution.py:384
  20.4 10.3 %copy-start = (bf16[1,2,128,1024]{3,2,1,0:T(8,128)(2,1)S(1)}, bf16[1,2,128,1024]{3,2,1,0:T(8,128)(2,1)}, u32[]{:S(2)}) copy-start(bf16[1,2,128,1024]{3,2,1,0:T(8,128)(2,1)} %param.8) | copy-start | bytes 1572868
  30.2 12.4 %collective-permute-start.4 = (bf16[128,1024]{1,0:T(8,128)(2,1)S(1)}, bf16[128,1024]{1,0:T(8,128)(2,1)S(1)}, u32[]{:S(2)}, u32[]{:S(2)}) collective-permute-start(bf16[128,1024]{1,0:T(8,128)(2,1)S(1)} %choose.6.refs_0_), channel_id=1, source_target_pairs={{0,1},{1,0},{2,3},{3,2},{4,5},{5,4},{6,7},{7,6},{8,9},{9,8},{10,11... | collective-permute-start | bytes 786440 | tf_op jit(solution)/shard_map/ppermute | solution.py:384
  30.8 21.3 %collective-permute-start.8 = (bf16[128,1024]{1,0:T(8,128)(2,1)S(1)}, bf16[128,1024]{1,0:T(8,128)(2,1)S(1)}, u32[]{:S(2)}, u32[]{:S(2)}) collective-permute-start(bf16[128,1024]{1,0:T(8,128)(2,1)S(1)} %hold.1.refs_0_), channel_id=1, source_target_pairs={{0,1},{1,2},{2,3},{3,0},{4,5},{5,6},{6,7},{7,4},{8,9},{9,10},{10,1... | collective-permute-start | bytes 786440 | tf_op jit(solution)/shard_map/ppermute | solution.py:380
  32.4 21.4 %collective-permute-start.9 = (bf16[128,1024]{1,0:T(8,128)(2,1)S(1)}, bf16[128,1024]{1,0:T(8,128)(2,1)S(1)}, u32[]{:S(2)}, u32[]{:S(2)}) collective-permute-start(bf16[128,1024]{1,0:T(8,128)(2,1)S(1)} %hold.1.refs_0_), channel_id=1, source_target_pairs={{0,3},{1,0},{2,1},{3,2},{4,7},{5,4},{6,5},{7,6},{8,11},{9,8},{10,9... | collective-permute-start | bytes 786440 | tf_op jit(solution)/shard_map/ppermute | solution.py:380
  46.9 7.2 %collective-permute-start.6 = (bf16[128,512]{1,0:T(8,128)(2,1)S(1)}, bf16[128,512]{1,0:T(8,128)(2,1)S(1)}, u32[]{:S(2)}, u32[]{:S(2)}) collective-permute-start(bf16[128,512]{1,0:T(8,128)(2,1)S(1)} %get-tuple-element.63), channel_id=1, source_target_pairs={{0,28},{1,29},{2,30},{3,31},{4,0},{5,1},{6,2},{7,3},{8,4},{9,5},{1... | collective-permute-start | bytes 393224 | tf_op jit(solution)/shard_map/ppermute | solution.py:394
  47.7 8.2 %collective-permute-start.7 = (bf16[128,512]{1,0:T(8,128)(2,1)S(1)}, bf16[128,512]{1,0:T(8,128)(2,1)S(1)}, u32[]{:S(2)}, u32[]{:S(2)}) collective-permute-start(bf16[128,512]{1,0:T(8,128)(2,1)S(1)} %get-tuple-element.64), channel_id=1, source_target_pairs={{0,1},{1,0},{2,3},{3,2},{4,5},{5,4},{6,7},{7,6},{8,9},{9,8},{10,11... | collective-permute-start | bytes 393224 | tf_op jit(solution)/shard_map/ppermute | solution.py:384
  49.7 9.8 %collective-permute-start.12 = (bf16[128,512]{1,0:T(8,128)(2,1)S(1)}, bf16[128,512]{1,0:T(8,128)(2,1)S(1)}, u32[]{:S(2)}, u32[]{:S(2)}) collective-permute-start(bf16[128,512]{1,0:T(8,128)(2,1)S(1)} %get-tuple-element.71), channel_id=1, source_target_pairs={{0,28},{1,29},{2,30},{3,31},{4,0},{5,1},{6,2},{7,3},{8,4},{9,5},{1... | collective-permute-start | bytes 393224 | tf_op jit(solution)/shard_map/ppermute | solution.py:394
  52.0 7.6 %collective-permute-start.13 = (bf16[128,512]{1,0:T(8,128)(2,1)S(1)}, bf16[128,512]{1,0:T(8,128)(2,1)S(1)}, u32[]{:S(2)}, u32[]{:S(2)}) collective-permute-start(bf16[128,512]{1,0:T(8,128)(2,1)S(1)} %get-tuple-element.72), channel_id=1, source_target_pairs={{0,1},{1,0},{2,3},{3,2},{4,5},{5,4},{6,7},{7,6},{8,9},{9,8},{10,11... | collective-permute-start | bytes 393224 | tf_op jit(solution)/shard_map/ppermute | solution.py:384
  53.8 23.8 %collective-permute-start.18 = (bf16[128,1024]{1,0:T(8,128)(2,1)S(1)}, bf16[128,1024]{1,0:T(8,128)(2,1)S(1)}, u32[]{:S(2)}, u32[]{:S(2)}) collective-permute-start(bf16[128,1024]{1,0:T(8,128)(2,1)S(1)} %choose.7), channel_id=1, source_target_pairs={{0,1},{1,0},{2,3},{3,2},{4,5},{5,4},{6,7},{7,6},{8,9},{9,8},{10,11... | collective-permute-start | bytes 786440 | tf_op jit(solution)/shard_map/ppermute | solution.py:384
  55.9 10.3 %collective-permute-start.10 = (bf16[128,512]{1,0:T(8,128)(2,1)S(1)}, bf16[128,512]{1,0:T(8,128)(2,1)S(1)}, u32[]{:S(2)}, u32[]{:S(2)}) collective-permute-start(bf16[128,512]{1,0:T(8,128)(2,1)S(1)} %get-tuple-element.67), channel_id=1, source_target_pairs={{0,31},{1,28},{2,29},{3,30},{4,3},{5,0},{6,1},{7,2},{8,7},{9,4},{1... | collective-permute-start | bytes 393224 | tf_op jit(solution)/shard_map/ppermute | solution.py:394
  59.1 9.9 %collective-permute-start.11 = (bf16[128,512]{1,0:T(8,128)(2,1)S(1)}, bf16[128,512]{1,0:T(8,128)(2,1)S(1)}, u32[]{:S(2)}, u32[]{:S(2)}) collective-permute-start(bf16[128,512]{1,0:T(8,128)(2,1)S(1)} %get-tuple-element.68), channel_id=1, source_target_pairs={{0,29},{1,30},{2,31},{3,28},{4,1},{5,2},{6,3},{7,0},{8,5},{9,6},{1... | collective-permute-start | bytes 393224 | tf_op jit(solution)/shard_map/ppermute | solution.py:394
  59.6 13.3 %collective-permute-start.14 = (bf16[128,512]{1,0:T(8,128)(2,1)S(1)}, bf16[128,512]{1,0:T(8,128)(2,1)S(1)}, u32[]{:S(2)}, u32[]{:S(2)}) collective-permute-start(bf16[128,512]{1,0:T(8,128)(2,1)S(1)} %get-tuple-element.75), channel_id=1, source_target_pairs={{0,31},{1,28},{2,29},{3,30},{4,3},{5,0},{6,1},{7,2},{8,7},{9,4},{1... | collective-permute-start | bytes 393224 | tf_op jit(solution)/shard_map/ppermute | solution.py:394
  62.8 10.8 %collective-permute-start.15 = (bf16[128,512]{1,0:T(8,128)(2,1)S(1)}, bf16[128,512]{1,0:T(8,128)(2,1)S(1)}, u32[]{:S(2)}, u32[]{:S(2)}) collective-permute-start(bf16[128,512]{1,0:T(8,128)(2,1)S(1)} %get-tuple-element.76), channel_id=1, source_target_pairs={{0,29},{1,30},{2,31},{3,28},{4,1},{5,2},{6,3},{7,0},{8,5},{9,6},{1... | collective-permute-start | bytes 393224 | tf_op jit(solution)/shard_map/ppermute | solution.py:394
  69.1 14.7 %collective-permute-start.16 = (bf16[128,512]{1,0:T(8,128)(2,1)S(1)}, bf16[128,512]{1,0:T(8,128)(2,1)S(1)}, u32[]{:S(2)}, u32[]{:S(2)}) collective-permute-start(bf16[128,512]{1,0:T(8,128)(2,1)S(1)} %sum.2.refs_3_.refs_0_), channel_id=1, source_target_pairs={{0,1},{1,2},{2,3},{3,0},{4,5},{5,6},{6,7},{7,4},{8,9},{9,10},{10,1... | collective-permute-start | bytes 393224 | tf_op jit(solution)/shard_map/ppermute | solution.py:380
  69.1 14.6 %collective-permute-start.19 = (bf16[128,512]{1,0:T(8,128)(2,1)S(1)}, bf16[128,512]{1,0:T(8,128)(2,1)S(1)}, u32[]{:S(2)}, u32[]{:S(2)}) collective-permute-start(bf16[128,512]{1,0:T(8,128)(2,1)S(1)} %sum.2.refs_3_.refs_0_), channel_id=1, source_target_pairs={{0,3},{1,0},{2,1},{3,2},{4,7},{5,4},{6,5},{7,6},{8,11},{9,8},{10,9... | collective-permute-start | bytes 393224 | tf_op jit(solution)/shard_map/ppermute | solution.py:380
  73.7 10.2 %collective-permute-start.17 = (bf16[128,512]{1,0:T(8,128)(2,1)S(1)}, bf16[128,512]{1,0:T(8,128)(2,1)S(1)}, u32[]{:S(2)}, u32[]{:S(2)}) collective-permute-start(bf16[128,512]{1,0:T(8,128)(2,1)S(1)} %sum.3.refs_1_), channel_id=1, source_target_pairs={{0,1},{1,2},{2,3},{3,0},{4,5},{5,6},{6,7},{7,4},{8,9},{9,10},{10,1... | collective-permute-start | bytes 393224 | tf_op jit(solution)/shard_map/ppermute | solution.py:380
  73.7 12.4 %collective-permute-start.21 = (bf16[128,512]{1,0:T(8,128)(2,1)S(1)}, bf16[128,512]{1,0:T(8,128)(2,1)S(1)}, u32[]{:S(2)}, u32[]{:S(2)}) collective-permute-start(bf16[128,512]{1,0:T(8,128)(2,1)S(1)} %sum.3.refs_1_), channel_id=1, source_target_pairs={{0,3},{1,0},{2,1},{3,2},{4,7},{5,4},{6,5},{7,6},{8,11},{9,8},{10,9... | collective-permute-start | bytes 393224 | tf_op jit(solution)/shard_map/ppermute | solution.py:380
  83.8 5.3 %collective-permute-start.20 = (bf16[128,512]{1,0:T(8,128)(2,1)S(1)}, bf16[128,512]{1,0:T(8,128)(2,1)S(1)}, u32[]{:S(2)}, u32[]{:S(2)}) collective-permute-start(bf16[128,512]{1,0:T(8,128)(2,1)S(1)} %choose.8), channel_id=1, source_target_pairs={{0,1},{1,0},{2,3},{3,2},{4,5},{5,4},{6,7},{7,6},{8,9},{9,8},{10,11... | collective-permute-start | bytes 393224 | tf_op jit(solution)/shard_map/ppermute | solution.py:384
  86.4 6.5 %collective-permute-start.22 = (bf16[128,512]{1,0:T(8,128)(2,1)S(1)}, bf16[128,512]{1,0:T(8,128)(2,1)S(1)}, u32[]{:S(2)}, u32[]{:S(2)}) collective-permute-start(bf16[128,512]{1,0:T(8,128)(2,1)S(1)} %choose.9), channel_id=1, source_target_pairs={{0,1},{1,0},{2,3},{3,2},{4,5},{5,4},{6,7},{7,6},{8,9},{9,8},{10,11... | collective-permute-start | bytes 393224 | tf_op jit(solution)/shard_map/ppermute | solution.py:384
  97.1 6.3 %collective-permute-start.26 = (bf16[128,512]{1,0:T(8,128)(2,1)S(1)}, bf16[128,512]{1,0:T(8,128)(2,1)S(1)}, u32[]{:S(2)}, u32[]{:S(2)}) collective-permute-start(bf16[128,512]{1,0:T(8,128)(2,1)S(1)} %get-tuple-element.92), channel_id=1, source_target_pairs={{0,1},{1,0},{2,3},{3,2},{4,5},{5,4},{6,7},{7,6},{8,9},{9,8},{10,11... | collective-permute-start | bytes 393224 | tf_op jit(solution)/shard_map/ppermute | solution.py:384
  99.7 6.6 %collective-permute-start.23 = (bf16[128,512]{1,0:T(8,128)(2,1)S(1)}, bf16[128,512]{1,0:T(8,128)(2,1)S(1)}, u32[]{:S(2)}, u32[]{:S(2)}) collective-permute-start(bf16[128,512]{1,0:T(8,128)(2,1)S(1)} %get-tuple-element.86), channel_id=1, source_target_pairs={{0,1},{1,0},{2,3},{3,2},{4,5},{5,4},{6,7},{7,6},{8,9},{9,8},{10,11... | collective-permute-start | bytes 393224 | tf_op jit(solution)/shard_map/ppermute | solution.py:384
  103.5 9.0 %collective-permute-start.27 = (bf16[128,512]{1,0:T(8,128)(2,1)S(1)}, bf16[128,512]{1,0:T(8,128)(2,1)S(1)}, u32[]{:S(2)}, u32[]{:S(2)}) collective-permute-start(bf16[128,512]{1,0:T(8,128)(2,1)S(1)} %get-tuple-element.95), channel_id=1, source_target_pairs={{0,3},{1,0},{2,1},{3,2},{4,7},{5,4},{6,5},{7,6},{8,11},{9,8},{10,9... | collective-permute-start | bytes 393224 | tf_op jit(solution)/shard_map/ppermute | solution.py:380
  104.0 8.5 %collective-permute-start.28 = (bf16[128,512]{1,0:T(8,128)(2,1)S(1)}, bf16[128,512]{1,0:T(8,128)(2,1)S(1)}, u32[]{:S(2)}, u32[]{:S(2)}) collective-permute-start(bf16[128,512]{1,0:T(8,128)(2,1)S(1)} %get-tuple-element.96), channel_id=1, source_target_pairs={{0,1},{1,2},{2,3},{3,0},{4,5},{5,6},{6,7},{7,4},{8,9},{9,10},{10,1... | collective-permute-start | bytes 393224 | tf_op jit(solution)/shard_map/ppermute | solution.py:380
  106.3 10.5 %collective-permute-start.24 = (bf16[128,512]{1,0:T(8,128)(2,1)S(1)}, bf16[128,512]{1,0:T(8,128)(2,1)S(1)}, u32[]{:S(2)}, u32[]{:S(2)}) collective-permute-start(bf16[128,512]{1,0:T(8,128)(2,1)S(1)} %get-tuple-element.89), channel_id=1, source_target_pairs={{0,3},{1,0},{2,1},{3,2},{4,7},{5,4},{6,5},{7,6},{8,11},{9,8},{10,9... | collective-permute-start | bytes 393224 | tf_op jit(solution)/shard_map/ppermute | solution.py:380
  107.9 8.8 %collective-permute-start.25 = (bf16[128,512]{1,0:T(8,128)(2,1)S(1)}, bf16[128,512]{1,0:T(8,128)(2,1)S(1)}, u32[]{:S(2)}, u32[]{:S(2)}) collective-permute-start(bf16[128,512]{1,0:T(8,128)(2,1)S(1)} %get-tuple-element.90), channel_id=1, source_target_pairs={{0,1},{1,2},{2,3},{3,0},{4,5},{5,6},{6,7},{7,4},{8,9},{9,10},{10,1... | collective-permute-start | bytes 393224 | tf_op jit(solution)/shard_map/ppermute | solution.py:380

commit v7 on v6

--- a/solution.py
+++ b/solution.py
@@ -31,6 +31,7 @@
     else:
         meta_refs = x_refs
     gate_ref, up_ref, a_ref, b_ref, pick_ref, place_ref, done_ref, rows_ref, weight_ref = refs
+    count = a_ref.shape[0]
     top = x_refs[0].shape[1] // tokens
 
     mine = lax.broadcasted_iota(jnp.int32, (local, tokens), 0).astype(F32) + base_ref[0].astype(F32)
@@ -68,15 +69,23 @@
             block = jnp.where(picked[e * PAIR : (e + 1) * PAIR], weight[e : e + 1], 0.0)
             weight_ref[e, pair * PAIR : (pair + 1) * PAIR, :] = jnp.sum(block, axis=1, keepdims=True)
     pick_rows(x_refs, tokens, pick_ref, rows_ref)
-    for e in range(local):
+    write_factors(0, count, rows_ref, weight_ref, gate_ref, up_ref, a_ref, b_ref)
+    done_ref[...] = jnp.zeros_like(done_ref)
+
+
+def write_factors(first, count, rows_ref, weight_ref, gate_ref, up_ref, a_ref, b_ref):
+    for e in range(first, first + count):
         rows = rows_ref[e]
         gate = dot(rows, gate_ref[e], ((1,), (1,)))
         up = dot(rows, up_ref[e], ((1,), (1,)))
         sig = 1.0 / (1.0 + jnp.exp(-gate))
         scaled = sig * weight_ref[e]
-        a_ref[e] = up * scaled * (1.0 + gate * (1.0 - sig))
-        b_ref[e] = gate * scaled
-    done_ref[...] = jnp.zeros_like(done_ref)
+        a_ref[e - first] = up * scaled * (1.0 + gate * (1.0 - sig))
+        b_ref[e - first] = gate * scaled
+
+
+def further_kernel(first, rows_ref, weight_ref, gate_ref, up_ref, after_ref, a_ref, b_ref):
+    write_factors(first, a_ref.shape[0], rows_ref, weight_ref, gate_ref, up_ref, a_ref, b_ref)
 
 
 def pick_rows(source_refs, tokens, pick_ref, rows_ref):
@@ -131,16 +140,18 @@
                 out[:, n:stop] = part.astype(out.dtype)
 
 
-def backward_kernel(sources, pieces, columns, *refs):
+def backward_kernel(sources, pieces, blocks, columns, *refs):
     g_refs, refs = refs[: sources * pieces], refs[sources * pieces :]
-    a_ref, b_ref, pick_ref, place_ref, gate_ref, up_ref, down_ref = refs[:7]
-    out_refs, refs = refs[7 : 7 + sources], refs[7 + sources :]
+    a_refs, b_refs, refs = refs[:blocks], refs[blocks : 2 * blocks], refs[2 * blocks :]
+    pick_ref, place_ref, gate_ref, up_ref, down_ref = refs[:5]
+    out_refs, refs = refs[5 : 5 + sources], refs[5 + sources :]
     gate_grad_ref, up_grad_ref, rows_ref, back_ref = refs
     pick_pieces(sources, pieces, g_refs, pick_ref, rows_ref)
     for e in range(rows_ref.shape[0]):
         hidden = dot(rows_ref[e], down_ref[e], ((1,), (0,)))
-        gate_grad_ref[e] = (hidden * a_ref[e]).astype(BF16)
-        up_grad_ref[e] = (hidden * b_ref[e]).astype(BF16)
+        block, place = divmod(e, rows_ref.shape[0] // blocks)
+        gate_grad_ref[e] = (hidden * a_refs[block][place]).astype(BF16)
+        up_grad_ref[e] = (hidden * b_refs[block][place]).astype(BF16)
     row_piece(g_refs[:pieces], gate_grad_ref, up_grad_ref, place_ref, gate_ref, up_ref, out_refs, back_ref, columns)
 
 
@@ -316,34 +327,49 @@
     )(*near(value, *after))
 
 
-def forward(step, who, tokens, xs, metas, gate, up):
+def forward(step, who, tokens, xs, metas, gate, up, count):
     sources, local = len(xs), gate.shape[0]
     width = xs[0].shape[1]
     hidden = gate.shape[1]
     rows = sources * MOST
     arrays = (*xs, *metas, gate, up) if step else (*xs, gate, up)
-    return pl.pallas_call(
+    kept = (pltpu.VMEM((local, rows, width), BF16), pltpu.VMEM((local, rows, 1), F32))
+    shared = kept if count < local else ()
+    a, b, pick, place, done, *others = pl.pallas_call(
         functools.partial(forward_kernel, sources, local, tokens, step),
         in_specs=[pl.BlockSpec(memory_space=pltpu.SMEM)] + [VMEM] * len(arrays),
-        out_specs=(VMEM,) * 5,
+        out_specs=(VMEM,) * (5 + len(shared)),
         out_shape=(
-            pltpu.VMEM((local, rows, hidden), F32),
-            pltpu.VMEM((local, rows, hidden), F32),
+            pltpu.VMEM((count, rows, hidden), F32),
+            pltpu.VMEM((count, rows, hidden), F32),
             pltpu.VMEM((sources // 2, local * PAIR, 2 * tokens), BF16),
             pltpu.VMEM((sources // 2, 2 * tokens, local * PAIR), BF16),
             DONE,
+            *shared,
         ),
-        scratch_shapes=[
-            pltpu.VMEM((local, rows, width), BF16),
-            pltpu.VMEM((local, rows, 1), F32),
-        ],
+        scratch_shapes=[] if shared else list(kept),
         compiler_params=pltpu.CompilerParams(vmem_limit_bytes=9 * MIB),
         cost_estimate=SMALL,
         name="forward",
     )(who[0], *near(*arrays))
-
-
-def backward(cut, kept_type, gs, a, b, pick, place, gate, up, down):
+    return [a], [b], (pick, place), (*others, gate, up), done
+
+
+def further(count, picked, weight, gate, up, after):
+    local, rows = picked.shape[:2]
+    shape = (local - count, rows, gate.shape[1])
+    return pl.pallas_call(
+        functools.partial(further_kernel, count),
+        in_specs=[VMEM] * 5,
+        out_specs=(VMEM,) * 2,
+        out_shape=(pltpu.VMEM(shape, F32),) * 2,
+        compiler_params=pltpu.CompilerParams(vmem_limit_bytes=6 * MIB),
+        cost_estimate=SMALL,
+        name="further",
+    )(*near(picked, weight, gate, up, after))
+
+
+def backward(cut, kept_type, gs, factors_a, factors_b, pick, place, gate, up, down):
     sources, pieces, local = len(gs), len(gs[0]), gate.shape[0]
     tokens = gs[0][0].shape[0]
     hidden, width = gate.shape[1:]
@@ -353,15 +379,15 @@
     factor = pltpu.VMEM((local, rows, hidden), BF16)
     backs = [pltpu.VMEM((sources // 2, local, PAIR, w), BF16) for w in (cut, width - cut)]
     *first, gate_grad, up_grad = pl.pallas_call(
-        functools.partial(backward_kernel, sources, pieces, slice(0, cut)),
-        in_specs=[VMEM] * (sources * pieces + 7),
+        functools.partial(backward_kernel, sources, pieces, len(factors_a), slice(0, cut)),
+        in_specs=[VMEM] * (sources * pieces + 2 * len(factors_a) + 5),
         out_specs=(VMEM,) * (sources + 2),
         out_shape=outs[0] + (factor, factor),
         scratch_shapes=[pltpu.VMEM((local, rows, width), BF16), backs[0]],
         compiler_params=pltpu.CompilerParams(vmem_limit_bytes=11 * MIB),
         cost_estimate=SMALL,
         name="backward",
-    )(*near(*[g for block in gs for g in block], a, b, pick, place, gate, up, down))
+    )(*near(*[g for block in gs for g in block], *factors_a, *factors_b, pick, place, gate, up, down))
     rest = pl.pallas_call(
         functools.partial(rest_kernel, sources, pieces, slice(cut, width)),
         in_specs=[VMEM] * (pieces + 5),
@@ -483,15 +509,20 @@
     gs = [[g] for g in gs]
     for step in range(steps):
         last = step + 1 == steps
-        *factors, done = forward(step, who, tokens, xs, metas, back[0], back[1])
+        count = local // 2 if step and ringed else local
+        a, b, tables, others, done = forward(step, who, tokens, xs, metas, back[0], back[1], count)
         if step:
-            gs = [list(block) for block in zip(*[gathered_far(who, g, done)[0] for g in gs])]
+            pieces = [gathered_far(who, g, done) for g in gs]
+            gs = [list(block) for block in zip(*[piece for piece, _ in pieces])]
+        if count < local:
+            more_a, more_b = further(count, *others, pieces[-1][1])
+            a, b = a + [more_a], b + [more_b]
         beside = ()
         if not last:
             following = held(saved_inputs[0], step + 1, passed) if ringed else saved_inputs[0, step + 1]
             xs = gathered_near(following)
             beside = xs[1::2] if ringed else ()
-        halves = backward(CUTS[last], F32 if last else BF16, gs, *factors, *back)
+        halves = backward(CUTS[last], F32 if last else BF16, gs, a, b, *tables, *back)
         owns = [parts[0] if last else moved_back(parts[0], 0) for parts in halves]
         sent = []
         for own, parts in zip(owns, halves):

time: 118 us -> 118 us (level)
  waiting for transfers between devices: 31.6 us -> 30.2 us
    ppermute x9, waiting for transfers between devices: 11.8 us -> 8.22 us  [swapped(): lax.ppermute(value, 'expert', [(i, i ^ 1) for i in range(lax.axis_size('e...]
    pallas_call x2 -> x3, Pallas kernels: 8.52 us -> 11.5 us  [the longest x2 8.39 us: backward(): pl.pallas_call(functools.partial(backward_kernel, sources, pieces, len(fa...]
    pallas_call x2, Pallas kernels: 12.4 us -> 10.1 us  [forward(): pl.pallas_call(functools.partial(forward_kernel, sources, local, tokens,...]
    ppermute x14, waiting for transfers between devices: 12.9 us -> 15.1 us  [moved(): lax.ppermute(value, 'expert', [(i, (i + by) % count) for i in range(count)])]
  transfers between devices with their start and end apart: 29 -> 29, of which waited for: 14 -> 16; matrix products, arithmetic and copies ran while one was open for 0% -> 0% of each run, Pallas kernels for 33% -> 34%
where the time goes in v7:
time: 118 us
  Pallas kernels  45.3 us (38%)
  starting transfers between devices  41.6 us (35%)
  waiting for transfers between devices  30.2 us (26%)
    ppermute x14, starting transfers between devices, moved(): lax.ppermute(value, 'expert', [(i, (i + by) % count) for i in range(count)])  24.8 us
    ppermute x14, waiting for transfers between devices, moved(): lax.ppermute(value, 'expert', [(i, (i + by) % count) for i in range(count)])  15.1 us
    pallas_call x2, Pallas kernels, forward(): pl.pallas_call(functools.partial(forward_kernel, sources, local, tokens,...  10.1 us
    pallas_call x1, Pallas kernels, turned(): pl.pallas_call(functools.partial(turn_kernel, len(weights) - 1), grid=(lo...  9.87 us
    ppermute x6, starting transfers between devices, moved_back(): return lax.ppermute(value, ('section', 'expert'), pairs)  9.83 us
    pallas_call x2, Pallas kernels, backward(): pl.pallas_call(functools.partial(backward_kernel, sources, pieces, len(fa...  8.39 us
    ppermute x9, waiting for transfers between devices, swapped(): lax.ppermute(value, 'expert', [(i, i ^ 1) for i in range(lax.axis_size('e...  8.22 us
    ppermute x9, starting transfers between devices, swapped(): lax.ppermute(value, 'expert', [(i, i ^ 1) for i in range(lax.axis_size('e...  6.97 us
  transfers between devices with their start and end apart: 29, of which 16 were waited for; matrix products, arithmetic and copies ran while one was open for 0% of the time, Pallas kernels for 34%

profile of v7, /device:TPU:0, one launch (start us, length us, event | category | flops | bytes accessed | tf_op | source)
XLA Modules:
  0.0 117.6 jit_solution(234105357806598042)
XLA Ops:
  0.0 1.1 first.1
  1.1 3.1 %collective-permute-start.1 = (bf16[136,1024]{1,0:T(8,128)(2,1)S(1)}, bf16[136,1024]{1,0:T(8,128)(2,1)S(1)}, u32[]{:S(2)}, u32[]{:S(2)}) collective-permute-start(bf16[136,1024]{1,0:T(8,128)(2,1)S(1)} %get-tuple-element.56.refs_2_.refs_0_.refs_4_), channel_id=1, source_target_pairs={{0,1},{1,2},{2,3},{3,0},{4,5},{5,6},{6,7},{7,4},{8,9},{9,10},{10,1... | collective-permute-start | bytes 835592 | tf_op jit(solution)/shard_map/ppermute | solution.py:406
  4.2 2.1 %collective-permute-start.2 = (bf16[136,1024]{1,0:T(8,128)(2,1)S(1)}, bf16[136,1024]{1,0:T(8,128)(2,1)S(1)}, u32[]{:S(2)}, u32[]{:S(2)}) collective-permute-start(bf16[136,1024]{1,0:T(8,128)(2,1)S(1)} %get-tuple-element.56.refs_2_.refs_0_.refs_4_), channel_id=1, source_target_pairs={{0,3},{1,0},{2,1},{3,2},{4,7},{5,4},{6,5},{7,6},{8,11},{9,8},{10,9... | collective-permute-start | bytes 835592 | tf_op jit(solution)/shard_map/ppermute | solution.py:406
  6.3 3.8 %collective-permute-start.3 = (bf16[128,1024]{1,0:T(8,128)(2,1)S(1)}, bf16[128,1024]{1,0:T(8,128)(2,1)S(1)}, u32[]{:S(2)}, u32[]{:S(2)}) collective-permute-start(bf16[128,1024]{1,0:T(8,128)(2,1)S(1)} %get-tuple-element.55.refs_0_), channel_id=1, source_target_pairs={{0,3},{1,0},{2,1},{3,2},{4,7},{5,4},{6,5},{7,6},{8,11},{9,8},{10,9... | collective-permute-start | bytes 786440 | tf_op jit(solution)/shard_map/ppermute | solution.py:406
  10.1 9.9 %turn.1 = (bf16[8,512,1024]{2,1,0:T(8,128)(2,1)S(1)}, bf16[8,512,1024]{2,1,0:T(8,128)(2,1)S(1)}, bf16[8,1024,512]{2,1,0:T(8,128)(2,1)S(1)}, f32[8,128]{1,0:T(8,128)S(1)}) custom-call(s32[1]{0:T(128)} %bitcast.8.refs_0_.base_ref, s32[1]{0:T(128)} %bitcast.6.refs_1_.odd_ref, bf16[136,1024]{1,0:T(8,128)(2,1)S(1)} %get-tuple-element.56.refs_2_.refs_0_.refs_4_, ...), custom_call_target="tpu_custom_call" | custom-call | bytes 1024 | tf_op jit(solution)/shard_map/turn/pallas_call | solution.py:224
  20.4 6.9 %turn_into.1 = (bf16[8,1024,512]{2,1,0:T(8,128)(2,1)S(1)}, f32[8,128]{1,0:T(8,128)S(1)}) custom-call(bf16[8,512,1024]{2,1,0:T(8,128)(2,1)} %bitcast.20, bf16[136,1024]{1,0:T(8,128)(2,1)S(1)} %choose.5.after_ref, bf16[8,1024,512]{2,1,0:T(8,128)(2,1)S(1)} %get-tuple-element.58.held_ref), custom_call_target="tpu_custom_call", output_to_operand_aliasing={{0}: (2, {})} | custom-call | bytes 1024 | tf_op jit(solution)/shard_map/turn_into/pallas_call | solution.py:237
  27.3 2.9 %collective-permute-done.3.right_ref.refs_3_ = bf16[128,1024]{1,0:T(8,128)(2,1)S(1)} collective-permute-done((bf16[128,1024]{1,0:T(8,128)(2,1)S(1)}, bf16[128,1024]{1,0:T(8,128)(2,1)S(1)}, u32[]{:S(2)}, u32[]{:S(2)}) %collective-permute-start.3) | collective-permute-done | bytes 262176 | tf_op jit(solution)/shard_map/ppermute | solution.py:406
  30.2 0.5 collective-permute-start.4
  30.8 1.7 %collective-permute-start.8 = (bf16[128,1024]{1,0:T(8,128)(2,1)S(1)}, bf16[128,1024]{1,0:T(8,128)(2,1)S(1)}, u32[]{:S(2)}, u32[]{:S(2)}) collective-permute-start(bf16[128,1024]{1,0:T(8,128)(2,1)S(1)} %hold.1.refs_0_), channel_id=1, source_target_pairs={{0,1},{1,2},{2,3},{3,0},{4,5},{5,6},{6,7},{7,4},{8,9},{9,10},{10,1... | collective-permute-start | bytes 786440 | tf_op jit(solution)/shard_map/ppermute | solution.py:406
  32.4 2.2 %collective-permute-start.9 = (bf16[128,1024]{1,0:T(8,128)(2,1)S(1)}, bf16[128,1024]{1,0:T(8,128)(2,1)S(1)}, u32[]{:S(2)}, u32[]{:S(2)}) collective-permute-start(bf16[128,1024]{1,0:T(8,128)(2,1)S(1)} %hold.1.refs_0_), channel_id=1, source_target_pairs={{0,3},{1,0},{2,1},{3,2},{4,7},{5,4},{6,5},{7,6},{8,11},{9,8},{10,9... | collective-permute-start | bytes 786440 | tf_op jit(solution)/shard_map/ppermute | solution.py:406
  34.6 1.6 %collective-permute-done.5.refs_2_.refs_6_ = bf16[136,1024]{1,0:T(8,128)(2,1)S(1)} collective-permute-done((bf16[136,1024]{1,0:T(8,128)(2,1)S(1)}, bf16[136,1024]{1,0:T(8,128)(2,1)S(1)}, u32[]{:S(2)}, u32[]{:S(2)}) %collective-permute-start.5) | collective-permute-done | bytes 278560 | tf_op jit(solution)/shard_map/ppermute | solution.py:410
  36.2 6.2 %forward.2 = (f32[8,160,512]{2,1,0:T(8,128)S(1)}, f32[8,160,512]{2,1,0:T(8,128)S(1)}, bf16[2,640,256]{2,1,0:T(8,128)(2,1)S(1)}, bf16[2,256,640]{2,1,0:T(8,128)(2,1)S(1)}, f32[8,128]{1,0:T(8,128)S(1)}) custom-call(s32[1]{0:T(128)} %bitcast.8.refs_0_.base_ref, bf16[136,1024]{1,0:T(8,128)(2,1)S(1)} %get-tuple-element.56.refs_2_.refs_0_.refs_4_, ...), custom_call_target="tpu_custom_call" | custom-call | bytes 1024 | tf_op jit(solution)/shard_map/forward/pallas_call | solution.py:338
  42.6 4.3 %backward.2 = (bf16[128,512]{1,0:T(8,128)(2,1)S(1)}, bf16[128,512]{1,0:T(8,128)(2,1)S(1)}, bf16[128,512]{1,0:T(8,128)(2,1)S(1)}, bf16[128,512]{1,0:T(8,128)(2,1)...) custom-call(bf16[128,1024]{1,0:T(8,128)(2,1)S(1)} %get-tuple-element.55.refs_0_, ...), custom_call_target="tpu_custom_call" | custom-call | bytes 1024 | tf_op jit(solution)/shard_map/backward/pallas_call | solution.py:381
  46.9 0.7 collective-permute-start.6
  47.8 2.0 %rest.2 = (bf16[128,512]{1,0:T(8,128)(2,1)S(1)}, bf16[128,512]{1,0:T(8,128)(2,1)S(1)}, bf16[128,512]{1,0:T(8,128)(2,1)S(1)}, bf16[128,512]{1,0:T(8,128)(2,1)S(1)}) custom-call(bf16[128,1024]{1,0:T(8,128)(2,1)S(1)} %get-tuple-element.55.refs_0_, bf16[8,160,512]{2,1,0:T(8,128)(2,1)S(1)} %get-tuple-element.73.refs_1_, ...), custom_call_target="tpu_custom_call" | custom-call | bytes 1024 | tf_op jit(solution)/shard_map/rest/pallas_call | solution.py:391
  49.8 2.3 %collective-permute-start.12 = (bf16[128,512]{1,0:T(8,128)(2,1)S(1)}, bf16[128,512]{1,0:T(8,128)(2,1)S(1)}, u32[]{:S(2)}, u32[]{:S(2)}) collective-permute-start(bf16[128,512]{1,0:T(8,128)(2,1)S(1)} %get-tuple-element.75), channel_id=1, source_target_pairs={{0,28},{1,29},{2,30},{3,31},{4,0},{5,1},{6,2},{7,3},{8,4},{9,5},{1... | collective-permute-start | bytes 393224 | tf_op jit(solution)/shard_map/ppermute | solution.py:420
  52.0 1.7 %collective-permute-start.13 = (bf16[128,512]{1,0:T(8,128)(2,1)S(1)}, bf16[128,512]{1,0:T(8,128)(2,1)S(1)}, u32[]{:S(2)}, u32[]{:S(2)}) collective-permute-start(bf16[128,512]{1,0:T(8,128)(2,1)S(1)} %get-tuple-element.76), channel_id=1, source_target_pairs={{0,1},{1,0},{2,3},{3,2},{4,5},{5,4},{6,7},{7,6},{8,9},{9,8},{10,11... | collective-permute-start | bytes 393224 | tf_op jit(solution)/shard_map/ppermute | solution.py:410
  54.2 1.7 %collective-permute-done.7.far_ref = bf16[128,512]{1,0:T(8,128)(2,1)S(1)} collective-permute-done((bf16[128,512]{1,0:T(8,128)(2,1)S(1)}, bf16[128,512]{1,0:T(8,128)(2,1)S(1)}, u32[]{:S(2)}, u32[]{:S(2)}) %collective-permute-start.7) | collective-permute-done | bytes 131104 | tf_op jit(solution)/shard_map/ppermute | solution.py:410
  55.9 3.3 %collective-permute-start.10 = (bf16[128,512]{1,0:T(8,128)(2,1)S(1)}, bf16[128,512]{1,0:T(8,128)(2,1)S(1)}, u32[]{:S(2)}, u32[]{:S(2)}) collective-permute-start(bf16[128,512]{1,0:T(8,128)(2,1)S(1)} %get-tuple-element.71), channel_id=1, source_target_pairs={{0,31},{1,28},{2,29},{3,30},{4,3},{5,0},{6,1},{7,2},{8,7},{9,4},{1... | collective-permute-start | bytes 393224 | tf_op jit(solution)/shard_map/ppermute | solution.py:420
  59.1 0.4 collective-permute-start.11
  59.6 3.2 %collective-permute-start.14 = (bf16[128,512]{1,0:T(8,128)(2,1)S(1)}, bf16[128,512]{1,0:T(8,128)(2,1)S(1)}, u32[]{:S(2)}, u32[]{:S(2)}) collective-permute-start(bf16[128,512]{1,0:T(8,128)(2,1)S(1)} %get-tuple-element.79), channel_id=1, source_target_pairs={{0,31},{1,28},{2,29},{3,30},{4,3},{5,0},{6,1},{7,2},{8,7},{9,4},{1... | collective-permute-start | bytes 393224 | tf_op jit(solution)/shard_map/ppermute | solution.py:420
  62.8 3.4 %collective-permute-done.10.refs_1_ = bf16[128,512]{1,0:T(8,128)(2,1)S(1)} collective-permute-done((bf16[128,512]{1,0:T(8,128)(2,1)S(1)}, bf16[128,512]{1,0:T(8,128)(2,1)S(1)}, u32[]{:S(2)}, u32[]{:S(2)}) %collective-permute-start.10) | collective-permute-done | bytes 131104 | tf_op jit(solution)/shard_map/ppermute | solution.py:420
  66.2 2.8 %collective-permute-done.11.refs_2_ = bf16[128,512]{1,0:T(8,128)(2,1)S(1)} collective-permute-done((bf16[128,512]{1,0:T(8,128)(2,1)S(1)}, bf16[128,512]{1,0:T(8,128)(2,1)S(1)}, u32[]{:S(2)}, u32[]{:S(2)}) %collective-permute-start.11) | collective-permute-done | bytes 131104 | tf_op jit(solution)/shard_map/ppermute | solution.py:420
  69.1 3.8 %collective-permute-start.19 = (bf16[128,512]{1,0:T(8,128)(2,1)S(1)}, bf16[128,512]{1,0:T(8,128)(2,1)S(1)}, u32[]{:S(2)}, u32[]{:S(2)}) collective-permute-start(bf16[128,512]{1,0:T(8,128)(2,1)S(1)} %sum.2.refs_3_.refs_0_), channel_id=1, source_target_pairs={{0,3},{1,0},{2,1},{3,2},{4,7},{5,4},{6,5},{7,6},{8,11},{9,8},{10,9... | collective-permute-start | bytes 393224 | tf_op jit(solution)/shard_map/ppermute | solution.py:406
  72.9 0.7 collective-permute-done.15.refs_2_
  73.7 3.8 %collective-permute-start.21 = (bf16[128,512]{1,0:T(8,128)(2,1)S(1)}, bf16[128,512]{1,0:T(8,128)(2,1)S(1)}, u32[]{:S(2)}, u32[]{:S(2)}) collective-permute-start(bf16[128,512]{1,0:T(8,128)(2,1)S(1)} %sum.3.refs_1_), channel_id=1, source_target_pairs={{0,3},{1,0},{2,1},{3,2},{4,7},{5,4},{6,5},{7,6},{8,11},{9,8},{10,9... | collective-permute-start | bytes 393224 | tf_op jit(solution)/shard_map/ppermute | solution.py:406
  77.5 3.9 %forward.3 = (f32[4,160,512]{2,1,0:T(8,128)S(1)}, f32[4,160,512]{2,1,0:T(8,128)S(1)}, bf16[2,640,256]{2,1,0:T(8,128)(2,1)S(1)}, bf16[2,256,640]{2,1,0:T(8,128)(2...) custom-call(s32[1]{0:T(128)} %bitcast.8.refs_0_.base_ref, ...), custom_call_target="tpu_custom_call" | custom-call | bytes 1024 | tf_op jit(solution)/shard_map/forward/pallas_call | solution.py:338
  81.5 0.6 collective-permute-start.20
  82.1 1.4 %collective-permute-done.17.left_ref.refs_3_ = bf16[128,512]{1,0:T(8,128)(2,1)S(1)} collective-permute-done((bf16[128,512]{1,0:T(8,128)(2,1)S(1)}, bf16[128,512]{1,0:T(8,128)(2,1)S(1)}, u32[]{:S(2)}, u32[]{:S(2)}) %collective-permute-start.17) | collective-permute-done | bytes 131104 | tf_op jit(solution)/shard_map/ppermute | solution.py:406
  83.5 2.6 %collective-permute-done.21.right_ref.refs_7_ = bf16[128,512]{1,0:T(8,128)(2,1)S(1)} collective-permute-done((bf16[128,512]{1,0:T(8,128)(2,1)S(1)}, bf16[128,512]{1,0:T(8,128)(2,1)S(1)}, u32[]{:S(2)}, u32[]{:S(2)}) %collective-permute-start.21) | collective-permute-done | bytes 131104 | tf_op jit(solution)/shard_map/ppermute | solution.py:406
  86.4 1.1 collective-permute-start.22
  87.5 3.1 %further.1 = (f32[4,160,512]{2,1,0:T(8,128)S(1)}, f32[4,160,512]{2,1,0:T(8,128)S(1)}) custom-call(bf16[8,160,1024]{2,1,0:T(8,128)(2,1)S(1)} %get-tuple-element.84.rows_ref, f32[8,160,1]{2,1,0:T(8,128)S(1)} %get-tuple-element.85.weight_ref, bf16[8,512,1024]{2,1,0:T(8,128)(2,1)S(1)} %get-tuple-element.60.refs_4_.refs_8_.gate_ref.refs_14_.refs_5_, ...), custom_call_target="tpu_custom_call" | custom-call | bytes 1024 | tf_op jit(solution)/shard_map/further/pallas_call | solution.py:361
  90.7 1.9 %collective-permute-done.22.refs_5_ = bf16[128,512]{1,0:T(8,128)(2,1)S(1)} collective-permute-done((bf16[128,512]{1,0:T(8,128)(2,1)S(1)}, bf16[128,512]{1,0:T(8,128)(2,1)S(1)}, u32[]{:S(2)}, u32[]{:S(2)}) %collective-permute-start.22) | collective-permute-done | bytes 131104 | tf_op jit(solution)/shard_map/ppermute | solution.py:410
  92.5 4.1 %backward.3 = (f32[128,512]{1,0:T(8,128)S(1)}, bf16[128,512]{1,0:T(8,128)(2,1)S(1)}, bf16[128,512]{1,0:T(8,128)(2,1)S(1)}, bf16[128,512]{1,0:T(8,128)(2,1)S(1)},...) custom-call(bf16[128,512]{1,0:T(8,128)(2,1)S(1)} %sum.2.refs_3_.refs_0_, ...), custom_call_target="tpu_custom_call" | custom-call | bytes 1024 | tf_op jit(solution)/shard_map/backward/pallas_call | solution.py:381
  96.6 0.6 collective-permute-start.26
  97.2 2.0 %rest.3 = (f32[128,512]{1,0:T(8,128)S(1)}, bf16[128,512]{1,0:T(8,128)(2,1)S(1)}, bf16[128,512]{1,0:T(8,128)(2,1)S(1)}, bf16[128,512]{1,0:T(8,128)(2,1)S(1)}) custom-call(bf16[128,512]{1,0:T(8,128)(2,1)S(1)} %sum.2.refs_3_.refs_0_, bf16[128,512]{1,0:T(8,128)(2,1)S(1)} %sum.3.refs_1_, bf16[8,160,512]{2,1,0:T(8,128)(2,1)S(1)} %get-tuple-element.91.refs_2_, ...), custom_call_target="tpu_custom_call" | custom-call | bytes 1024 | tf_op jit(solution)/shard_map/rest/pallas_call | solution.py:391
  99.2 1.5 %collective-permute-start.23 = (bf16[128,512]{1,0:T(8,128)(2,1)S(1)}, bf16[128,512]{1,0:T(8,128)(2,1)S(1)}, u32[]{:S(2)}, u32[]{:S(2)}) collective-permute-start(bf16[128,512]{1,0:T(8,128)(2,1)S(1)} %get-tuple-element.94), channel_id=1, source_target_pairs={{0,1},{1,0},{2,3},{3,2},{4,5},{5,4},{6,7},{7,6},{8,9},{9,8},{10,11... | collective-permute-start | bytes 393224 | tf_op jit(solution)/shard_map/ppermute | solution.py:410
  100.7 1.9 %collective-permute-done.26.far_ref = bf16[128,512]{1,0:T(8,128)(2,1)S(1)} collective-permute-done((bf16[128,512]{1,0:T(8,128)(2,1)S(1)}, bf16[128,512]{1,0:T(8,128)(2,1)S(1)}, u32[]{:S(2)}, u32[]{:S(2)}) %collective-permute-start.26) | collective-permute-done | bytes 131104 | tf_op jit(solution)/shard_map/ppermute | solution.py:410
  102.7 0.5 collective-permute-start.27
  103.2 1.6 %collective-permute-start.28 = (bf16[128,512]{1,0:T(8,128)(2,1)S(1)}, bf16[128,512]{1,0:T(8,128)(2,1)S(1)}, u32[]{:S(2)}, u32[]{:S(2)}) collective-permute-start(bf16[128,512]{1,0:T(8,128)(2,1)S(1)} %get-tuple-element.104), channel_id=1, source_target_pairs={{0,1},{1,2},{2,3},{3,0},{4,5},{5,6},{6,7},{7,4},{8,9},{9,10},{10,1... | collective-permute-start | bytes 393224 | tf_op jit(solution)/shard_map/ppermute | solution.py:406
  104.8 1.0 collective-permute-done.23.far_ref
  105.8 1.7 %collective-permute-start.24 = (bf16[128,512]{1,0:T(8,128)(2,1)S(1)}, bf16[128,512]{1,0:T(8,128)(2,1)S(1)}, u32[]{:S(2)}, u32[]{:S(2)}) collective-permute-start(bf16[128,512]{1,0:T(8,128)(2,1)S(1)} %get-tuple-element.97), channel_id=1, source_target_pairs={{0,3},{1,0},{2,1},{3,2},{4,7},{5,4},{6,5},{7,6},{8,11},{9,8},{10,9... | collective-permute-start | bytes 393224 | tf_op jit(solution)/shard_map/ppermute | solution.py:406
  107.8 3.0 %collective-permute-done.27.refs_1_ = bf16[128,512]{1,0:T(8,128)(2,1)S(1)} collective-permute-done((bf16[128,512]{1,0:T(8,128)(2,1)S(1)}, bf16[128,512]{1,0:T(8,128)(2,1)S(1)}, u32[]{:S(2)}, u32[]{:S(2)}) %collective-permute-start.27) | collective-permute-done | bytes 131104 | tf_op jit(solution)/shard_map/ppermute | solution.py:406
  110.9 2.0 %collective-permute-done.28.refs_2_ = bf16[128,512]{1,0:T(8,128)(2,1)S(1)} collective-permute-done((bf16[128,512]{1,0:T(8,128)(2,1)S(1)}, bf16[128,512]{1,0:T(8,128)(2,1)S(1)}, u32[]{:S(2)}, u32[]{:S(2)}) %collective-permute-start.28) | collective-permute-done | bytes 131104 | tf_op jit(solution)/shard_map/ppermute | solution.py:406
  112.9 0.7 write.2.refs_3_
  113.6 0.8 collective-permute-done.24.refs_1_
  114.4 2.3 %collective-permute-done.25.refs_2_ = bf16[128,512]{1,0:T(8,128)(2,1)S(1)} collective-permute-done((bf16[128,512]{1,0:T(8,128)(2,1)S(1)}, bf16[128,512]{1,0:T(8,128)(2,1)S(1)}, u32[]{:S(2)}, u32[]{:S(2)}) %collective-permute-start.25) | collective-permute-done | bytes 131104 | tf_op jit(solution)/shard_map/ppermute | solution.py:406
  116.7 0.7 write.3
  (43 shorter events, 2.2 us)
Async XLA Ops:
  1.1 18.9 %collective-permute-start.1 = (bf16[136,1024]{1,0:T(8,128)(2,1)S(1)}, bf16[136,1024]{1,0:T(8,128)(2,1)S(1)}, u32[]{:S(2)}, u32[]{:S(2)}) collective-permute-start(bf16[136,1024]{1,0:T(8,128)(2,1)S(1)} %get-tuple-element.56.refs_2_.refs_0_.refs_4_), channel_id=1, source_target_pairs={{0,1},{1,2},{2,3},{3,0},{4,5},{5,6},{6,7},{7,4},{8,9},{9,10},{10,1... | collective-permute-start | bytes 835592 | tf_op jit(solution)/shard_map/ppermute | solution.py:406
  4.2 15.8 %collective-permute-start.2 = (bf16[136,1024]{1,0:T(8,128)(2,1)S(1)}, bf16[136,1024]{1,0:T(8,128)(2,1)S(1)}, u32[]{:S(2)}, u32[]{:S(2)}) collective-permute-start(bf16[136,1024]{1,0:T(8,128)(2,1)S(1)} %get-tuple-element.56.refs_2_.refs_0_.refs_4_), channel_id=1, source_target_pairs={{0,3},{1,0},{2,1},{3,2},{4,7},{5,4},{6,5},{7,6},{8,11},{9,8},{10,9... | collective-permute-start | bytes 835592 | tf_op jit(solution)/shard_map/ppermute | solution.py:406
  6.3 21.0 %collective-permute-start = (bf16[128,1024]{1,0:T(8,128)(2,1)S(1)}, bf16[128,1024]{1,0:T(8,128)(2,1)S(1)}, u32[]{:S(2)}, u32[]{:S(2)}) collective-permute-start(bf16[128,1024]{1,0:T(8,128)(2,1)S(1)} %get-tuple-element.55.refs_0_), channel_id=1, source_target_pairs={{0,1},{1,2},{2,3},{3,0},{4,5},{5,6},{6,7},{7,4},{8,9},{9,10},{10,1... | collective-permute-start | bytes 786440 | tf_op jit(solution)/shard_map/ppermute | solution.py:406
  6.3 23.9 %collective-permute-start.3 = (bf16[128,1024]{1,0:T(8,128)(2,1)S(1)}, bf16[128,1024]{1,0:T(8,128)(2,1)S(1)}, u32[]{:S(2)}, u32[]{:S(2)}) collective-permute-start(bf16[128,1024]{1,0:T(8,128)(2,1)S(1)} %get-tuple-element.55.refs_0_), channel_id=1, source_target_pairs={{0,3},{1,0},{2,1},{3,2},{4,7},{5,4},{6,5},{7,6},{8,11},{9,8},{10,9... | collective-permute-start | bytes 786440 | tf_op jit(solution)/shard_map/ppermute | solution.py:406
  20.0 16.2 %collective-permute-start.5 = (bf16[136,1024]{1,0:T(8,128)(2,1)S(1)}, bf16[136,1024]{1,0:T(8,128)(2,1)S(1)}, u32[]{:S(2)}, u32[]{:S(2)}) collective-permute-start(bf16[136,1024]{1,0:T(8,128)(2,1)S(1)} %choose.5.after_ref), channel_id=1, source_target_pairs={{0,1},{1,0},{2,3},{3,2},{4,5},{5,4},{6,7},{7,6},{8,9},{9,8},{10,11... | collective-permute-start | bytes 835592 | tf_op jit(solution)/shard_map/ppermute | solution.py:410
  20.4 10.3 %copy-start.1 = (bf16[1,2,128,1024]{3,2,1,0:T(8,128)(2,1)S(1)}, bf16[1,2,128,1024]{3,2,1,0:T(8,128)(2,1)}, u32[]{:S(2)}) copy-start(bf16[1,2,128,1024]{3,2,1,0:T(8,128)(2,1)} %param.8) | copy-start | bytes 1572868
  27.3 15.4 %copy-start = (bf16[8,1024,512]{2,1,0:T(8,128)(2,1)}, bf16[8,1024,512]{2,1,0:T(8,128)(2,1)S(1)}, u32[]{:S(2)}) copy-start(bf16[8,1024,512]{2,1,0:T(8,128)(2,1)S(1)} %get-tuple-element.66.refs_10_.refs_16_) | copy-start | bytes 25165828
  30.2 12.4 %collective-permute-start.4 = (bf16[128,1024]{1,0:T(8,128)(2,1)S(1)}, bf16[128,1024]{1,0:T(8,128)(2,1)S(1)}, u32[]{:S(2)}, u32[]{:S(2)}) collective-permute-start(bf16[128,1024]{1,0:T(8,128)(2,1)S(1)} %choose.6.refs_0_), channel_id=1, source_target_pairs={{0,1},{1,0},{2,3},{3,2},{4,5},{5,4},{6,7},{7,6},{8,9},{9,8},{10,11... | collective-permute-start | bytes 786440 | tf_op jit(solution)/shard_map/ppermute | solution.py:410
  30.8 21.3 %collective-permute-start.8 = (bf16[128,1024]{1,0:T(8,128)(2,1)S(1)}, bf16[128,1024]{1,0:T(8,128)(2,1)S(1)}, u32[]{:S(2)}, u32[]{:S(2)}) collective-permute-start(bf16[128,1024]{1,0:T(8,128)(2,1)S(1)} %hold.1.refs_0_), channel_id=1, source_target_pairs={{0,1},{1,2},{2,3},{3,0},{4,5},{5,6},{6,7},{7,4},{8,9},{9,10},{10,1... | collective-permute-start | bytes 786440 | tf_op jit(solution)/shard_map/ppermute | solution.py:406
  32.4 21.4 %collective-permute-start.9 = (bf16[128,1024]{1,0:T(8,128)(2,1)S(1)}, bf16[128,1024]{1,0:T(8,128)(2,1)S(1)}, u32[]{:S(2)}, u32[]{:S(2)}) collective-permute-start(bf16[128,1024]{1,0:T(8,128)(2,1)S(1)} %hold.1.refs_0_), channel_id=1, source_target_pairs={{0,3},{1,0},{2,1},{3,2},{4,7},{5,4},{6,5},{7,6},{8,11},{9,8},{10,9... | collective-permute-start | bytes 786440 | tf_op jit(solution)/shard_map/ppermute | solution.py:406
  46.9 7.2 %collective-permute-start.6 = (bf16[128,512]{1,0:T(8,128)(2,1)S(1)}, bf16[128,512]{1,0:T(8,128)(2,1)S(1)}, u32[]{:S(2)}, u32[]{:S(2)}) collective-permute-start(bf16[128,512]{1,0:T(8,128)(2,1)S(1)} %get-tuple-element.67), channel_id=1, source_target_pairs={{0,28},{1,29},{2,30},{3,31},{4,0},{5,1},{6,2},{7,3},{8,4},{9,5},{1... | collective-permute-start | bytes 393224 | tf_op jit(solution)/shard_map/ppermute | solution.py:420
  47.7 8.2 %collective-permute-start.7 = (bf16[128,512]{1,0:T(8,128)(2,1)S(1)}, bf16[128,512]{1,0:T(8,128)(2,1)S(1)}, u32[]{:S(2)}, u32[]{:S(2)}) collective-permute-start(bf16[128,512]{1,0:T(8,128)(2,1)S(1)} %get-tuple-element.68), channel_id=1, source_target_pairs={{0,1},{1,0},{2,3},{3,2},{4,5},{5,4},{6,7},{7,6},{8,9},{9,8},{10,11... | collective-permute-start | bytes 393224 | tf_op jit(solution)/shard_map/ppermute | solution.py:410
  49.8 9.8 %collective-permute-start.12 = (bf16[128,512]{1,0:T(8,128)(2,1)S(1)}, bf16[128,512]{1,0:T(8,128)(2,1)S(1)}, u32[]{:S(2)}, u32[]{:S(2)}) collective-permute-start(bf16[128,512]{1,0:T(8,128)(2,1)S(1)} %get-tuple-element.75), channel_id=1, source_target_pairs={{0,28},{1,29},{2,30},{3,31},{4,0},{5,1},{6,2},{7,3},{8,4},{9,5},{1... | collective-permute-start | bytes 393224 | tf_op jit(solution)/shard_map/ppermute | solution.py:420
  52.0 7.5 %collective-permute-start.13 = (bf16[128,512]{1,0:T(8,128)(2,1)S(1)}, bf16[128,512]{1,0:T(8,128)(2,1)S(1)}, u32[]{:S(2)}, u32[]{:S(2)}) collective-permute-start(bf16[128,512]{1,0:T(8,128)(2,1)S(1)} %get-tuple-element.76), channel_id=1, source_target_pairs={{0,1},{1,0},{2,3},{3,2},{4,5},{5,4},{6,7},{7,6},{8,9},{9,8},{10,11... | collective-permute-start | bytes 393224 | tf_op jit(solution)/shard_map/ppermute | solution.py:410
  53.8 23.7 %collective-permute-start.18 = (bf16[128,1024]{1,0:T(8,128)(2,1)S(1)}, bf16[128,1024]{1,0:T(8,128)(2,1)S(1)}, u32[]{:S(2)}, u32[]{:S(2)}) collective-permute-start(bf16[128,1024]{1,0:T(8,128)(2,1)S(1)} %choose.7), channel_id=1, source_target_pairs={{0,1},{1,0},{2,3},{3,2},{4,5},{5,4},{6,7},{7,6},{8,9},{9,8},{10,11... | collective-permute-start | bytes 786440 | tf_op jit(solution)/shard_map/ppermute | solution.py:410
  55.9 10.3 %collective-permute-start.10 = (bf16[128,512]{1,0:T(8,128)(2,1)S(1)}, bf16[128,512]{1,0:T(8,128)(2,1)S(1)}, u32[]{:S(2)}, u32[]{:S(2)}) collective-permute-start(bf16[128,512]{1,0:T(8,128)(2,1)S(1)} %get-tuple-element.71), channel_id=1, source_target_pairs={{0,31},{1,28},{2,29},{3,30},{4,3},{5,0},{6,1},{7,2},{8,7},{9,4},{1... | collective-permute-start | bytes 393224 | tf_op jit(solution)/shard_map/ppermute | solution.py:420
  59.1 9.9 %collective-permute-start.11 = (bf16[128,512]{1,0:T(8,128)(2,1)S(1)}, bf16[128,512]{1,0:T(8,128)(2,1)S(1)}, u32[]{:S(2)}, u32[]{:S(2)}) collective-permute-start(bf16[128,512]{1,0:T(8,128)(2,1)S(1)} %get-tuple-element.72), channel_id=1, source_target_pairs={{0,29},{1,30},{2,31},{3,28},{4,1},{5,2},{6,3},{7,0},{8,5},{9,6},{1... | collective-permute-start | bytes 393224 | tf_op jit(solution)/shard_map/ppermute | solution.py:420
  59.6 13.3 %collective-permute-start.14 = (bf16[128,512]{1,0:T(8,128)(2,1)S(1)}, bf16[128,512]{1,0:T(8,128)(2,1)S(1)}, u32[]{:S(2)}, u32[]{:S(2)}) collective-permute-start(bf16[128,512]{1,0:T(8,128)(2,1)S(1)} %get-tuple-element.79), channel_id=1, source_target_pairs={{0,31},{1,28},{2,29},{3,30},{4,3},{5,0},{6,1},{7,2},{8,7},{9,4},{1... | collective-permute-start | bytes 393224 | tf_op jit(solution)/shard_map/ppermute | solution.py:420
  62.8 10.8 %collective-permute-start.15 = (bf16[128,512]{1,0:T(8,128)(2,1)S(1)}, bf16[128,512]{1,0:T(8,128)(2,1)S(1)}, u32[]{:S(2)}, u32[]{:S(2)}) collective-permute-start(bf16[128,512]{1,0:T(8,128)(2,1)S(1)} %get-tuple-element.80), channel_id=1, source_target_pairs={{0,29},{1,30},{2,31},{3,28},{4,1},{5,2},{6,3},{7,0},{8,5},{9,6},{1... | collective-permute-start | bytes 393224 | tf_op jit(solution)/shard_map/ppermute | solution.py:420
  69.1 12.4 %collective-permute-start.16 = (bf16[128,512]{1,0:T(8,128)(2,1)S(1)}, bf16[128,512]{1,0:T(8,128)(2,1)S(1)}, u32[]{:S(2)}, u32[]{:S(2)}) collective-permute-start(bf16[128,512]{1,0:T(8,128)(2,1)S(1)} %sum.2.refs_3_.refs_0_), channel_id=1, source_target_pairs={{0,1},{1,2},{2,3},{3,0},{4,5},{5,6},{6,7},{7,4},{8,9},{9,10},{10,1... | collective-permute-start | bytes 393224 | tf_op jit(solution)/shard_map/ppermute | solution.py:406
  69.1 12.3 %collective-permute-start.19 = (bf16[128,512]{1,0:T(8,128)(2,1)S(1)}, bf16[128,512]{1,0:T(8,128)(2,1)S(1)}, u32[]{:S(2)}, u32[]{:S(2)}) collective-permute-start(bf16[128,512]{1,0:T(8,128)(2,1)S(1)} %sum.2.refs_3_.refs_0_), channel_id=1, source_target_pairs={{0,3},{1,0},{2,1},{3,2},{4,7},{5,4},{6,5},{7,6},{8,11},{9,8},{10,9... | collective-permute-start | bytes 393224 | tf_op jit(solution)/shard_map/ppermute | solution.py:406
  73.7 9.9 %collective-permute-start.17 = (bf16[128,512]{1,0:T(8,128)(2,1)S(1)}, bf16[128,512]{1,0:T(8,128)(2,1)S(1)}, u32[]{:S(2)}, u32[]{:S(2)}) collective-permute-start(bf16[128,512]{1,0:T(8,128)(2,1)S(1)} %sum.3.refs_1_), channel_id=1, source_target_pairs={{0,1},{1,2},{2,3},{3,0},{4,5},{5,6},{6,7},{7,4},{8,9},{9,10},{10,1... | collective-permute-start | bytes 393224 | tf_op jit(solution)/shard_map/ppermute | solution.py:406
  73.7 12.5 %collective-permute-start.21 = (bf16[128,512]{1,0:T(8,128)(2,1)S(1)}, bf16[128,512]{1,0:T(8,128)(2,1)S(1)}, u32[]{:S(2)}, u32[]{:S(2)}) collective-permute-start(bf16[128,512]{1,0:T(8,128)(2,1)S(1)} %sum.3.refs_1_), channel_id=1, source_target_pairs={{0,3},{1,0},{2,1},{3,2},{4,7},{5,4},{6,5},{7,6},{8,11},{9,8},{10,9... | collective-permute-start | bytes 393224 | tf_op jit(solution)/shard_map/ppermute | solution.py:406
  81.5 9.1 %collective-permute-start.20 = (bf16[128,512]{1,0:T(8,128)(2,1)S(1)}, bf16[128,512]{1,0:T(8,128)(2,1)S(1)}, u32[]{:S(2)}, u32[]{:S(2)}) collective-permute-start(bf16[128,512]{1,0:T(8,128)(2,1)S(1)} %choose.8), channel_id=1, source_target_pairs={{0,1},{1,0},{2,3},{3,2},{4,5},{5,4},{6,7},{7,6},{8,9},{9,8},{10,11... | collective-permute-start | bytes 393224 | tf_op jit(solution)/shard_map/ppermute | solution.py:410
  86.4 6.1 %collective-permute-start.22 = (bf16[128,512]{1,0:T(8,128)(2,1)S(1)}, bf16[128,512]{1,0:T(8,128)(2,1)S(1)}, u32[]{:S(2)}, u32[]{:S(2)}) collective-permute-start(bf16[128,512]{1,0:T(8,128)(2,1)S(1)} %choose.9.after_ref), channel_id=1, source_target_pairs={{0,1},{1,0},{2,3},{3,2},{4,5},{5,4},{6,7},{7,6},{8,9},{9,8},{10,11... | collective-permute-start | bytes 393224 | tf_op jit(solution)/shard_map/ppermute | solution.py:410
  87.5 5.0 %slice-start = ((s8[8388608]{0:T(1024)(128)(4,1)}), s8[4194304]{0:T(1024)(128)(4,1)S(1)}, s32[]{:S(2)}) async-start(s8[8388608]{0:T(1024)(128)(4,1)} %bitcast.14), calls=%async_computation | async-start | bytes 8388608
  87.5 5.0 %slice-start.1 = ((s8[8388608]{0:T(1024)(128)(4,1)}), s8[4194304]{0:T(1024)(128)(4,1)S(1)}, s32[]{:S(2)}) async-start(s8[8388608]{0:T(1024)(128)(4,1)} %bitcast.14), calls=%async_computation.1 | async-start | bytes 8388608
  96.6 6.0 %collective-permute-start.26 = (bf16[128,512]{1,0:T(8,128)(2,1)S(1)}, bf16[128,512]{1,0:T(8,128)(2,1)S(1)}, u32[]{:S(2)}, u32[]{:S(2)}) collective-permute-start(bf16[128,512]{1,0:T(8,128)(2,1)S(1)} %get-tuple-element.100), channel_id=1, source_target_pairs={{0,1},{1,0},{2,3},{3,2},{4,5},{5,4},{6,7},{7,6},{8,9},{9,8},{10,11... | collective-permute-start | bytes 393224 | tf_op jit(solution)/shard_map/ppermute | solution.py:410
  99.2 6.5 %collective-permute-start.23 = (bf16[128,512]{1,0:T(8,128)(2,1)S(1)}, bf16[128,512]{1,0:T(8,128)(2,1)S(1)}, u32[]{:S(2)}, u32[]{:S(2)}) collective-permute-start(bf16[128,512]{1,0:T(8,128)(2,1)S(1)} %get-tuple-element.94), channel_id=1, source_target_pairs={{0,1},{1,0},{2,3},{3,2},{4,5},{5,4},{6,7},{7,6},{8,9},{9,8},{10,11... | collective-permute-start | bytes 393224 | tf_op jit(solution)/shard_map/ppermute | solution.py:410
  102.7 8.2 %collective-permute-start.27 = (bf16[128,512]{1,0:T(8,128)(2,1)S(1)}, bf16[128,512]{1,0:T(8,128)(2,1)S(1)}, u32[]{:S(2)}, u32[]{:S(2)}) collective-permute-start(bf16[128,512]{1,0:T(8,128)(2,1)S(1)} %get-tuple-element.103), channel_id=1, source_target_pairs={{0,3},{1,0},{2,1},{3,2},{4,7},{5,4},{6,5},{7,6},{8,11},{9,8},{10,9... | collective-permute-start | bytes 393224 | tf_op jit(solution)/shard_map/ppermute | solution.py:406
  103.2 9.7 %collective-permute-start.28 = (bf16[128,512]{1,0:T(8,128)(2,1)S(1)}, bf16[128,512]{1,0:T(8,128)(2,1)S(1)}, u32[]{:S(2)}, u32[]{:S(2)}) collective-permute-start(bf16[128,512]{1,0:T(8,128)(2,1)S(1)} %get-tuple-element.104), channel_id=1, source_target_pairs={{0,1},{1,2},{2,3},{3,0},{4,5},{5,6},{6,7},{7,4},{8,9},{9,10},{10,1... | collective-permute-start | bytes 393224 | tf_op jit(solution)/shard_map/ppermute | solution.py:406
  105.8 8.7 %collective-permute-start.24 = (bf16[128,512]{1,0:T(8,128)(2,1)S(1)}, bf16[128,512]{1,0:T(8,128)(2,1)S(1)}, u32[]{:S(2)}, u32[]{:S(2)}) collective-permute-start(bf16[128,512]{1,0:T(8,128)(2,1)S(1)} %get-tuple-element.97), channel_id=1, source_target_pairs={{0,3},{1,0},{2,1},{3,2},{4,7},{5,4},{6,5},{7,6},{8,11},{9,8},{10,9... | collective-permute-start | bytes 393224 | tf_op jit(solution)/shard_map/ppermute | solution.py:406
  107.5 9.2 %collective-permute-start.25 = (bf16[128,512]{1,0:T(8,128)(2,1)S(1)}, bf16[128,512]{1,0:T(8,128)(2,1)S(1)}, u32[]{:S(2)}, u32[]{:S(2)}) collective-permute-start(bf16[128,512]{1,0:T(8,128)(2,1)S(1)} %get-tuple-element.98), channel_id=1, source_target_pairs={{0,1},{1,2},{2,3},{3,0},{4,5},{5,6},{6,7},{7,4},{8,9},{9,10},{10,1... | collective-permute-start | bytes 393224 | tf_op jit(solution)/shard_map/ppermute | solution.py:406
